TPU v7x, 32 devices: a whole 2x2x4 slice. The times are simulated.
32 devices in a mesh: groups: 2 (over y), row: 4 (over z), col: 2 (over x), rep: 2 (over core).
Axes of the slice: x: 2, y: 2, z: 4, core: 2. Of those that a mesh axis runs over, the one named last changes fastest.
Arguments:
- source_emb: bfloat16 [16384, 256], P(('groups', 'row')), parts along dimension 0, may hold values from -6 to 6
- target_emb: bfloat16 [8192, 256], P(('groups', 'col')), parts along dimension 0, may hold values from -6 to 6
- warm_start: float32 [8192], P(('groups', 'col')), parts along dimension 0, may hold values from -4 to 210
- source_weight: float32 [16384], P(('groups', 'row')), parts along dimension 0, may hold values from 1 to 10
- target_weight: float32 [8192], P(('groups', 'col')), parts along dimension 0, may hold values from 1 to 10
- source_bounds: int32 [18], P('groups'), parts along dimension 0, may hold values from 0 to 16, as said below
- target_bounds: int32 [10], P('groups'), parts along dimension 0, may hold values from 0 to 8, as said below
- kept_pairs: int32 [32, 2], P('groups'), parts along dimension 0, may hold values from 0 to 7, as said below
Outputs:
- grad_source: bfloat16 [16384, 256], P(('groups', 'row', 'col', 'rep')), parts along dimension 0
- grad_target: bfloat16 [8192, 256], P(('groups', 'col')), parts along dimension 0
There are 2 independent parts, one for each index of `groups`. A program takes and returns all parts, laid end to end along the dimension named above; each array names one. Nothing has to cross between parts.
Inputs may be any that keep to these rules, and one draw needn't show every extreme that they name: Cluster k of the source cohort is tiles source_bounds[k] to source_bounds[k + 1] - 1; the bounds rise strictly from 0 to the end; each block of 4 tiles of one index of row holds exactly two clusters. Cluster k of the target cohort is tiles target_bounds[k] to target_bounds[k + 1] - 1; the bounds rise strictly from 0 to the end; each block of 4 tiles of one index of col holds exactly two clusters. `kept_pairs`: each pair of a source block and a target block holds exactly two listed pairs, which match its two source clusters one to one with its two target clusters; in some pair of blocks (3) * 3 + 1 tiles are kept, and in none more.
All inputs are finite; a program needn't handle non-finite values.
Results may differ from a plain program's by a relative error of at most 0.0042.
Values may be sent and summed in bfloat16 or wider, within the bound.
No kernel may reach another device: no remote copies, remote signals or barrier semaphores. Data moves between devices by JAX's collectives and lax.ppermute only.
A program may use at most 64 MiB of HBM per device.

v0:
```python
import jax
import jax.numpy as jnp
from jax import lax
from jax.sharding import PartitionSpec as P

TILE = 512
SLOTS = 5


temper = 1.0
sentinel = -1e30


def shards(
    source_emb,
    target_emb,
    warm_start,
    source_weight,
    target_weight,
    source_bounds,
    target_bounds,
    kept_pairs,
):
    feature_width = source_emb.shape[1]
    src_count = source_emb.shape[0] // TILE
    tgt_count = target_emb.shape[0] // TILE
    inv_root = feature_width ** (-0.5)
    row_pos = lax.axis_index("row")
    col_pos = lax.axis_index("col")
    rep_pos = lax.axis_index("rep")
    src_ids = row_pos * src_count + jnp.arange(src_count, dtype=jnp.int32)
    tgt_ids = col_pos * tgt_count + jnp.arange(tgt_count, dtype=jnp.int32)
    src_cluster = jnp.sum(
        (source_bounds[1:-1][None, :] <= src_ids[:, None]).astype(jnp.int32), axis=1
    )
    tgt_cluster = jnp.sum(
        (target_bounds[1:-1][None, :] <= tgt_ids[:, None]).astype(jnp.int32), axis=1
    )
    matches = (kept_pairs[:, 0][None, None, :] == src_cluster[:, None, None]) & (
        kept_pairs[:, 1][None, None, :] == tgt_cluster[None, :, None]
    )
    marks = jnp.any(matches, axis=2).reshape(-1).astype(jnp.int32)
    order_rank = jnp.cumsum(marks) - 1
    wanted = 2 * jnp.arange(SLOTS, dtype=jnp.int32) + rep_pos
    chosen = (marks[None, :] == 1) & (order_rank[None, :] == wanted[:, None])
    occupied = jnp.any(chosen, axis=1)
    flat_index = jnp.sum(
        chosen.astype(jnp.int32) * jnp.arange(src_count * tgt_count, dtype=jnp.int32), axis=1
    )
    src_slot = flat_index // tgt_count
    tgt_slot = flat_index % tgt_count
    x_tiles = jnp.take(source_emb.reshape(src_count, TILE, feature_width), src_slot, axis=0)
    y_tiles = jnp.take(target_emb.reshape(tgt_count, TILE, feature_width), tgt_slot, axis=0)
    tile_cost = -inv_root * jnp.einsum(
        "kid,kjd->kij", x_tiles, y_tiles, preferred_element_type=jnp.float32
    )
    is_live = occupied[:, None, None]
    src_hot = (src_slot[:, None] == jnp.arange(src_count, dtype=jnp.int32)[None, :]) & occupied[
        :, None
    ]
    tgt_hot = (tgt_slot[:, None] == jnp.arange(tgt_count, dtype=jnp.int32)[None, :]) & occupied[
        :, None
    ]

    def rows_of(vector):
        return jnp.take(vector.reshape(src_count, TILE), src_slot, axis=0)

    def columns_of(vector):
        return jnp.take(vector.reshape(tgt_count, TILE), tgt_slot, axis=0)

    def add_rows(values):
        return jnp.sum(jnp.where(src_hot[:, :, None], values[:, None, :], 0.0), axis=0).reshape(-1)

    def add_columns(values):
        return jnp.sum(jnp.where(tgt_hot[:, :, None], values[:, None, :], 0.0), axis=0).reshape(-1)

    def largest_rows(values):
        return jnp.max(
            jnp.where(src_hot[:, :, None], values[:, None, :], sentinel), axis=0
        ).reshape(-1)

    def largest_columns(values):
        return jnp.max(
            jnp.where(tgt_hot[:, :, None], values[:, None, :], sentinel), axis=0
        ).reshape(-1)

    def source_step(target_pot):
        scores = jnp.where(
            is_live, (columns_of(target_pot)[:, None, :] - tile_cost) / temper, sentinel
        )
        largest = lax.pmax(largest_rows(jnp.max(scores, axis=2)), ("col", "rep"))
        shifted = jnp.where(is_live, jnp.exp(scores - rows_of(largest)[:, :, None]), 0.0)
        totals = lax.psum(add_rows(jnp.sum(shifted, axis=2)), ("col", "rep"))
        return -temper * (largest + jnp.log(totals))

    def target_step(source_pot):
        scores = jnp.where(
            is_live, (rows_of(source_pot)[:, :, None] - tile_cost) / temper, sentinel
        )
        largest = lax.pmax(largest_columns(jnp.max(scores, axis=1)), ("row", "rep"))
        shifted = jnp.where(is_live, jnp.exp(scores - columns_of(largest)[:, None, :]), 0.0)
        totals = lax.psum(add_columns(jnp.sum(shifted, axis=1)), ("row", "rep"))
        return -temper * (largest + jnp.log(totals))

    def transport(row_pot, column_pot):
        return jnp.where(
            is_live,
            jnp.exp((row_pot[:, :, None] + column_pot[:, None, :] - tile_cost) / temper),
            0.0,
        )

    def source_adjoint(values):
        return lax.psum(add_rows(values), ("col", "rep"))

    first_source = source_step(warm_start)
    first_target = target_step(first_source)
    second_source = source_step(first_target)
    second_target = target_step(second_source)
    bar_cost = (
        transport(rows_of(second_source), columns_of(second_target))
        * columns_of(target_weight)[:, None, :]
    )
    adjoint_late = source_weight - source_adjoint(jnp.sum(bar_cost, axis=2))
    addend = (
        transport(rows_of(second_source), columns_of(first_target))
        * rows_of(adjoint_late)[:, :, None]
    )
    adjoint_mid = -lax.psum(add_columns(jnp.sum(addend, axis=1)), ("row", "rep"))
    bar_cost = bar_cost + addend
    addend = (
        transport(rows_of(first_source), columns_of(first_target))
        * columns_of(adjoint_mid)[:, None, :]
    )
    adjoint_early = -source_adjoint(jnp.sum(addend, axis=2))
    bar_cost = bar_cost + addend
    bar_cost = (
        bar_cost
        + transport(rows_of(first_source), columns_of(warm_start))
        * rows_of(adjoint_early)[:, :, None]
    )
    rounded = bar_cost.astype(jnp.bfloat16)
    source_part = -inv_root * jnp.einsum(
        "kij,kjd->kid", rounded, y_tiles, preferred_element_type=jnp.float32
    )
    target_part = -inv_root * jnp.einsum(
        "kij,kid->kjd", rounded, x_tiles, preferred_element_type=jnp.float32
    )
    source_rows = jnp.einsum(
        "ka,kid->aid", src_hot.astype(jnp.float32), source_part, precision=lax.Precision.HIGHEST
    ).reshape(-1, feature_width)
    target_rows = jnp.einsum(
        "ka,kjd->ajd", tgt_hot.astype(jnp.float32), target_part, precision=lax.Precision.HIGHEST
    ).reshape(-1, feature_width)
    grad_source = lax.psum_scatter(
        source_rows, ("col", "rep"), scatter_dimension=0, tiled=True
    ).astype(jnp.bfloat16)
    grad_target = lax.psum(target_rows, ("row", "rep")).astype(jnp.bfloat16)
    return (grad_source, grad_target)


def solution(mesh):
    return jax.shard_map(
        shards,
        mesh=mesh,
        in_specs=(
            P(("groups", "row"), None),
            P(("groups", "col"), None),
            P(("groups", "col")),
            P(("groups", "row")),
            P(("groups", "col")),
            P("groups"),
            P("groups"),
            P("groups", None),
        ),
        out_specs=(P(("groups", "row", "col", "rep"), None), P(("groups", "col"), None)),
        check_vma=False,
    )
```

profile of v0, /device:TPU:0, one launch (start us, length us, event | category | flops | bytes accessed | tf_op | source)
XLA Modules:
  0.0 266.4 jit_solution(7660278437770676787)
XLA Ops:
  13.7 1.8 gather_fusion.2
  15.6 1.9 gather_fusion.1
  17.4 4.8 %fusion.3 = (f32[5,512]{1,0:T(8,128)S(1)}, f32[5,512,512]{1,2,0:T(8,128)}) fusion(f32[5,512]{1,0:T(8,128)S(1)} %broadcast_select_fusion.18, pred[5]{0:T(512)(128)(4,1)S(1)} %fusion.11, bf16[5,512,256]{2,1,0:T(8,128)(2,1)} %gather_fusion.2, pred[5]{0:T(512)(128)(4,1)S(1)} %get-tuple-element.4, bf16[5,512,256]{2,1,0:T(8,128)(2,1)S(1)} %gather_fusion.1, ...), kind=kOutput, calls=%fused_computation.30 | convolution fusion | flops 677639680 | bytes 7884815 | tf_op jit(solution)/shard_map/kid,kjd->kij/dot_general | solution.py:54
  22.3 8.5 %pmax.28 = f32[2048]{0:T(1024)S(1)} all-reduce(f32[2048]{0:T(1024)S(1)} %bitcast.53), channel_id=1, replica_groups=mesh['groups'=2,'row'=4,'col'=2,'rep'=2] {'col','rep'}, use_global_device_ids=true, to_apply=%region_8.11 | all-reduce | flops 2048 | bytes 16384 | tf_op jit(solution)/shard_map/pmax | solution.py:91
  31.4 3.2 %select_reduce_fusion.3 = f32[5,512]{1,0:T(8,128)S(1)} fusion(f32[5,512,512]{1,2,0:T(8,128)} %get-tuple-element.19, f32[5,512]{1,0:T(8,128)S(1)} %broadcast_select_fusion.17, f32[5,512]{1,0:T(8,128)S(1)} %broadcast_select_fusion.18, pred[5]{0:T(512)(128)(4,1)S(1)} %fusion.11), kind=kLoop, calls=%fused_computation.28 | loop fusion | flops 6551040 | bytes 5273605 | tf_op jit(solution)/shard_map/reduce_sum | solution.py:93
  34.8 5.9 %psum.56 = f32[2048]{0:T(1024)S(1)} all-reduce(f32[2048]{0:T(1024)S(1)} %bitcast.54), channel_id=1, replica_groups=mesh['groups'=2,'row'=4,'col'=2,'rep'=2] {'col','rep'}, use_global_device_ids=true, to_apply=%region_11.14 | all-reduce | flops 2048 | bytes 16384 | tf_op jit(solution)/shard_map/psum | solution.py:93
  41.3 3.2 %fusion.4 = f32[5,512]{1,0:T(8,128)S(1)} fusion(f32[5,512,512]{1,2,0:T(8,128)} %get-tuple-element.19, f32[5,512]{1,0:T(8,128)S(1)} %broadcast_select_fusion.16, pred[5]{0:T(512)(128)(4,1)S(1)} %fusion.11), kind=kLoop, calls=%fused_computation.31 | loop fusion | flops 3929600 | bytes 5263365 | tf_op jit(solution)/shard_map/reduce_max | solution.py:100
  44.6 16.8 %pmax.29 = f32[2048]{0:T(1024)S(1)} all-reduce(f32[2048]{0:T(1024)S(1)} %bitcast.55), channel_id=1, replica_groups=mesh['groups'=2,'row'=4,'col'=2,'rep'=2] {'row','rep'}, use_global_device_ids=true, to_apply=%region_14.17 | all-reduce | flops 2048 | bytes 16384 | tf_op jit(solution)/shard_map/pmax | solution.py:100
  62.0 3.4 %select_reduce_fusion.2 = f32[5,512]{1,0:T(8,128)S(1)} fusion(f32[5,512,512]{1,2,0:T(8,128)} %get-tuple-element.19, f32[5,512]{1,0:T(8,128)S(1)} %broadcast_select_fusion.15, f32[5,512]{1,0:T(8,128)S(1)} %broadcast_select_fusion.16, pred[5]{0:T(512)(128)(4,1)S(1)} %fusion.11), kind=kLoop, calls=%fused_computation.26 | loop fusion | flops 6551040 | bytes 5273605 | tf_op jit(solution)/shard_map/reduce_sum | solution.py:102
  65.5 13.9 %psum.57 = f32[2048]{0:T(1024)S(1)} all-reduce(f32[2048]{0:T(1024)S(1)} %bitcast.56), channel_id=1, replica_groups=mesh['groups'=2,'row'=4,'col'=2,'rep'=2] {'row','rep'}, use_global_device_ids=true, to_apply=%region_17.20 | all-reduce | flops 2048 | bytes 16384 | tf_op jit(solution)/shard_map/psum | solution.py:102
  80.1 3.1 %fusion.5 = f32[5,512]{1,0:T(8,128)S(1)} fusion(f32[5,512,512]{1,2,0:T(8,128)} %get-tuple-element.19, f32[5,512]{1,0:T(8,128)S(1)} %broadcast_select_fusion.14, pred[5]{0:T(512)(128)(4,1)S(1)} %fusion.11), kind=kLoop, calls=%fused_computation.32 | loop fusion | flops 3929600 | bytes 5263365 | tf_op jit(solution)/shard_map/reduce_max | solution.py:91
  83.3 6.1 %pmax.30 = f32[2048]{0:T(1024)S(1)} all-reduce(f32[2048]{0:T(1024)S(1)} %bitcast.57), channel_id=1, replica_groups=mesh['groups'=2,'row'=4,'col'=2,'rep'=2] {'col','rep'}, use_global_device_ids=true, to_apply=%region_20.23 | all-reduce | flops 2048 | bytes 16384 | tf_op jit(solution)/shard_map/pmax | solution.py:91
  90.1 3.2 %select_reduce_fusion.1 = f32[5,512]{1,0:T(8,128)S(1)} fusion(f32[5,512,512]{1,2,0:T(8,128)} %get-tuple-element.19, f32[5,512]{1,0:T(8,128)S(1)} %broadcast_select_fusion.13, f32[5,512]{1,0:T(8,128)S(1)} %broadcast_select_fusion.14, pred[5]{0:T(512)(128)(4,1)S(1)} %fusion.11), kind=kLoop, calls=%fused_computation.24 | loop fusion | flops 6551040 | bytes 5273605 | tf_op jit(solution)/shard_map/reduce_sum | solution.py:93
  93.5 5.8 %psum.58 = f32[2048]{0:T(1024)S(1)} all-reduce(f32[2048]{0:T(1024)S(1)} %bitcast.58), channel_id=1, replica_groups=mesh['groups'=2,'row'=4,'col'=2,'rep'=2] {'col','rep'}, use_global_device_ids=true, to_apply=%region_23.26 | all-reduce | flops 2048 | bytes 16384 | tf_op jit(solution)/shard_map/psum | solution.py:93
  99.9 3.2 %fusion.6 = f32[5,512]{1,0:T(8,128)S(1)} fusion(f32[5,512,512]{1,2,0:T(8,128)} %get-tuple-element.19, f32[5,512]{1,0:T(8,128)S(1)} %broadcast_select_fusion.12, pred[5]{0:T(512)(128)(4,1)S(1)} %fusion.11), kind=kLoop, calls=%fused_computation.33 | loop fusion | flops 3929600 | bytes 5263365 | tf_op jit(solution)/shard_map/reduce_max | solution.py:100
  103.2 13.9 %pmax.31 = f32[2048]{0:T(1024)S(1)} all-reduce(f32[2048]{0:T(1024)S(1)} %bitcast.59), channel_id=1, replica_groups=mesh['groups'=2,'row'=4,'col'=2,'rep'=2] {'row','rep'}, use_global_device_ids=true, to_apply=%region_26.29 | all-reduce | flops 2048 | bytes 16384 | tf_op jit(solution)/shard_map/pmax | solution.py:100
  117.8 3.4 %select_reduce_fusion = f32[5,512]{1,0:T(8,128)S(1)} fusion(f32[5,512,512]{1,2,0:T(8,128)} %get-tuple-element.19, f32[5,512]{1,0:T(8,128)S(1)} %broadcast_select_fusion.11, f32[5,512]{1,0:T(8,128)S(1)} %broadcast_select_fusion.12, pred[5]{0:T(512)(128)(4,1)S(1)} %fusion.11), kind=kLoop, calls=%fused_computation.22 | loop fusion | flops 6551040 | bytes 5273605 | tf_op jit(solution)/shard_map/reduce_sum | solution.py:102
  121.3 13.9 %psum.59 = f32[2048]{0:T(1024)S(1)} all-reduce(f32[2048]{0:T(1024)S(1)} %bitcast.60), channel_id=1, replica_groups=mesh['groups'=2,'row'=4,'col'=2,'rep'=2] {'row','rep'}, use_global_device_ids=true, to_apply=%region_29.32 | all-reduce | flops 2048 | bytes 16384 | tf_op jit(solution)/shard_map/psum | solution.py:102
  135.9 3.3 %fusion.2 = f32[5,512]{1,0:T(8,128)S(1)} fusion(f32[5,512,512]{1,2,0:T(8,128)} %get-tuple-element.19, f32[5,512]{1,0:T(8,128)S(1)} %get-tuple-element.11, f32[5,512]{1,0:T(8,128)S(1)} %get-tuple-element.10, f32[5,512]{1,0:T(8,128)S(1)} %broadcast_select_fusion.12, pred[5]{0:T(512)(128)(4,1)S(1)} %fusion.11), kind=kLoop, calls=%fused_computation.21 | loop fusion | flops 6551040 | bytes 5283845 | tf_op jit(solution)/shard_map/reduce_sum | solution.py:123
  139.3 7.2 %psum.60 = f32[2048]{0:T(1024)S(1)} all-reduce(f32[2048]{0:T(1024)S(1)} %bitcast.61), channel_id=1, replica_groups=mesh['groups'=2,'row'=4,'col'=2,'rep'=2] {'col','rep'}, use_global_device_ids=true, to_apply=%region_32.35 | all-reduce | flops 2048 | bytes 16384 | tf_op jit(solution)/shard_map/psum | solution.py:113
  147.2 3.3 %fusion.1 = f32[5,512]{1,0:T(8,128)S(1)} fusion(f32[5,512,512]{1,2,0:T(8,128)} %get-tuple-element.19, f32[5,512]{1,0:T(8,128)S(1)} %broadcast_select_fusion.8, f32[5,512]{1,0:T(8,128)S(1)} %broadcast_select_fusion.12, f32[5,512]{1,0:T(8,128)S(1)} %broadcast_select_fusion.14, pred[5]{0:T(512)(128)(4,1)S(1)} %fusion.11), kind=kLoop, calls=%fused_computation.19 | loop fusion | flops 6551040 | bytes 5283845 | tf_op jit(solution)/shard_map/reduce_sum | solution.py:128
  150.6 13.9 %psum.61 = f32[2048]{0:T(1024)S(1)} all-reduce(f32[2048]{0:T(1024)S(1)} %bitcast.62), channel_id=1, replica_groups=mesh['groups'=2,'row'=4,'col'=2,'rep'=2] {'row','rep'}, use_global_device_ids=true, to_apply=%region_35.38 | all-reduce | flops 2048 | bytes 16384 | tf_op jit(solution)/shard_map/psum | solution.py:128
  165.2 3.3 %fusion = f32[5,512]{1,0:T(8,128)S(1)} fusion(f32[5,512,512]{1,2,0:T(8,128)} %get-tuple-element.19, f32[5,512]{1,0:T(8,128)S(1)} %broadcast_select_fusion.7, f32[5,512]{1,0:T(8,128)S(1)} %broadcast_select_fusion.14, f32[5,512]{1,0:T(8,128)S(1)} %broadcast_select_fusion.16, pred[5]{0:T(512)(128)(4,1)S(1)} %fusion.11), kind=kLoop, calls=%fused_computation.17 | loop fusion | flops 6551040 | bytes 5283845 | tf_op jit(solution)/shard_map/reduce_sum | solution.py:134
  168.6 6.0 %psum.62 = f32[2048]{0:T(1024)S(1)} all-reduce(f32[2048]{0:T(1024)S(1)} %bitcast.63), channel_id=1, replica_groups=mesh['groups'=2,'row'=4,'col'=2,'rep'=2] {'col','rep'}, use_global_device_ids=true, to_apply=%region_38.41 | all-reduce | flops 2048 | bytes 16384 | tf_op jit(solution)/shard_map/psum | solution.py:113
  175.3 6.9 %add_convert_fusion = bf16[5,512,512]{1,2,0:T(8,128)(2,1)S(1)} fusion(f32[5,512,512]{1,2,0:T(8,128)} %get-tuple-element.19, f32[5,512]{1,0:T(8,128)S(1)} %broadcast_select_fusion.6, f32[5,512]{1,0:T(8,128)S(1)} %broadcast_select_fusion.7, f32[5,512]{1,0:T(8,128)S(1)} %broadcast_select_fusion.8, f32[5,512]{1,0:T(8,128)S(1)} %get-tuple-element.11, ...), kind=kLoop, calls=%fused_computation.15 | loop fusion | flops 26214400 | bytes 7956485 | tf_op jit(solution)/shard_map/convert_element_type | solution.py:141
  182.2 1.1 convolution_multiply_fusion.1
  183.4 3.5 %fusion.9 = f32[4,512,256]{2,0,1:T(4,128)S(1)} fusion(f32[5,512,256]{2,1,0:T(8,128)S(1)} %convolution_multiply_fusion.1, pred[5,4]{0,1:T(4,128)(4,1)S(1)} %get-tuple-element.13), kind=kOutput, calls=%fused_computation.36 | convolution fusion | flops 31457280 | bytes 4718612 | tf_op jit(solution)/shard_map/ka,kid->aid/dot_general | solution.py:148
  186.8 1.7 copy.23
  188.6 2.7 convolution_multiply_fusion
  191.2 3.5 %fusion.7 = f32[4,512,256]{2,0,1:T(4,128)S(1)} fusion(f32[5,512,256]{2,1,0:T(8,128)S(1)} %convolution_multiply_fusion, pred[5,4]{0,1:T(4,128)(4,1)S(1)} %get-tuple-element.12), kind=kOutput, calls=%fused_computation.34 | convolution fusion | flops 31457280 | bytes 4718612 | tf_op jit(solution)/shard_map/ka,kjd->ajd/dot_general | solution.py:151
  195.1 62.6 %all-reduce.1 = bf16[2048,256]{1,0:T(8,128)(2,1)} all-reduce(f32[2048,256]{1,0:T(8,128)S(1)} %bitcast.40), channel_id=1, replica_groups=mesh['groups'=2,'row'=4,'col'=2,'rep'=2] {'row','rep'}, use_global_device_ids=true, to_apply=%region_40.43 | all-reduce | flops 524288 | bytes 3145728 | tf_op jit(solution)/shard_map/psum | solution.py:157
  257.7 1.8 convert_element_type.46
  (104 shorter events, 15.1 us)
Async XLA Ops:
  7.2 6.5 %copy-start = (bf16[2048,256]{1,0:T(8,128)(2,1)S(1)}, bf16[2048,256]{1,0:T(8,128)(2,1)}, u32[]{:S(2)}) copy-start(bf16[2048,256]{1,0:T(8,128)(2,1)} %param.13) | copy-start | bytes 3145732
  7.2 250.6 %reduce-scatter.2.cloned.1.call-start = ((), (), s32[]{:S(2)}) async-start(), calls=%async_computation.1 | async-start | bytes 2621440 | tf_op jit(solution)/shard_map/reduce_scatter | solution.py:154
  117.8 28.7 %copy-start.2 = (f32[2048]{0:T(1024)S(1)}, f32[2048]{0:T(1024)}, u32[]{:S(2)}) copy-start(f32[2048]{0:T(1024)} %param.15) | copy-start | bytes 24580
  175.2 7.0 %copy-start.1 = (bf16[5,512,256]{2,1,0:T(8,128)(2,1)S(1)}, bf16[5,512,256]{2,1,0:T(8,128)(2,1)}, u32[]{:S(2)}) copy-start(bf16[5,512,256]{2,1,0:T(8,128)(2,1)} %gather_fusion.2) | copy-start | bytes 3932164
  182.2 6.3 %copy-start.3 = (bf16[5,512,512]{1,2,0:T(8,128)(2,1)}, bf16[5,512,512]{1,2,0:T(8,128)(2,1)S(1)}, u32[]{:S(2)}) copy-start(bf16[5,512,512]{1,2,0:T(8,128)(2,1)S(1)} %add_convert_fusion) | copy-start | bytes 7864324
Sparse Core Ops, SparseCore 0:
  188.7 29.6 reduce-scatter.1
where the time goes:
time: 267 us; the launch traced here: 266 us
  blocking collectives  175 us (66%)
  other arithmetic  44.4 us (17%)
  local copies, waits for them, and re-layouts  17.3 us (6%)
  matrix products  15.5 us (6%)
  between operations  14.5 us (5%)
    psum x1, blocking collectives, shards(): grad_target = lax.psum(target_rows, ('row', 'rep')).astype(jnp.bfloat16)  62.6 us
    pmax x2, blocking collectives, target_step(): largest = lax.pmax(largest_columns(jnp.max(scores, axis=1)), ('row', 'rep'))  30.7 us
    psum x2, blocking collectives, target_step(): totals = lax.psum(add_columns(jnp.sum(shifted, axis=1)), ('row', 'rep'))  27.8 us
    pmax x2, blocking collectives, source_step(): largest = lax.pmax(largest_rows(jnp.max(scores, axis=2)), ('col', 'rep'))  14.6 us
    psum x1, blocking collectives, shards(): lax.psum(add_columns(jnp.sum(addend, axis=1)), ('row', 'rep'))  13.9 us
    psum x2, blocking collectives, source_adjoint(): return lax.psum(add_rows(values), ('col', 'rep'))  13.2 us
    psum x2, blocking collectives, source_step(): totals = lax.psum(add_rows(jnp.sum(shifted, axis=2)), ('col', 'rep'))  11.6 us
    convert_element_type x1, other arithmetic, shards(): rounded = bar_cost.astype(jnp.bfloat16)  6.89 us
  transfers between devices with their start and end apart: 1, of which 0 were waited for; matrix products, arithmetic and copies ran while one was open for 2% of the time, Pallas kernels for 0%

commit v1 on v0

v1 whole, which is shorter than its diff:
```python
import functools
import math

import jax
import jax.numpy as jnp
from jax import lax
from jax.experimental import pallas as pl
from jax.experimental.pallas import tpu as pltpu
from jax.sharding import PartitionSpec as P

TILE = 512
HALF = 256
BLOCK = 4
LANES = 128
ROWS = 64
LIMIT = 24 * 1024 * 1024
LOWEST = -1e30
F32 = jnp.float32
NT_DIMS = (((1,), (1,)), ((), ()))
NN_DIMS = (((1,), (0,)), ((), ()))
TN_DIMS = (((0,), (0,)), ((), ()))


def kept_range(first_cut, second_cut, straight, tile):
    is_low = (tile < first_cut).astype(jnp.int32) == straight
    return jnp.where(is_low, 0, second_cut), jnp.where(is_low, second_cut, BLOCK)


def read_meta(meta_ref):
    return meta_ref[0, 0], meta_ref[0, 1], meta_ref[0, 2]


def to_column(row):
    return jnp.broadcast_to(row, (LANES, row.shape[1])).T


def lane_sums(values):
    return jnp.sum(values.T, axis=0, keepdims=True)


def total(refs, index):
    value = refs[0][index]
    for ref in refs[1:]:
        value = value + ref[index]
    return value


def weighted_rows(e_ref, meta, vector_ref, out_ref):
    for s in range(BLOCK):
        low, high = kept_range(*meta, s)
        for start in range(0, TILE, HALF):

            def step(t, acc):
                vector = vector_ref[t]
                parts = []
                for at in range(0, HALF, ROWS):
                    e = e_ref[s, t, start + at : start + at + ROWS, :]
                    parts.append(
                        acc[at : at + ROWS]
                        + (e[:, :LANES] * vector[:, :LANES] + e[:, LANES:] * vector[:, LANES:])
                    )
                return jnp.concatenate(parts, axis=0)

            acc = lax.fori_loop(low, high, step, jnp.zeros((HALF, LANES), F32))
            out_ref[s, :, start : start + HALF] = lane_sums(acc)


def weighted_columns(e_ref, meta, rows, column_ref, eight_ref):
    eight_ref[...] = jnp.zeros_like(eight_ref)
    for s in range(BLOCK):
        low, high = kept_range(*meta, s)
        column_ref[...] = to_column(rows(s))

        def step(t, carry):
            left = jnp.zeros((8, LANES), F32)
            right = jnp.zeros((8, LANES), F32)
            for at in range(0, TILE, ROWS):
                e = e_ref[s, t, at : at + ROWS, :]
                u = column_ref[at : at + ROWS, :]
                left = left + jnp.sum((e[:, :LANES] * u).reshape(-1, 8, LANES), axis=0)
                right = right + jnp.sum((e[:, LANES:] * u).reshape(-1, 8, LANES), axis=0)
            eight_ref[t, :, :LANES] += left
            eight_ref[t, :, LANES:] += right
            return carry

        lax.fori_loop(low, high, step, 0)


def first_source_kernel(
    x_ref, y_ref, warm_ref, sb_ref, tb_ref, kp_ref, e_ref, out_ref, meta_ref, largest_ref
):
    row_pos = lax.axis_index("row")
    col_pos = lax.axis_index("col")
    rep_pos = lax.axis_index("rep")
    first_cut = sb_ref[2 * row_pos + 1] - BLOCK * row_pos
    second_cut = tb_ref[2 * col_pos + 1] - BLOCK * col_pos

    def look(i, found):
        here = (kp_ref[i, 0] == 2 * row_pos) & (kp_ref[i, 1] == 2 * col_pos)
        return found | here.astype(jnp.int32)

    straight = lax.fori_loop(0, kp_ref.shape[0], look, jnp.int32(0))
    lanes = lax.broadcasted_iota(jnp.int32, meta_ref.shape, 1)
    meta_ref[...] = jnp.where(lanes == 0, first_cut, jnp.where(lanes == 1, second_cut, straight))
    meta = (first_cut, second_cut, straight)
    inv_root = x_ref.shape[1] ** (-0.5)
    for s in range(BLOCK):
        low, high = kept_range(*meta, s)
        largest_ref[...] = jnp.full_like(largest_ref, LOWEST)

        def score(t, carry):
            warm = warm_ref[2 * t + rep_pos]
            y = y_ref[pl.ds(pl.multiple_of(t * TILE + rep_pos * HALF, HALF), HALF), :]
            for at in range(0, TILE, HALF):
                x = x_ref[s * TILE + at : s * TILE + at + HALF, :]
                scores = lax.dot_general(x, y, NT_DIMS, preferred_element_type=F32) * inv_root
                e_ref[s, t, at : at + HALF, :] = scores
                shifted = scores + warm
                largest_ref[at : at + HALF, :] = jnp.maximum(
                    largest_ref[at : at + HALF, :],
                    jnp.maximum(shifted[:, :LANES], shifted[:, LANES:]),
                )
            return carry

        lax.fori_loop(low, high, score, 0)
        for start in range(0, TILE, HALF):
            largest = jnp.max(largest_ref[start : start + HALF, :], axis=1, keepdims=True)
            largest = jnp.broadcast_to(largest, (HALF, LANES))

            def step(t, acc):
                warm = warm_ref[2 * t + rep_pos]
                parts = []
                for at in range(0, HALF, ROWS):
                    e = e_ref[s, t, start + at : start + at + ROWS, :]
                    m = largest[at : at + ROWS]
                    parts.append(
                        acc[at : at + ROWS]
                        + jnp.exp(e[:, :LANES] + warm[:, :LANES] - m)
                        + jnp.exp(e[:, LANES:] + warm[:, LANES:] - m)
                    )
                return jnp.concatenate(parts, axis=0)

            acc = lax.fori_loop(low, high, step, jnp.zeros((HALF, LANES), F32))
            out_ref[s, :, start : start + HALF] = largest.T[:1]
            out_ref[BLOCK + s, :, start : start + HALF] = lane_sums(acc)


def combine(refs, at, offset):
    largest = refs[0][at]
    for ref in refs[1:]:
        largest = jnp.maximum(largest, ref[at])
    sums = refs[0][offset + at] * jnp.exp(refs[0][at] - largest)
    for ref in refs[1:]:
        sums = sums + ref[offset + at] * jnp.exp(ref[at] - largest)
    return -(largest + jnp.log(sums))


def first_target_kernel(count, *args):
    parts = args[:count]
    score_ref, meta_ref, e_ref, out_ref, column_ref, eight_ref = args[count:]
    meta = read_meta(meta_ref)
    eight_ref[...] = jnp.full_like(eight_ref, LOWEST)
    for s in range(BLOCK):
        low, high = kept_range(*meta, s)
        column_ref[s] = to_column(combine(parts, s, BLOCK))

        def peak(t, carry):
            left = eight_ref[t, :, :LANES]
            right = eight_ref[t, :, LANES:]
            for at in range(0, TILE, ROWS):
                e = score_ref[s, t, at : at + ROWS, :]
                u = column_ref[s, at : at + ROWS, :]
                left = jnp.maximum(left, jnp.max((e[:, :LANES] + u).reshape(-1, 8, LANES), axis=0))
                right = jnp.maximum(
                    right, jnp.max((e[:, LANES:] + u).reshape(-1, 8, LANES), axis=0)
                )
            eight_ref[t, :, :LANES] = left
            eight_ref[t, :, LANES:] = right
            return carry

        lax.fori_loop(low, high, peak, 0)
    for t in range(BLOCK):
        out_ref[t] = jnp.max(eight_ref[t], axis=0, keepdims=True)
    eight_ref[...] = jnp.zeros_like(eight_ref)
    for s in range(BLOCK):
        low, high = kept_range(*meta, s)

        def step(t, carry):
            largest = out_ref[t]
            left = jnp.zeros((8, LANES), F32)
            right = jnp.zeros((8, LANES), F32)
            for at in range(0, TILE, ROWS):
                e = score_ref[s, t, at : at + ROWS, :]
                u = column_ref[s, at : at + ROWS, :]
                e_left = jnp.exp(e[:, :LANES] + u - largest[:, :LANES])
                e_right = jnp.exp(e[:, LANES:] + u - largest[:, LANES:])
                e_ref[s, t, at : at + ROWS, :LANES] = e_left
                e_ref[s, t, at : at + ROWS, LANES:] = e_right
                left = left + jnp.sum(e_left.reshape(-1, 8, LANES), axis=0)
                right = right + jnp.sum(e_right.reshape(-1, 8, LANES), axis=0)
            eight_ref[t, :, :LANES] += left
            eight_ref[t, :, LANES:] += right
            return carry

        lax.fori_loop(low, high, step, 0)
    for t in range(BLOCK):
        out_ref[BLOCK + t] = jnp.sum(eight_ref[t], axis=0, keepdims=True)


def second_source_kernel(count, *args):
    parts = args[:count]
    warm_ref, e_ref, meta_ref, out_ref, q_ref, wq_ref = args[count:]
    rep_pos = lax.axis_index("rep")
    for t in range(BLOCK):
        potential = combine(parts, t, BLOCK)
        q = jnp.exp(parts[0][t] + potential)
        q_ref[t] = q
        wq_ref[t] = q * jnp.exp(warm_ref[2 * t + rep_pos] - potential)
    weighted_rows(e_ref, read_meta(meta_ref), q_ref, out_ref)


def second_target_kernel(count, *args):
    parts = args[:count]
    e_ref, meta_ref, q_ref, out_ref, a_ref, column_ref, eight_ref = args[count:]
    for s in range(BLOCK):
        a_ref[s] = 1.0 / total(parts, s)
    weighted_columns(e_ref, read_meta(meta_ref), lambda s: a_ref[s], column_ref, eight_ref)
    for t in range(BLOCK):
        out_ref[t] = q_ref[t] * jnp.sum(eight_ref[t], axis=0, keepdims=True)


def late_kernel(count, *args):
    parts = args[:count]
    e_ref, meta_ref, q_ref, weight_ref, out_ref, p_ref = args[count:]
    rep_pos = lax.axis_index("rep")
    for t in range(BLOCK):
        p_ref[t] = weight_ref[2 * t + rep_pos] * q_ref[t] / total(parts, t)
    weighted_rows(e_ref, read_meta(meta_ref), p_ref, out_ref)


def mid_kernel(count, *args):
    parts = args[:count]
    e_ref, meta_ref, q_ref, a_ref, weight_ref, out_ref, b_ref, column_ref, eight_ref = args[count:]
    for s in range(BLOCK):
        a = a_ref[s]
        b_ref[s] = a * (weight_ref[s] - a * total(parts, s))
    weighted_columns(e_ref, read_meta(meta_ref), lambda s: b_ref[s], column_ref, eight_ref)
    for t in range(BLOCK):
        out_ref[t] = -q_ref[t] * jnp.sum(eight_ref[t], axis=0, keepdims=True)


def early_kernel(count, *args):
    parts = args[:count]
    e_ref, meta_ref, q_ref, out_ref, h_ref = args[count:]
    for t in range(BLOCK):
        h_ref[t] = q_ref[t] * total(parts, t)
    weighted_rows(e_ref, read_meta(meta_ref), h_ref, out_ref)


def gradient_kernel(count, others, rows, *args):
    parts = args[:count]
    args = args[count:]
    x_ref, y_ref, e_ref, meta_ref, a_ref, b_ref, p_ref, q_ref, h_ref, wq_ref = args[:10]
    source_refs = args[10 : 10 + others]
    target_refs = args[10 + others : 10 + others + rows]
    a_col, b_col, early_col, bar_ref, source_acc, target_acc = args[10 + others + rows :]
    rep_pos = lax.axis_index("rep")
    own = lax.axis_index("col") * 2 + rep_pos
    row_pos = lax.axis_index("row")
    meta = read_meta(meta_ref)
    inv_root = x_ref.shape[1] ** (-0.5)
    target_acc[...] = jnp.zeros_like(target_acc)
    source_acc[...] = jnp.zeros_like(source_acc)
    for s in range(BLOCK):
        low, high = kept_range(*meta, s)
        a_col[...] = to_column(a_ref[s])
        b_col[...] = to_column(b_ref[s])
        early_col[...] = to_column(-total(parts, s))

        def step(t, carry):
            p, q, h, wq = p_ref[t], q_ref[t], h_ref[t], wq_ref[t]
            for at in range(0, TILE, ROWS):
                e = e_ref[s, t, at : at + ROWS, :]
                a = a_col[at : at + ROWS, :]
                b = b_col[at : at + ROWS, :]
                early = early_col[at : at + ROWS, :]
                for side in (slice(0, LANES), slice(LANES, HALF)):
                    factor = a * p[:, side] + b * q[:, side] + (h[:, side] + early * wq[:, side])
                    bar_ref[at : at + ROWS, side] = (e[:, side] * factor).astype(jnp.bfloat16)
            y = y_ref[pl.ds(pl.multiple_of(t * TILE + rep_pos * HALF, HALF), HALF), :]
            bar = bar_ref[...]
            source_acc[s * TILE : (s + 1) * TILE, :] += lax.dot_general(
                bar, y, NN_DIMS, preferred_element_type=F32
            )
            x = x_ref[s * TILE : (s + 1) * TILE, :]
            begin = pl.multiple_of(t * HALF, HALF)
            target_acc[pl.ds(begin, HALF), :] += lax.dot_general(
                bar, x, TN_DIMS, preferred_element_type=F32
            )
            return carry

        lax.fori_loop(low, high, step, 0)
    for refs, acc, position in (
        (source_refs, source_acc, own),
        (target_refs, target_acc, row_pos),
    ):
        piece = acc.shape[0] // len(refs)
        for k, ref in enumerate(refs):
            begin = pl.multiple_of((position ^ k) * piece, piece)
            ref[...] = (-inv_root * acc[pl.ds(begin, piece), :]).astype(ref.dtype)


def place_kernel(rows, *args):
    own, other, out_ref = args[:rows], args[rows : 2 * rows], args[2 * rows]
    rep_pos = lax.axis_index("rep")
    row_pos = lax.axis_index("row")
    piece = own[0].shape[0]
    per_tile = HALF // piece
    for refs, rep in ((own, rep_pos), (other, 1 - rep_pos)):
        for k, ref in enumerate(refs):
            at = row_pos ^ k
            begin = (at // per_tile) * TILE + rep * HALF + (at % per_tile) * piece
            out_ref[pl.ds(pl.multiple_of(begin, piece), piece), :] = ref[...]


def in_vmem(value):
    return pltpu.with_memory_space_constraint(value, pltpu.VMEM)


def call(kernel, name, outs, scratch, args, spaces=None):
    specs = [
        pl.BlockSpec(memory_space=pltpu.VMEM if spaces is None else spaces[i])
        for i in range(len(args))
    ]
    args = [
        in_vmem(value) if spaces is None or spaces[i] == pltpu.VMEM else value
        for i, value in enumerate(args)
    ]
    return pl.pallas_call(
        kernel,
        name=name,
        out_shape=[pltpu.VMEM(shape, dtype) for shape, dtype in outs],
        in_specs=specs,
        out_specs=[pl.BlockSpec(memory_space=pltpu.VMEM) for _ in outs],
        scratch_shapes=scratch,
        compiler_params=pltpu.CompilerParams(vmem_limit_bytes=LIMIT),
    )(*args)


def shards(
    sizes,
    source_emb,
    target_emb,
    warm_start,
    source_weight,
    target_weight,
    source_bounds,
    target_bounds,
    kept_pairs,
):
    width = source_emb.shape[1]

    def swap(value, axes, k):
        count = math.prod(sizes[axis] for axis in axes)
        return lax.ppermute(value, axes, [(i, i ^ k) for i in range(count)])

    def spread(value, axes):
        count = math.prod(sizes[axis] for axis in axes)
        return [value] + [swap(value, axes, k) for k in range(1, count)]

    over_source = ("col", "rep")
    over_target = ("row",)
    warm = warm_start.reshape(2 * BLOCK, 1, HALF)
    target_weight = target_weight.reshape(2 * BLOCK, 1, HALF)
    source_weight = source_weight.reshape(BLOCK, 1, TILE)
    source_vector = ((BLOCK, 1, TILE), F32)
    target_vector = ((BLOCK, 1, HALF), F32)
    matrix = ((BLOCK, BLOCK, TILE, HALF), F32)
    column = pltpu.VMEM((TILE, LANES), F32)
    eight = pltpu.VMEM((BLOCK, 8, HALF), F32)
    vmem, smem = pltpu.VMEM, pltpu.SMEM

    score, packed, meta = call(
        first_source_kernel,
        "first_source",
        [matrix, ((2 * BLOCK, 1, TILE), F32), ((8, LANES), jnp.int32)],
        [column],
        [source_emb, target_emb, warm, source_bounds, target_bounds, kept_pairs],
        [vmem, vmem, vmem, smem, smem, smem],
    )
    parts = spread(packed, over_source)
    n_source = len(parts)
    e, packed = call(
        functools.partial(first_target_kernel, n_source),
        "first_target",
        [matrix, ((2 * BLOCK, 1, HALF), F32)],
        [pltpu.VMEM((BLOCK, TILE, LANES), F32), eight],
        [*parts, score, meta],
    )
    parts = spread(packed, over_target)
    n_target = len(parts)
    sums, q, wq = call(
        functools.partial(second_source_kernel, n_target),
        "second_source",
        [source_vector, target_vector, target_vector],
        [],
        [*parts, warm, e, meta],
    )
    parts = spread(sums, over_source)
    sums, a = call(
        functools.partial(second_target_kernel, n_source),
        "second_target",
        [target_vector, source_vector],
        [column, eight],
        [*parts, e, meta, q],
    )
    parts = spread(sums, over_target)
    sums, p = call(
        functools.partial(late_kernel, n_target),
        "late",
        [source_vector, target_vector],
        [],
        [*parts, e, meta, q, target_weight],
    )
    parts = spread(sums, over_source)
    sums, b = call(
        functools.partial(mid_kernel, n_source),
        "mid",
        [target_vector, source_vector],
        [column, eight],
        [*parts, e, meta, q, a, source_weight],
    )
    parts = spread(sums, over_target)
    sums, h = call(
        functools.partial(early_kernel, n_target),
        "early",
        [source_vector, target_vector],
        [],
        [*parts, e, meta, q],
    )
    parts = spread(sums, over_source)
    rows = sizes["row"]
    source_piece = BLOCK * TILE // n_source
    target_piece = BLOCK * HALF // rows
    outs = call(
        functools.partial(gradient_kernel, n_source, n_source, rows),
        "gradient",
        [((source_piece, width), F32 if k == 0 else jnp.bfloat16) for k in range(n_source)]
        + [((target_piece, width), F32 if k == 0 else jnp.bfloat16) for k in range(rows)],
        [
            column,
            column,
            column,
            pltpu.VMEM((TILE, HALF), jnp.bfloat16),
            pltpu.VMEM((BLOCK * TILE, width), F32),
            pltpu.VMEM((BLOCK * HALF, width), F32),
        ],
        [*parts, source_emb, target_emb, e, meta, a, b, p, q, h, wq],
    )
    source_parts, target_parts = outs[:n_source], outs[n_source:]

    def reduced(pieces, axes):
        value = pieces[0]
        for k in range(1, len(pieces)):
            value = value + swap(pieces[k], axes, k).astype(F32)
        return value.astype(jnp.bfloat16)

    target_rows = reduced(target_parts, over_target)
    grad_source = reduced(source_parts, over_source)
    pieces = spread(target_rows, over_target)
    pieces = pieces + [swap(value, ("rep",), 1) for value in pieces]
    grad_target = pl.pallas_call(
        functools.partial(place_kernel, rows),
        name="place",
        out_shape=jax.ShapeDtypeStruct(target_emb.shape, jnp.bfloat16),
        in_specs=[pl.BlockSpec(memory_space=pltpu.VMEM)] * len(pieces),
        out_specs=pl.BlockSpec(memory_space=pltpu.VMEM),
        compiler_params=pltpu.CompilerParams(vmem_limit_bytes=LIMIT),
    )(*pieces)
    return grad_source, grad_target


def solution(mesh):
    return jax.shard_map(
        functools.partial(shards, dict(mesh.shape)),
        mesh=mesh,
        in_specs=(
            P(("groups", "row"), None),
            P(("groups", "col"), None),
            P(("groups", "col")),
            P(("groups", "row")),
            P(("groups", "col")),
            P("groups"),
            P("groups"),
            P("groups", None),
        ),
        out_specs=(P(("groups", "row", "col", "rep"), None), P(("groups", "col"), None)),
        check_vma=False,
    )
```

time: 267 us -> 98.7 us (0.37)
  blocking collectives: 175 us -> 0 us
  other arithmetic: 44.4 us -> 0.91 us
  starting transfers between devices: 0.04 us -> 43 us
  waiting for transfers between devices: 0.02 us -> 31 us
  Pallas kernels: 0 us -> 17.7 us
  matrix products: 15.5 us -> 0 us
  between operations: 14.5 us -> 0.76 us
  local copies, waits for them, and re-layouts: 17.3 us -> 5.22 us
    psum x8 -> x0, blocking collectives: 129 us -> none  [the longest x1 62.6 us: shards(): grad_target = lax.psum(target_rows, ('row', 'rep')).astype(jnp.bfloat16)]
    pmax x4 -> x0, blocking collectives: 45.3 us -> none  [the longest x2 30.7 us: target_step(): largest = lax.pmax(largest_columns(jnp.max(scores, axis=1)), ('row', 'rep'))]
    ppermute x0 -> x34, starting transfers between devices: none -> 43 us  [swap(): return lax.ppermute(value, axes, [(i, i ^ k) for i in range(count)])]
    ppermute x0 -> x34, waiting for transfers between devices: none -> 31 us  [swap(): return lax.ppermute(value, axes, [(i, i ^ k) for i in range(count)])]
    reduce_sum x17 -> x0, other arithmetic: 24.4 us -> none  [the longest x2 6.82 us: target_step(): totals = lax.psum(add_columns(jnp.sum(shifted, axis=1)), ('row', 'rep'))]
    pallas_call x0 -> x9, Pallas kernels: none -> 17.7 us  [the longest x8 16.7 us: call(): pl.pallas_call(kernel, name=name, out_shape=[pltpu.VMEM(shape, dtype) for...]
    dot_general x5 -> x0, matrix products: 15.5 us -> none  [the longest x1 4.75 us: shards(): jnp.einsum('kid,kjd->kij', x_tiles, y_tiles, preferred_element_type=jnp.f...]
    gather x15 -> x0, local copies, waits for them, and re-layouts: 10.9 us -> none  [the longest x7 3.91 us: columns_of(): return jnp.take(vector.reshape(tgt_count, TILE), tgt_slot, axis=0)]
  transfers between devices with their start and end apart: 1 -> 34, of which waited for: 0 -> 21; matrix products, arithmetic and copies ran while one was open for 2% -> 1% of each run, Pallas kernels for 0% -> 0%
where the time goes in v1:
time: 98.7 us; the launch traced here: 98.6 us
  starting transfers between devices  43 us (44%)
  waiting for transfers between devices  31 us (31%)
  Pallas kernels  17.7 us (18%)
  local copies, waits for them, and re-layouts  5.22 us (5%)
    ppermute x34, starting transfers between devices, swap(): return lax.ppermute(value, axes, [(i, i ^ k) for i in range(count)])  43 us
    ppermute x34, waiting for transfers between devices, swap(): return lax.ppermute(value, axes, [(i, i ^ k) for i in range(count)])  31 us
    pallas_call x8, Pallas kernels, call(): pl.pallas_call(kernel, name=name, out_shape=[pltpu.VMEM(shape, dtype) for...  16.7 us
    unnamed x17, local copies, waits for them, and re-layouts  5.22 us
  transfers between devices with their start and end apart: 34, of which 21 were waited for; matrix products, arithmetic and copies ran while one was open for 1% of the time, Pallas kernels for 0%

profile of v1, /device:TPU:0, one launch (start us, length us, event | category | flops | bytes accessed | tf_op | source)
XLA Modules:
  0.0 98.6 jit_solution(15118425327126999591)
XLA Ops:
  1.4 1.2 %copy-done = bf16[2048,256]{1,0:T(8,128)(2,1)S(1)} copy-done((bf16[2048,256]{1,0:T(8,128)(2,1)S(1)}, bf16[2048,256]{1,0:T(8,128)(2,1)}, u32[]{:S(2)}) %copy-start) | copy-done | bytes 1048600
  2.6 1.2 %copy-done.2 = bf16[2048,256]{1,0:T(8,128)(2,1)S(1)} copy-done((bf16[2048,256]{1,0:T(8,128)(2,1)S(1)}, bf16[2048,256]{1,0:T(8,128)(2,1)}, u32[]{:S(2)}) %copy-start.2) | copy-done | bytes 1048600
  5.8 5.0 %first_source.1 = (f32[4,4,512,256]{3,2,1,0:T(8,128)S(1)}, f32[8,1,512]{2,1,0:T(1,128)S(1)}, s32[8,128]{1,0:T(8,128)S(1)}) custom-call(bf16[2048,256]{1,0:T(8,128)(2,1)S(1)} %copy-done, bf16[2048,256]{1,0:T(8,128)(2,1)S(1)} %copy-done.2, f32[8,1,256]{2,1,0:T(1,128)S(1)} %bitcast.3, s32[9]{0:T(128)S(1)} %copy-done.6, s32[5]{0:T(128)S(1)} %copy-done.7, ...), custom_call_target="tpu_custom_call" | custom-call | tf_op jit(solution)/shard_map/first_source/pallas_call | solution.py:339
  10.8 4.0 %collective-permute-start.2 = (f32[8,1,512]{2,1,0:T(1,128)S(1)}, f32[8,1,512]{2,1,0:T(1,128)S(1)}, u32[]{:S(2)}, u32[]{:S(2)}) collective-permute-start(f32[8,1,512]{2,1,0:T(1,128)S(1)} %get-tuple-element.26.args_0_), channel_id=1, source_target_pairs={{0,3},{1,2},{2,1},{3,0},{4,7},{5,6},{6,5},{7,4},{8,11},{9,10},{10,... | collective-permute-start | bytes 49160 | tf_op jit(solution)/shard_map/ppermute | solution.py:365
  16.3 2.3 %collective-permute-done.1.args_2_ = f32[8,1,512]{2,1,0:T(1,128)S(1)} collective-permute-done((f32[8,1,512]{2,1,0:T(1,128)S(1)}, f32[8,1,512]{2,1,0:T(1,128)S(1)}, u32[]{:S(2)}, u32[]{:S(2)}) %collective-permute-start.1) | collective-permute-done | bytes 16416 | tf_op jit(solution)/shard_map/ppermute | solution.py:365
  18.6 1.7 %first_target.1 = (f32[4,4,512,256]{3,2,1,0:T(8,128)S(1)}, f32[8,1,256]{2,1,0:T(1,128)S(1)}) custom-call(f32[8,1,512]{2,1,0:T(1,128)S(1)} %get-tuple-element.26.args_0_, f32[8,1,512]{2,1,0:T(1,128)S(1)} %collective-permute-done.args_1_, f32[8,1,512]{2,1,0:T(1,128)S(1)} %collective-permute-done.1.args_2_, f32[8,1,512]{2,1,0:T(1,128)S(1)} %collective-permute-done.2.args_3_, ...), custom_call_target="tpu_custom_call" | custom-call | tf_op jit(solution)/shard_map/first_target/pallas_call | solution.py:339
  20.3 4.3 %collective-permute-start.5 = (f32[8,1,256]{2,1,0:T(1,128)S(1)}, f32[8,1,256]{2,1,0:T(1,128)S(1)}, u32[]{:S(2)}, u32[]{:S(2)}) collective-permute-start(f32[8,1,256]{2,1,0:T(1,128)S(1)} %get-tuple-element.29.args_0_), channel_id=1, source_target_pairs={{0,12},{4,8},{8,4},{12,0},{1,13},{5,9},{9,5},{13,1},{2,14},{6,10},... | collective-permute-start | bytes 24584 | tf_op jit(solution)/shard_map/ppermute | solution.py:365
  26.3 2.9 %collective-permute-done.4.args_2_ = f32[8,1,256]{2,1,0:T(1,128)S(1)} collective-permute-done((f32[8,1,256]{2,1,0:T(1,128)S(1)}, f32[8,1,256]{2,1,0:T(1,128)S(1)}, u32[]{:S(2)}, u32[]{:S(2)}) %collective-permute-start.4) | collective-permute-done | bytes 8224 | tf_op jit(solution)/shard_map/ppermute | solution.py:365
  29.2 1.3 %second_source.1 = (f32[4,1,512]{2,1,0:T(1,128)S(1)}, f32[4,1,256]{2,1,0:T(1,128)S(1)}, f32[4,1,256]{2,1,0:T(1,128)S(1)}) custom-call(f32[8,1,256]{2,1,0:T(1,128)S(1)} %get-tuple-element.29.args_0_, f32[8,1,256]{2,1,0:T(1,128)S(1)} %collective-permute-done.3.args_1_, f32[8,1,256]{2,1,0:T(1,128)S(1)} %collective-permute-done.4.args_2_, ...), custom_call_target="tpu_custom_call" | custom-call | tf_op jit(solution)/shard_map/second_source/pallas_call | solution.py:339
  32.5 1.2 %collective-permute-done.8.args_3_ = f32[4,1,512]{2,1,0:T(1,128)S(1)} collective-permute-done((f32[4,1,512]{2,1,0:T(1,128)S(1)}, f32[4,1,512]{2,1,0:T(1,128)S(1)}, u32[]{:S(2)}, u32[]{:S(2)}) %collective-permute-start.8) | collective-permute-done | bytes 8224 | tf_op jit(solution)/shard_map/ppermute | solution.py:365
  35.4 2.0 %collective-permute-start.11 = (f32[4,1,256]{2,1,0:T(1,128)S(1)}, f32[4,1,256]{2,1,0:T(1,128)S(1)}, u32[]{:S(2)}, u32[]{:S(2)}) collective-permute-start(f32[4,1,256]{2,1,0:T(1,128)S(1)} %get-tuple-element.33.args_0_), channel_id=1, source_target_pairs={{0,12},{4,8},{8,4},{12,0},{1,13},{5,9},{9,5},{13,1},{2,14},{6,10},... | collective-permute-start | bytes 12296 | tf_op jit(solution)/shard_map/ppermute | solution.py:365
  37.6 2.3 %collective-permute-start.9 = (f32[4,1,256]{2,1,0:T(1,128)S(1)}, f32[4,1,256]{2,1,0:T(1,128)S(1)}, u32[]{:S(2)}, u32[]{:S(2)}) collective-permute-start(f32[4,1,256]{2,1,0:T(1,128)S(1)} %get-tuple-element.33.args_0_), channel_id=1, source_target_pairs={{0,4},{4,0},{8,12},{12,8},{1,5},{5,1},{9,13},{13,9},{2,6},{6,2},{1... | collective-permute-start | bytes 12296 | tf_op jit(solution)/shard_map/ppermute | solution.py:365
  41.9 1.3 %late.1 = (f32[4,1,512]{2,1,0:T(1,128)S(1)}, f32[4,1,256]{2,1,0:T(1,128)S(1)}) custom-call(f32[4,1,256]{2,1,0:T(1,128)S(1)} %get-tuple-element.33.args_0_, f32[4,1,256]{2,1,0:T(1,128)S(1)} %collective-permute-done.9.args_1_, f32[4,1,256]{2,1,0:T(1,128)S(1)} %collective-permute-done.10.args_2_, f32[4,1,256]{2,1,0:T(1,128)S(1)} %collective-permute-done.11.args_3_, ...), custom_call_target="tpu_custom_call" | custom-call | tf_op jit(solution)/shard_map/late/pallas_call | solution.py:339
  45.2 1.2 %collective-permute-done.14.args_3_ = f32[4,1,512]{2,1,0:T(1,128)S(1)} collective-permute-done((f32[4,1,512]{2,1,0:T(1,128)S(1)}, f32[4,1,512]{2,1,0:T(1,128)S(1)}, u32[]{:S(2)}, u32[]{:S(2)}) %collective-permute-start.14) | collective-permute-done | bytes 8224 | tf_op jit(solution)/shard_map/ppermute | solution.py:365
  48.2 2.6 %collective-permute-start.17 = (f32[4,1,256]{2,1,0:T(1,128)S(1)}, f32[4,1,256]{2,1,0:T(1,128)S(1)}, u32[]{:S(2)}, u32[]{:S(2)}) collective-permute-start(f32[4,1,256]{2,1,0:T(1,128)S(1)} %get-tuple-element.36.args_0_), channel_id=1, source_target_pairs={{0,12},{4,8},{8,4},{12,0},{1,13},{5,9},{9,5},{13,1},{2,14},{6,10},... | collective-permute-start | bytes 12296 | tf_op jit(solution)/shard_map/ppermute | solution.py:365
  53.6 1.6 %collective-permute-done.16.args_2_ = f32[4,1,256]{2,1,0:T(1,128)S(1)} collective-permute-done((f32[4,1,256]{2,1,0:T(1,128)S(1)}, f32[4,1,256]{2,1,0:T(1,128)S(1)}, u32[]{:S(2)}, u32[]{:S(2)}) %collective-permute-start.16) | collective-permute-done | bytes 4128 | tf_op jit(solution)/shard_map/ppermute | solution.py:365
  55.3 1.3 %early.1 = (f32[4,1,512]{2,1,0:T(1,128)S(1)}, f32[4,1,256]{2,1,0:T(1,128)S(1)}) custom-call(f32[4,1,256]{2,1,0:T(1,128)S(1)} %get-tuple-element.36.args_0_, f32[4,1,256]{2,1,0:T(1,128)S(1)} %collective-permute-done.15.args_1_, f32[4,1,256]{2,1,0:T(1,128)S(1)} %collective-permute-done.16.args_2_, f32[4,1,256]{2,1,0:T(1,128)S(1)} %collective-permute-done.17.args_3_, ...), custom_call_target="tpu_custom_call" | custom-call | tf_op jit(solution)/shard_map/early/pallas_call | solution.py:339
  56.8 1.5 %collective-permute-start.19 = (f32[4,1,512]{2,1,0:T(1,128)S(1)}, f32[4,1,512]{2,1,0:T(1,128)S(1)}, u32[]{:S(2)}, u32[]{:S(2)}) collective-permute-start(f32[4,1,512]{2,1,0:T(1,128)S(1)} %get-tuple-element.37.args_0_), channel_id=1, source_target_pairs={{0,2},{1,3},{2,0},{3,1},{4,6},{5,7},{6,4},{7,5},{8,10},{9,11},{10,... | collective-permute-start | bytes 24584 | tf_op jit(solution)/shard_map/ppermute | solution.py:365
  58.6 1.2 %collective-permute-done.20.args_3_ = f32[4,1,512]{2,1,0:T(1,128)S(1)} collective-permute-done((f32[4,1,512]{2,1,0:T(1,128)S(1)}, f32[4,1,512]{2,1,0:T(1,128)S(1)}, u32[]{:S(2)}, u32[]{:S(2)}) %collective-permute-start.20) | collective-permute-done | bytes 8224 | tf_op jit(solution)/shard_map/ppermute | solution.py:365
  60.5 3.9 %gradient.1 = (f32[512,256]{1,0:T(8,128)S(1)}, bf16[512,256]{1,0:T(8,128)(2,1)S(1)}, bf16[512,256]{1,0:T(8,128)(2,1)S(1)}, bf16[512,256]{1,0:T(8,128)(2,1)S(1)},...) custom-call(f32[4,1,512]{2,1,0:T(1,128)S(1)} %get-tuple-element.37.a, ...), custom_call_target="tpu_custom_call" | custom-call | tf_op jit(solution)/shard_map/gradient/pallas_call | solution.py:339
  64.4 2.9 %collective-permute-start.24 = (bf16[256,256]{1,0:T(8,128)(2,1)S(1)}, bf16[256,256]{1,0:T(8,128)(2,1)S(1)}, u32[]{:S(2)}, u32[]{:S(2)}) collective-permute-start(bf16[256,256]{1,0:T(8,128)(2,1)S(1)} %get-tuple-element.47), channel_id=1, source_target_pairs={{0,4},{4,0},{8,12},{12,8},{1,5},{5,1},{9,13},{13,9},{2,6},{6,2},{1... | collective-permute-start | bytes 393224 | tf_op jit(solution)/shard_map/ppermute | solution.py:365
  67.3 1.1 %collective-permute-start.25 = (bf16[256,256]{1,0:T(8,128)(2,1)S(1)}, bf16[256,256]{1,0:T(8,128)(2,1)S(1)}, u32[]{:S(2)}, u32[]{:S(2)}) collective-permute-start(bf16[256,256]{1,0:T(8,128)(2,1)S(1)} %get-tuple-element.48), channel_id=1, source_target_pairs={{0,8},{4,12},{8,0},{12,4},{1,9},{5,13},{9,1},{13,5},{2,10},{6,14},... | collective-permute-start | bytes 393224 | tf_op jit(solution)/shard_map/ppermute | solution.py:365
  68.4 1.4 %collective-permute-start.26 = (bf16[256,256]{1,0:T(8,128)(2,1)S(1)}, bf16[256,256]{1,0:T(8,128)(2,1)S(1)}, u32[]{:S(2)}, u32[]{:S(2)}) collective-permute-start(bf16[256,256]{1,0:T(8,128)(2,1)S(1)} %get-tuple-element.49), channel_id=1, source_target_pairs={{0,12},{4,8},{8,4},{12,0},{1,13},{5,9},{9,5},{13,1},{2,14},{6,10},... | collective-permute-start | bytes 393224 | tf_op jit(solution)/shard_map/ppermute | solution.py:365
  69.7 2.1 %collective-permute-done.24 = bf16[256,256]{1,0:T(8,128)(2,1)S(1)} collective-permute-done((bf16[256,256]{1,0:T(8,128)(2,1)S(1)}, bf16[256,256]{1,0:T(8,128)(2,1)S(1)}, u32[]{:S(2)}, u32[]{:S(2)}) %collective-permute-start.24) | collective-permute-done | bytes 131104 | tf_op jit(solution)/shard_map/ppermute | solution.py:365
  71.8 7.9 %collective-permute-done.25 = bf16[256,256]{1,0:T(8,128)(2,1)S(1)} collective-permute-done((bf16[256,256]{1,0:T(8,128)(2,1)S(1)}, bf16[256,256]{1,0:T(8,128)(2,1)S(1)}, u32[]{:S(2)}, u32[]{:S(2)}) %collective-permute-start.25) | collective-permute-done | bytes 131104 | tf_op jit(solution)/shard_map/ppermute | solution.py:365
  79.9 1.1 %collective-permute-start.29 = (bf16[256,256]{1,0:T(8,128)(2,1)S(1)}, bf16[256,256]{1,0:T(8,128)(2,1)S(1)}, u32[]{:S(2)}, u32[]{:S(2)}) collective-permute-start(bf16[256,256]{1,0:T(8,128)(2,1)S(1)} %add_convert_fusion.1.args_0_), channel_id=1, source_target_pairs={{0,12},{4,8},{8,4},{12,0},{1,13},{5,9},{9,5},{13,1},{2,14},{6,10},... | collective-permute-start | bytes 393224 | tf_op jit(solution)/shard_map/ppermute | solution.py:365
  81.0 2.8 %collective-permute-start.22 = (bf16[512,256]{1,0:T(8,128)(2,1)S(1)}, bf16[512,256]{1,0:T(8,128)(2,1)S(1)}, u32[]{:S(2)}, u32[]{:S(2)}) collective-permute-start(bf16[512,256]{1,0:T(8,128)(2,1)S(1)} %get-tuple-element.44), channel_id=1, source_target_pairs={{0,2},{1,3},{2,0},{3,1},{4,6},{5,7},{6,4},{7,5},{8,10},{9,11},{10,... | collective-permute-start | bytes 786440 | tf_op jit(solution)/shard_map/ppermute | solution.py:365
  83.9 2.8 %collective-permute-start.28 = (bf16[256,256]{1,0:T(8,128)(2,1)S(1)}, bf16[256,256]{1,0:T(8,128)(2,1)S(1)}, u32[]{:S(2)}, u32[]{:S(2)}) collective-permute-start(bf16[256,256]{1,0:T(8,128)(2,1)S(1)} %add_convert_fusion.1.args_0_), channel_id=1, source_target_pairs={{0,8},{4,12},{8,0},{12,4},{1,9},{5,13},{9,1},{13,5},{2,10},{6,14},... | collective-permute-start | bytes 393224 | tf_op jit(solution)/shard_map/ppermute | solution.py:365
  86.8 6.0 %collective-permute-start.27 = (bf16[256,256]{1,0:T(8,128)(2,1)S(1)}, bf16[256,256]{1,0:T(8,128)(2,1)S(1)}, u32[]{:S(2)}, u32[]{:S(2)}) collective-permute-start(bf16[256,256]{1,0:T(8,128)(2,1)S(1)} %add_convert_fusion.1.args_0_), channel_id=1, source_target_pairs={{0,4},{4,0},{8,12},{12,8},{1,5},{5,1},{9,13},{13,9},{2,6},{6,2},{1... | collective-permute-start | bytes 393224 | tf_op jit(solution)/shard_map/ppermute | solution.py:365
  92.8 1.4 %collective-permute-done.28.args_2_ = bf16[256,256]{1,0:T(8,128)(2,1)S(1)} collective-permute-done((bf16[256,256]{1,0:T(8,128)(2,1)S(1)}, bf16[256,256]{1,0:T(8,128)(2,1)S(1)}, u32[]{:S(2)}, u32[]{:S(2)}) %collective-permute-start.28) | collective-permute-done | bytes 131104 | tf_op jit(solution)/shard_map/ppermute | solution.py:365
  94.2 1.5 %collective-permute-done.27.args_1_ = bf16[256,256]{1,0:T(8,128)(2,1)S(1)} collective-permute-done((bf16[256,256]{1,0:T(8,128)(2,1)S(1)}, bf16[256,256]{1,0:T(8,128)(2,1)S(1)}, u32[]{:S(2)}, u32[]{:S(2)}) %collective-permute-start.27) | collective-permute-done | bytes 131104 | tf_op jit(solution)/shard_map/ppermute | solution.py:365
  97.6 1.0 %place.1 = bf16[2048,256]{1,0:T(8,128)(2,1)} custom-call(bf16[256,256]{1,0:T(8,128)(2,1)S(1)} %add_convert_fusion.1.args_0_, bf16[256,256]{1,0:T(8,128)(2,1)S(1)} %collective-permute-done.27.args_1_, bf16[256,256]{1,0:T(8,128)(2,1)S(1)} %collective-permute-done.28.args_2_, bf16[256,256]{1,0:T(8,128)(2,1)S(1)} %collective-permute-done.29.args_3_, ...), custom_call_target="tpu_custom_call" | custom-call | tf_op jit(solution)/shard_map/place/pallas_call | solution.py:472
  (64 shorter events, 21.5 us)
Async XLA Ops:
  10.8 5.5 %collective-permute-start.2 = (f32[8,1,512]{2,1,0:T(1,128)S(1)}, f32[8,1,512]{2,1,0:T(1,128)S(1)}, u32[]{:S(2)}, u32[]{:S(2)}) collective-permute-start(f32[8,1,512]{2,1,0:T(1,128)S(1)} %get-tuple-element.26.args_0_), channel_id=1, source_target_pairs={{0,3},{1,2},{2,1},{3,0},{4,7},{5,6},{6,5},{7,4},{8,11},{9,10},{10,... | collective-permute-start | bytes 49160 | tf_op jit(solution)/shard_map/ppermute | solution.py:365
  14.9 3.7 %collective-permute-start.1 = (f32[8,1,512]{2,1,0:T(1,128)S(1)}, f32[8,1,512]{2,1,0:T(1,128)S(1)}, u32[]{:S(2)}, u32[]{:S(2)}) collective-permute-start(f32[8,1,512]{2,1,0:T(1,128)S(1)} %get-tuple-element.26.args_0_), channel_id=1, source_target_pairs={{0,2},{1,3},{2,0},{3,1},{4,6},{5,7},{6,4},{7,5},{8,10},{9,11},{10,... | collective-permute-start | bytes 49160 | tf_op jit(solution)/shard_map/ppermute | solution.py:365
  15.5 3.1 %collective-permute-start = (f32[8,1,512]{2,1,0:T(1,128)S(1)}, f32[8,1,512]{2,1,0:T(1,128)S(1)}, u32[]{:S(2)}, u32[]{:S(2)}) collective-permute-start(f32[8,1,512]{2,1,0:T(1,128)S(1)} %get-tuple-element.26.args_0_), channel_id=1, source_target_pairs={{0,1},{1,0},{2,3},{3,2},{4,5},{5,4},{6,7},{7,6},{8,9},{9,8},{10,11... | collective-permute-start | bytes 49160 | tf_op jit(solution)/shard_map/ppermute | solution.py:365
  20.3 6.0 %collective-permute-start.5 = (f32[8,1,256]{2,1,0:T(1,128)S(1)}, f32[8,1,256]{2,1,0:T(1,128)S(1)}, u32[]{:S(2)}, u32[]{:S(2)}) collective-permute-start(f32[8,1,256]{2,1,0:T(1,128)S(1)} %get-tuple-element.29.args_0_), channel_id=1, source_target_pairs={{0,12},{4,8},{8,4},{12,0},{1,13},{5,9},{9,5},{13,1},{2,14},{6,10},... | collective-permute-start | bytes 24584 | tf_op jit(solution)/shard_map/ppermute | solution.py:365
  24.6 4.5 %collective-permute-start.4 = (f32[8,1,256]{2,1,0:T(1,128)S(1)}, f32[8,1,256]{2,1,0:T(1,128)S(1)}, u32[]{:S(2)}, u32[]{:S(2)}) collective-permute-start(f32[8,1,256]{2,1,0:T(1,128)S(1)} %get-tuple-element.29.args_0_), channel_id=1, source_target_pairs={{0,8},{4,12},{8,0},{12,4},{1,9},{5,13},{9,1},{13,5},{2,10},{6,14},... | collective-permute-start | bytes 24584 | tf_op jit(solution)/shard_map/ppermute | solution.py:365
  24.6 4.5 %collective-permute-start.3 = (f32[8,1,256]{2,1,0:T(1,128)S(1)}, f32[8,1,256]{2,1,0:T(1,128)S(1)}, u32[]{:S(2)}, u32[]{:S(2)}) collective-permute-start(f32[8,1,256]{2,1,0:T(1,128)S(1)} %get-tuple-element.29.args_0_), channel_id=1, source_target_pairs={{0,4},{4,0},{8,12},{12,8},{1,5},{5,1},{9,13},{13,9},{2,6},{6,2},{1... | collective-permute-start | bytes 24584 | tf_op jit(solution)/shard_map/ppermute | solution.py:365
  30.6 3.1 %collective-permute-start.8 = (f32[4,1,512]{2,1,0:T(1,128)S(1)}, f32[4,1,512]{2,1,0:T(1,128)S(1)}, u32[]{:S(2)}, u32[]{:S(2)}) collective-permute-start(f32[4,1,512]{2,1,0:T(1,128)S(1)} %get-tuple-element.31.args_0_), channel_id=1, source_target_pairs={{0,3},{1,2},{2,1},{3,0},{4,7},{5,6},{6,5},{7,4},{8,11},{9,10},{10,... | collective-permute-start | bytes 24584 | tf_op jit(solution)/shard_map/ppermute | solution.py:365
  30.6 3.7 %collective-permute-start.7 = (f32[4,1,512]{2,1,0:T(1,128)S(1)}, f32[4,1,512]{2,1,0:T(1,128)S(1)}, u32[]{:S(2)}, u32[]{:S(2)}) collective-permute-start(f32[4,1,512]{2,1,0:T(1,128)S(1)} %get-tuple-element.31.args_0_), channel_id=1, source_target_pairs={{0,2},{1,3},{2,0},{3,1},{4,6},{5,7},{6,4},{7,5},{8,10},{9,11},{10,... | collective-permute-start | bytes 24584 | tf_op jit(solution)/shard_map/ppermute | solution.py:365
  31.6 2.8 %collective-permute-start.6 = (f32[4,1,512]{2,1,0:T(1,128)S(1)}, f32[4,1,512]{2,1,0:T(1,128)S(1)}, u32[]{:S(2)}, u32[]{:S(2)}) collective-permute-start(f32[4,1,512]{2,1,0:T(1,128)S(1)} %get-tuple-element.31.args_0_), channel_id=1, source_target_pairs={{0,1},{1,0},{2,3},{3,2},{4,5},{5,4},{6,7},{7,6},{8,9},{9,8},{10,11... | collective-permute-start | bytes 24584 | tf_op jit(solution)/shard_map/ppermute | solution.py:365
  35.4 5.5 %collective-permute-start.11 = (f32[4,1,256]{2,1,0:T(1,128)S(1)}, f32[4,1,256]{2,1,0:T(1,128)S(1)}, u32[]{:S(2)}, u32[]{:S(2)}) collective-permute-start(f32[4,1,256]{2,1,0:T(1,128)S(1)} %get-tuple-element.33.args_0_), channel_id=1, source_target_pairs={{0,12},{4,8},{8,4},{12,0},{1,13},{5,9},{9,5},{13,1},{2,14},{6,10},... | collective-permute-start | bytes 12296 | tf_op jit(solution)/shard_map/ppermute | solution.py:365
  37.4 4.5 %collective-permute-start.10 = (f32[4,1,256]{2,1,0:T(1,128)S(1)}, f32[4,1,256]{2,1,0:T(1,128)S(1)}, u32[]{:S(2)}, u32[]{:S(2)}) collective-permute-start(f32[4,1,256]{2,1,0:T(1,128)S(1)} %get-tuple-element.33.args_0_), channel_id=1, source_target_pairs={{0,8},{4,12},{8,0},{12,4},{1,9},{5,13},{9,1},{13,5},{2,10},{6,14},... | collective-permute-start | bytes 12296 | tf_op jit(solution)/shard_map/ppermute | solution.py:365
  37.6 4.3 %collective-permute-start.9 = (f32[4,1,256]{2,1,0:T(1,128)S(1)}, f32[4,1,256]{2,1,0:T(1,128)S(1)}, u32[]{:S(2)}, u32[]{:S(2)}) collective-permute-start(f32[4,1,256]{2,1,0:T(1,128)S(1)} %get-tuple-element.33.args_0_), channel_id=1, source_target_pairs={{0,4},{4,0},{8,12},{12,8},{1,5},{5,1},{9,13},{13,9},{2,6},{6,2},{1... | collective-permute-start | bytes 12296 | tf_op jit(solution)/shard_map/ppermute | solution.py:365
  43.3 3.1 %collective-permute-start.14 = (f32[4,1,512]{2,1,0:T(1,128)S(1)}, f32[4,1,512]{2,1,0:T(1,128)S(1)}, u32[]{:S(2)}, u32[]{:S(2)}) collective-permute-start(f32[4,1,512]{2,1,0:T(1,128)S(1)} %get-tuple-element.34.args_0_), channel_id=1, source_target_pairs={{0,3},{1,2},{2,1},{3,0},{4,7},{5,6},{6,5},{7,4},{8,11},{9,10},{10,... | collective-permute-start | bytes 24584 | tf_op jit(solution)/shard_map/ppermute | solution.py:365
  43.4 3.8 %collective-permute-start.13 = (f32[4,1,512]{2,1,0:T(1,128)S(1)}, f32[4,1,512]{2,1,0:T(1,128)S(1)}, u32[]{:S(2)}, u32[]{:S(2)}) collective-permute-start(f32[4,1,512]{2,1,0:T(1,128)S(1)} %get-tuple-element.34.args_0_), channel_id=1, source_target_pairs={{0,2},{1,3},{2,0},{3,1},{4,6},{5,7},{6,4},{7,5},{8,10},{9,11},{10,... | collective-permute-start | bytes 24584 | tf_op jit(solution)/shard_map/ppermute | solution.py:365
  44.3 2.8 %collective-permute-start.12 = (f32[4,1,512]{2,1,0:T(1,128)S(1)}, f32[4,1,512]{2,1,0:T(1,128)S(1)}, u32[]{:S(2)}, u32[]{:S(2)}) collective-permute-start(f32[4,1,512]{2,1,0:T(1,128)S(1)} %get-tuple-element.34.args_0_), channel_id=1, source_target_pairs={{0,1},{1,0},{2,3},{3,2},{4,5},{5,4},{6,7},{7,6},{8,9},{9,8},{10,11... | collective-permute-start | bytes 24584 | tf_op jit(solution)/shard_map/ppermute | solution.py:365
  48.2 5.5 %collective-permute-start.17 = (f32[4,1,256]{2,1,0:T(1,128)S(1)}, f32[4,1,256]{2,1,0:T(1,128)S(1)}, u32[]{:S(2)}, u32[]{:S(2)}) collective-permute-start(f32[4,1,256]{2,1,0:T(1,128)S(1)} %get-tuple-element.36.args_0_), channel_id=1, source_target_pairs={{0,12},{4,8},{8,4},{12,0},{1,13},{5,9},{9,5},{13,1},{2,14},{6,10},... | collective-permute-start | bytes 12296 | tf_op jit(solution)/shard_map/ppermute | solution.py:365
  50.8 4.5 %collective-permute-start.16 = (f32[4,1,256]{2,1,0:T(1,128)S(1)}, f32[4,1,256]{2,1,0:T(1,128)S(1)}, u32[]{:S(2)}, u32[]{:S(2)}) collective-permute-start(f32[4,1,256]{2,1,0:T(1,128)S(1)} %get-tuple-element.36.args_0_), channel_id=1, source_target_pairs={{0,8},{4,12},{8,0},{12,4},{1,9},{5,13},{9,1},{13,5},{2,10},{6,14},... | collective-permute-start | bytes 12296 | tf_op jit(solution)/shard_map/ppermute | solution.py:365
  51.7 3.6 %collective-permute-start.15 = (f32[4,1,256]{2,1,0:T(1,128)S(1)}, f32[4,1,256]{2,1,0:T(1,128)S(1)}, u32[]{:S(2)}, u32[]{:S(2)}) collective-permute-start(f32[4,1,256]{2,1,0:T(1,128)S(1)} %get-tuple-element.36.args_0_), channel_id=1, source_target_pairs={{0,4},{4,0},{8,12},{12,8},{1,5},{5,1},{9,13},{13,9},{2,6},{6,2},{1... | collective-permute-start | bytes 12296 | tf_op jit(solution)/shard_map/ppermute | solution.py:365
  56.7 3.2 %collective-permute-start.20 = (f32[4,1,512]{2,1,0:T(1,128)S(1)}, f32[4,1,512]{2,1,0:T(1,128)S(1)}, u32[]{:S(2)}, u32[]{:S(2)}) collective-permute-start(f32[4,1,512]{2,1,0:T(1,128)S(1)} %get-tuple-element.37.args_0_), channel_id=1, source_target_pairs={{0,3},{1,2},{2,1},{3,0},{4,7},{5,6},{6,5},{7,4},{8,11},{9,10},{10,... | collective-permute-start | bytes 24584 | tf_op jit(solution)/shard_map/ppermute | solution.py:365
  56.8 3.7 %collective-permute-start.19 = (f32[4,1,512]{2,1,0:T(1,128)S(1)}, f32[4,1,512]{2,1,0:T(1,128)S(1)}, u32[]{:S(2)}, u32[]{:S(2)}) collective-permute-start(f32[4,1,512]{2,1,0:T(1,128)S(1)} %get-tuple-element.37.args_0_), channel_id=1, source_target_pairs={{0,2},{1,3},{2,0},{3,1},{4,6},{5,7},{6,4},{7,5},{8,10},{9,11},{10,... | collective-permute-start | bytes 24584 | tf_op jit(solution)/shard_map/ppermute | solution.py:365
  58.2 2.3 %collective-permute-start.18 = (f32[4,1,512]{2,1,0:T(1,128)S(1)}, f32[4,1,512]{2,1,0:T(1,128)S(1)}, u32[]{:S(2)}, u32[]{:S(2)}) collective-permute-start(f32[4,1,512]{2,1,0:T(1,128)S(1)} %get-tuple-element.37.args_0_), channel_id=1, source_target_pairs={{0,1},{1,0},{2,3},{3,2},{4,5},{5,4},{6,7},{7,6},{8,9},{9,8},{10,11... | collective-permute-start | bytes 24584 | tf_op jit(solution)/shard_map/ppermute | solution.py:365
  64.4 7.4 %collective-permute-start.24 = (bf16[256,256]{1,0:T(8,128)(2,1)S(1)}, bf16[256,256]{1,0:T(8,128)(2,1)S(1)}, u32[]{:S(2)}, u32[]{:S(2)}) collective-permute-start(bf16[256,256]{1,0:T(8,128)(2,1)S(1)} %get-tuple-element.47), channel_id=1, source_target_pairs={{0,4},{4,0},{8,12},{12,8},{1,5},{5,1},{9,13},{13,9},{2,6},{6,2},{1... | collective-permute-start | bytes 393224 | tf_op jit(solution)/shard_map/ppermute | solution.py:365
  67.3 12.5 %collective-permute-start.25 = (bf16[256,256]{1,0:T(8,128)(2,1)S(1)}, bf16[256,256]{1,0:T(8,128)(2,1)S(1)}, u32[]{:S(2)}, u32[]{:S(2)}) collective-permute-start(bf16[256,256]{1,0:T(8,128)(2,1)S(1)} %get-tuple-element.48), channel_id=1, source_target_pairs={{0,8},{4,12},{8,0},{12,4},{1,9},{5,13},{9,1},{13,5},{2,10},{6,14},... | collective-permute-start | bytes 393224 | tf_op jit(solution)/shard_map/ppermute | solution.py:365
  68.4 11.4 %collective-permute-start.26 = (bf16[256,256]{1,0:T(8,128)(2,1)S(1)}, bf16[256,256]{1,0:T(8,128)(2,1)S(1)}, u32[]{:S(2)}, u32[]{:S(2)}) collective-permute-start(bf16[256,256]{1,0:T(8,128)(2,1)S(1)} %get-tuple-element.49), channel_id=1, source_target_pairs={{0,12},{4,8},{8,4},{12,0},{1,13},{5,9},{9,5},{13,1},{2,14},{6,10},... | collective-permute-start | bytes 393224 | tf_op jit(solution)/shard_map/ppermute | solution.py:365
  79.9 6.9 %collective-permute-start.29 = (bf16[256,256]{1,0:T(8,128)(2,1)S(1)}, bf16[256,256]{1,0:T(8,128)(2,1)S(1)}, u32[]{:S(2)}, u32[]{:S(2)}) collective-permute-start(bf16[256,256]{1,0:T(8,128)(2,1)S(1)} %add_convert_fusion.1.args_0_), channel_id=1, source_target_pairs={{0,12},{4,8},{8,4},{12,0},{1,13},{5,9},{9,5},{13,1},{2,14},{6,10},... | collective-permute-start | bytes 393224 | tf_op jit(solution)/shard_map/ppermute | solution.py:365
  81.0 14.7 %collective-permute-start.21 = (bf16[512,256]{1,0:T(8,128)(2,1)S(1)}, bf16[512,256]{1,0:T(8,128)(2,1)S(1)}, u32[]{:S(2)}, u32[]{:S(2)}) collective-permute-start(bf16[512,256]{1,0:T(8,128)(2,1)S(1)} %get-tuple-element.43), channel_id=1, source_target_pairs={{0,1},{1,0},{2,3},{3,2},{4,5},{5,4},{6,7},{7,6},{8,9},{9,8},{10,11... | collective-permute-start | bytes 786440 | tf_op jit(solution)/shard_map/ppermute | solution.py:365
  81.0 15.2 %collective-permute-start.22 = (bf16[512,256]{1,0:T(8,128)(2,1)S(1)}, bf16[512,256]{1,0:T(8,128)(2,1)S(1)}, u32[]{:S(2)}, u32[]{:S(2)}) collective-permute-start(bf16[512,256]{1,0:T(8,128)(2,1)S(1)} %get-tuple-element.44), channel_id=1, source_target_pairs={{0,2},{1,3},{2,0},{3,1},{4,6},{5,7},{6,4},{7,5},{8,10},{9,11},{10,... | collective-permute-start | bytes 786440 | tf_op jit(solution)/shard_map/ppermute | solution.py:365
  83.8 12.5 %collective-permute-start.23 = (bf16[512,256]{1,0:T(8,128)(2,1)S(1)}, bf16[512,256]{1,0:T(8,128)(2,1)S(1)}, u32[]{:S(2)}, u32[]{:S(2)}) collective-permute-start(bf16[512,256]{1,0:T(8,128)(2,1)S(1)} %get-tuple-element.45), channel_id=1, source_target_pairs={{0,3},{1,2},{2,1},{3,0},{4,7},{5,6},{6,5},{7,4},{8,11},{9,10},{10,... | collective-permute-start | bytes 786440 | tf_op jit(solution)/shard_map/ppermute | solution.py:365
  83.9 10.2 %collective-permute-start.28 = (bf16[256,256]{1,0:T(8,128)(2,1)S(1)}, bf16[256,256]{1,0:T(8,128)(2,1)S(1)}, u32[]{:S(2)}, u32[]{:S(2)}) collective-permute-start(bf16[256,256]{1,0:T(8,128)(2,1)S(1)} %add_convert_fusion.1.args_0_), channel_id=1, source_target_pairs={{0,8},{4,12},{8,0},{12,4},{1,9},{5,13},{9,1},{13,5},{2,10},{6,14},... | collective-permute-start | bytes 393224 | tf_op jit(solution)/shard_map/ppermute | solution.py:365
  86.8 8.9 %collective-permute-start.27 = (bf16[256,256]{1,0:T(8,128)(2,1)S(1)}, bf16[256,256]{1,0:T(8,128)(2,1)S(1)}, u32[]{:S(2)}, u32[]{:S(2)}) collective-permute-start(bf16[256,256]{1,0:T(8,128)(2,1)S(1)} %add_convert_fusion.1.args_0_), channel_id=1, source_target_pairs={{0,4},{4,0},{8,12},{12,8},{1,5},{5,1},{9,13},{13,9},{2,6},{6,2},{1... | collective-permute-start | bytes 393224 | tf_op jit(solution)/shard_map/ppermute | solution.py:365
  94.2 3.0 %collective-permute-start.30 = (bf16[256,256]{1,0:T(8,128)(2,1)S(1)}, bf16[256,256]{1,0:T(8,128)(2,1)S(1)}, u32[]{:S(2)}, u32[]{:S(2)}) collective-permute-start(bf16[256,256]{1,0:T(8,128)(2,1)S(1)} %add_convert_fusion.1.args_0_), channel_id=1, source_target_pairs={{0,1},{1,0},{2,3},{3,2},{4,5},{5,4},{6,7},{7,6},{8,9},{9,8},{10,11... | collective-permute-start | bytes 393224 | tf_op jit(solution)/shard_map/ppermute | solution.py:365
  95.7 1.5 %collective-permute-start.32 = (bf16[256,256]{1,0:T(8,128)(2,1)S(1)}, bf16[256,256]{1,0:T(8,128)(2,1)S(1)}, u32[]{:S(2)}, u32[]{:S(2)}) collective-permute-start(bf16[256,256]{1,0:T(8,128)(2,1)S(1)} %collective-permute-done.28.args_2_), channel_id=1, source_target_pairs={{0,1},{1,0},{2,3},{3,2},{4,5},{5,4},{6,7},{7,6},{8,9},{9,8},{10,11... | collective-permute-start | bytes 393224 | tf_op jit(solution)/shard_map/ppermute | solution.py:365
  (10 other events, 46.1 us)

commit v2 on v1

v2 whole, which is shorter than its diff:
```python
import functools
import math

import jax
import jax.numpy as jnp
from jax import lax
from jax.experimental import pallas as pl
from jax.experimental.pallas import tpu as pltpu
from jax.sharding import PartitionSpec as P

TILE = 512
HALF = 256
BLOCK = 4
LANES = 128
ROWS = 64
LIMIT = 24 * 1024 * 1024
LOWEST = -1e30
F32 = jnp.float32
NT_DIMS = (((1,), (1,)), ((), ()))
NN_DIMS = (((1,), (0,)), ((), ()))
TN_DIMS = (((0,), (0,)), ((), ()))


def kept_targets(meta, s):
    first_cut, second_cut, straight = meta
    is_low = (s < first_cut).astype(jnp.int32) == straight
    return jnp.where(is_low, 0, second_cut), jnp.where(is_low, second_cut, BLOCK)


def kept_sources(meta, t):
    first_cut, second_cut, straight = meta
    is_low = (t < second_cut).astype(jnp.int32) == straight
    return jnp.where(is_low, 0, first_cut), jnp.where(is_low, first_cut, BLOCK)


def tile_lanes(t):
    return pl.ds(pl.multiple_of(t * HALF, HALF), HALF)


def read_meta(meta_ref):
    return meta_ref[0, 0], meta_ref[0, 1], meta_ref[0, 2]


def to_column(row):
    return jnp.broadcast_to(row, (LANES, row.shape[1])).T


def lane_sums(values):
    return jnp.sum(values.T, axis=0, keepdims=True)


def total(refs, index):
    value = refs[0][index]
    for ref in refs[1:]:
        value = value + ref[index]
    return value


def for_widths(low, high, body):
    for n in range(1, BLOCK):
        pl.when(high - low == n)(functools.partial(body, n))


def weighted_rows(e_ref, meta, vector_ref, out_ref):
    def one(s, carry):
        low, high = kept_targets(meta, s)

        def body(n):
            vectors = [vector_ref[low + i] for i in range(n)]
            for at in range(0, TILE, LANES):
                acc = None
                for i in range(n):
                    e = e_ref[s, at : at + LANES, tile_lanes(low + i)]
                    term = e[:, :LANES] * vectors[i][:, :LANES] + e[:, LANES:] * vectors[i][:, LANES:]
                    acc = term if acc is None else acc + term
                out_ref[s, :, at : at + LANES] = lane_sums(acc)

        for_widths(low, high, body)
        return carry

    lax.fori_loop(0, BLOCK, one, 0)


def eight_rows(values, reduce):
    return reduce(values.reshape(-1, 8, LANES), axis=0)


def weighted_columns(e_ref, meta, column_ref, scale_ref, out_ref):
    def one(t, carry):
        low, high = kept_sources(meta, t)

        def step(s, acc):
            left, right = acc
            for at in range(0, TILE, ROWS):
                e = e_ref[s, at : at + ROWS, tile_lanes(t)]
                u = column_ref[s, at : at + ROWS, :]
                left = left + eight_rows(e[:, :LANES] * u, jnp.sum)
                right = right + eight_rows(e[:, LANES:] * u, jnp.sum)
            return left, right

        zero = jnp.zeros((8, LANES), F32)
        left, right = lax.fori_loop(low, high, step, (zero, zero))
        scale = scale_ref[t]
        out_ref[t, :, :LANES] = scale[:, :LANES] * jnp.sum(left, axis=0, keepdims=True)
        out_ref[t, :, LANES:] = scale[:, LANES:] * jnp.sum(right, axis=0, keepdims=True)
        return carry

    lax.fori_loop(0, BLOCK, one, 0)


def first_source_kernel(
    x_hbm,
    y_hbm,
    warm_hbm,
    sb_hbm,
    tb_hbm,
    kp_hbm,
    score_ref,
    out_ref,
    meta_ref,
    x_ref,
    y_ref,
    warm_ref,
    sb_ref,
    tb_ref,
    kp_ref,
    x_sems,
    y_sems,
    warm_sems,
    bound_sems,
):
    row_pos = lax.axis_index("row")
    col_pos = lax.axis_index("col")
    rep_pos = lax.axis_index("rep")
    bounds = [
        pltpu.make_async_copy(source, target, bound_sems.at[i])
        for i, (source, target) in enumerate(
            ((sb_hbm, sb_ref), (tb_hbm, tb_ref), (kp_hbm, kp_ref))
        )
    ]
    x_copies, y_copies, warm_copies = [], [], []
    for t in range(BLOCK):
        begin = pl.multiple_of(t * TILE + rep_pos * HALF, HALF)
        y_copies.append(
            pltpu.make_async_copy(
                y_hbm.at[pl.ds(begin, HALF)], y_ref.at[pl.ds(t * HALF, HALF)], y_sems.at[t]
            )
        )
        warm_copies.append(
            pltpu.make_async_copy(warm_hbm.at[2 * t + rep_pos], warm_ref.at[t], warm_sems.at[t])
        )
        x_copies.append(
            pltpu.make_async_copy(
                x_hbm.at[pl.ds(t * TILE, TILE)], x_ref.at[pl.ds(t * TILE, TILE)], x_sems.at[t]
            )
        )
    for copy in bounds + y_copies + x_copies[:1] + warm_copies + x_copies[1:]:
        copy.start()
    for copy in bounds:
        copy.wait()
    first_cut = sb_ref[2 * row_pos + 1] - BLOCK * row_pos
    second_cut = tb_ref[2 * col_pos + 1] - BLOCK * col_pos

    def look(i, found):
        here = (kp_ref[0, i] == 2 * row_pos) & (kp_ref[1, i] == 2 * col_pos)
        return found | here.astype(jnp.int32)

    straight = lax.fori_loop(0, kp_ref.shape[1], look, jnp.int32(0))
    lanes = lax.broadcasted_iota(jnp.int32, meta_ref.shape, 1)
    meta_ref[...] = jnp.where(lanes == 0, first_cut, jnp.where(lanes == 1, second_cut, straight))
    meta = (first_cut, second_cut, straight)
    inv_root = x_ref.shape[1] ** (-0.5)
    for copy in y_copies:
        copy.wait()
    for s in range(BLOCK):
        x_copies[s].wait()
        score_ref[s] = inv_root * lax.dot_general(
            x_ref[s * TILE : (s + 1) * TILE, :],
            y_ref[...],
            NT_DIMS,
            preferred_element_type=F32,
        )
    for copy in warm_copies:
        copy.wait()

    def one(s, carry):
        low, high = kept_targets(meta, s)

        def body(n):
            warm = [warm_ref[low + i] for i in range(n)]
            for at in range(0, TILE, LANES):
                largest = None
                for i in range(n):
                    e = score_ref[s, at : at + LANES, tile_lanes(low + i)]
                    term = jnp.maximum(
                        e[:, :LANES] + warm[i][:, :LANES], e[:, LANES:] + warm[i][:, LANES:]
                    )
                    largest = term if largest is None else jnp.maximum(largest, term)
                largest = jnp.max(largest, axis=1, keepdims=True)
                largest = jnp.broadcast_to(largest, (LANES, LANES))
                acc = None
                for i in range(n):
                    e = score_ref[s, at : at + LANES, tile_lanes(low + i)]
                    term = jnp.exp(e[:, :LANES] + warm[i][:, :LANES] - largest) + jnp.exp(
                        e[:, LANES:] + warm[i][:, LANES:] - largest
                    )
                    acc = term if acc is None else acc + term
                out_ref[s, :, at : at + LANES] = largest.T[:1]
                out_ref[BLOCK + s, :, at : at + LANES] = lane_sums(acc)

        for_widths(low, high, body)
        return carry

    lax.fori_loop(0, BLOCK, one, 0)


def combine(refs, at, offset):
    largest = refs[0][at]
    for ref in refs[1:]:
        largest = jnp.maximum(largest, ref[at])
    sums = refs[0][offset + at] * jnp.exp(refs[0][at] - largest)
    for ref in refs[1:]:
        sums = sums + ref[offset + at] * jnp.exp(ref[at] - largest)
    return -(largest + jnp.log(sums))


def first_target_kernel(count, *args):
    parts = args[:count]
    score_ref, meta_ref, e_ref, out_ref, column_ref = args[count:]
    meta = read_meta(meta_ref)
    for s in range(BLOCK):
        column_ref[s] = to_column(combine(parts, s, BLOCK))

    def one(t, carry):
        low, high = kept_sources(meta, t)

        def peak(s, acc):
            left, right = acc
            for at in range(0, TILE, ROWS):
                e = score_ref[s, at : at + ROWS, tile_lanes(t)]
                u = column_ref[s, at : at + ROWS, :]
                left = jnp.maximum(left, eight_rows(e[:, :LANES] + u, jnp.max))
                right = jnp.maximum(right, eight_rows(e[:, LANES:] + u, jnp.max))
            return left, right

        lowest = jnp.full((8, LANES), LOWEST, F32)
        left, right = lax.fori_loop(low, high, peak, (lowest, lowest))
        left = jnp.max(left, axis=0, keepdims=True)
        right = jnp.max(right, axis=0, keepdims=True)
        out_ref[t, :, :LANES] = left
        out_ref[t, :, LANES:] = right

        def step(s, acc):
            left_sum, right_sum = acc
            for at in range(0, TILE, ROWS):
                e = score_ref[s, at : at + ROWS, tile_lanes(t)]
                u = column_ref[s, at : at + ROWS, :]
                e_left = jnp.exp(e[:, :LANES] + u - left)
                e_right = jnp.exp(e[:, LANES:] + u - right)
                e_ref[s, at : at + ROWS, tile_lanes(t)] = jnp.concatenate([e_left, e_right], axis=1)
                left_sum = left_sum + eight_rows(e_left, jnp.sum)
                right_sum = right_sum + eight_rows(e_right, jnp.sum)
            return left_sum, right_sum

        zero = jnp.zeros((8, LANES), F32)
        left_sum, right_sum = lax.fori_loop(low, high, step, (zero, zero))
        out_ref[BLOCK + t, :, :LANES] = jnp.sum(left_sum, axis=0, keepdims=True)
        out_ref[BLOCK + t, :, LANES:] = jnp.sum(right_sum, axis=0, keepdims=True)
        return carry

    lax.fori_loop(0, BLOCK, one, 0)


def second_source_kernel(count, *args):
    parts = args[:count]
    warm_ref, e_ref, meta_ref, out_ref, q_ref, wq_ref = args[count:]
    for t in range(BLOCK):
        potential = combine(parts, t, BLOCK)
        q = jnp.exp(parts[0][t] + potential)
        q_ref[t] = q
        wq_ref[t] = q * jnp.exp(warm_ref[t] - potential)
    weighted_rows(e_ref, read_meta(meta_ref), q_ref, out_ref)


def second_target_kernel(count, *args):
    parts = args[:count]
    e_ref, meta_ref, q_ref, out_ref, a_ref, column_ref = args[count:]
    for s in range(BLOCK):
        a = 1.0 / total(parts, s)
        a_ref[s] = a
        column_ref[s] = to_column(a)
    weighted_columns(e_ref, read_meta(meta_ref), column_ref, q_ref, out_ref)


def late_kernel(count, *args):
    parts = args[:count]
    e_ref, meta_ref, q_ref, weight_ref, out_ref, p_ref = args[count:]
    rep_pos = lax.axis_index("rep")
    for t in range(BLOCK):
        p_ref[t] = weight_ref[2 * t + rep_pos] * q_ref[t] / total(parts, t)
    weighted_rows(e_ref, read_meta(meta_ref), p_ref, out_ref)


def mid_kernel(count, *args):
    parts = args[:count]
    e_ref, meta_ref, q_ref, a_ref, weight_ref, out_ref, column_ref = args[count:]
    for s in range(BLOCK):
        a = a_ref[s]
        column_ref[s] = to_column(a * (weight_ref[s] - a * total(parts, s)))
    weighted_columns(e_ref, read_meta(meta_ref), column_ref, q_ref, out_ref)


def early_kernel(count, *args):
    parts = args[:count]
    e_ref, meta_ref, q_ref, out_ref, h_ref = args[count:]
    for t in range(BLOCK):
        h_ref[t] = -q_ref[t] * total(parts, t)
    weighted_rows(e_ref, read_meta(meta_ref), h_ref, out_ref)


def target_gradient_kernel(part, count, *args):
    if count:
        parts = args[:count]
        x_ref, e_ref, meta_ref, a_ref, b_ref, p_ref, q_ref, h_ref, wq_ref = args[count : count + 9]
        bar_ref, early_ref, *out_refs = args[count + 9 :]
        for s in range(BLOCK):
            early_ref[s] = to_column(-total(parts, s))
    else:
        x_ref, e_ref, meta_ref, a_ref, b_ref, p_ref, q_ref, h_ref, wq_ref = args[:9]
        early_ref, _, bar_ref, *out_refs = args[9:]
    row_pos = lax.axis_index("row")
    per_tile = len(out_refs)
    t = (row_pos // per_tile) ^ part
    low, high = kept_sources(read_meta(meta_ref), t)
    p, q, h, wq = p_ref[t], q_ref[t], h_ref[t], wq_ref[t]
    for s in range(BLOCK):

        @pl.when((s >= low) & (s < high))
        def _():
            for at in range(0, TILE, ROWS):
                e = e_ref[s, at : at + ROWS, tile_lanes(t)]
                a = a_ref[s, at : at + ROWS, :]
                b = b_ref[s, at : at + ROWS, :]
                early = early_ref[s, at : at + ROWS, :]
                sides = []
                for side in (slice(0, LANES), slice(LANES, HALF)):
                    factor = a * p[:, side] + b * q[:, side] + (h[:, side] + early * wq[:, side])
                    sides.append((e[:, side] * factor).astype(jnp.bfloat16))
                bar_ref[s, at : at + ROWS, tile_lanes(t)] = jnp.concatenate(sides, axis=1)

        @pl.when((s < low) | (s >= high))
        def _():
            bar_ref[s, :, tile_lanes(t)] = jnp.zeros((TILE, HALF), jnp.bfloat16)

    bar = bar_ref[:, :, tile_lanes(t)].reshape(BLOCK * TILE, HALF)
    inv_root = x_ref.shape[1] ** (-0.5)
    result = -inv_root * lax.dot_general(bar, x_ref[...], TN_DIMS, preferred_element_type=F32)
    if per_tile == 1:
        out_refs[0][...] = result.astype(out_refs[0].dtype)
        return
    piece = HALF // per_tile
    for i, ref in enumerate(out_refs):
        at = (row_pos % per_tile) ^ i
        for j in range(per_tile):

            @pl.when(at == j)
            def _():
                ref[...] = result[j * piece : (j + 1) * piece, :].astype(ref.dtype)


def source_gradient_kernel(bar_ref, y_ref, near_ref, far_ref, acc_ref):
    inv_root = y_ref.shape[1] ** (-0.5)
    col_pos = lax.axis_index("col")
    rep_pos = lax.axis_index("rep")
    for s in range(BLOCK):
        acc_ref[s * TILE : (s + 1) * TILE, :] = -inv_root * lax.dot_general(
            bar_ref[s], y_ref[...], NN_DIMS, preferred_element_type=F32
        )
    piece = near_ref.shape[1]
    for d in range(near_ref.shape[0]):
        at = 2 * (col_pos ^ d)
        for ref, rep in ((near_ref, rep_pos), (far_ref, 1 - rep_pos)):
            begin = pl.multiple_of((at + rep) * piece, piece)
            ref[d] = acc_ref[pl.ds(begin, piece), :].astype(ref.dtype)


def merge_kernel(near_ref, far_ref, *out_refs):
    for d, ref in enumerate(out_refs):
        ref[...] = (near_ref[d] + far_ref[d].astype(F32)).astype(ref.dtype)


def finish_kernel(rows, *args):
    own, other, args = args[:rows], args[rows : 2 * rows], args[2 * rows :]
    terms, (source_out, target_out, sum_ref, sems) = args[:-4], args[-4:]
    rep_pos = lax.axis_index("rep")
    row_pos = lax.axis_index("row")
    piece = own[0].shape[0]
    per_tile = HALF // piece
    copies = []
    for refs, rep in ((own, rep_pos), (other, 1 - rep_pos)):
        for k, ref in enumerate(refs):
            at = row_pos ^ k
            begin = (at // per_tile) * TILE + rep * HALF + (at % per_tile) * piece
            copies.append(
                pltpu.make_async_copy(
                    ref,
                    target_out.at[pl.ds(pl.multiple_of(begin, piece), piece)],
                    sems.at[len(copies)],
                )
            )
    for copy in copies:
        copy.start()
    value = terms[0][...]
    for term in terms[1:]:
        value = value + term[...].astype(F32)
    sum_ref[...] = value.astype(sum_ref.dtype)
    copies.append(pltpu.make_async_copy(sum_ref, source_out, sems.at[len(copies)]))
    copies[-1].start()
    for copy in copies:
        copy.wait()


def call(kernel, name, outs, scratch, args, spaces=None, aliases=None, cost=None):
    spaces = spaces or [pltpu.VMEM] * len(args)
    args = [
        pltpu.with_memory_space_constraint(value, space)
        for value, space in zip(args, spaces)
    ]
    return pl.pallas_call(
        kernel,
        name=name,
        out_shape=[pltpu.VMEM(shape, dtype) for shape, dtype in outs],
        in_specs=[pl.BlockSpec(memory_space=space) for space in spaces],
        out_specs=[pl.BlockSpec(memory_space=pltpu.VMEM) for _ in outs],
        scratch_shapes=scratch,
        input_output_aliases=aliases or {},
        cost_estimate=cost,
        compiler_params=pltpu.CompilerParams(vmem_limit_bytes=LIMIT),
    )(*args)


def shards(
    sizes,
    source_emb,
    target_emb,
    warm_start,
    source_weight,
    target_weight,
    source_bounds,
    target_bounds,
    kept_pairs,
):
    width = source_emb.shape[1]

    def swap(value, axes, k):
        count = math.prod(sizes[axis] for axis in axes)
        return lax.ppermute(value, axes, [(i, i ^ k) for i in range(count)])

    def spread(value, axes):
        count = math.prod(sizes[axis] for axis in axes)
        return [value] + [swap(value, axes, k) for k in range(1, count)]

    bf16 = jnp.bfloat16
    over_source = ("col", "rep")
    over_target = ("row",)
    target_weight = target_weight.reshape(2 * BLOCK, 1, HALF)
    source_weight = source_weight.reshape(BLOCK, 1, TILE)
    source_vector = ((BLOCK, 1, TILE), F32)
    target_vector = ((BLOCK, 1, HALF), F32)
    matrix = (BLOCK, TILE, BLOCK * HALF)
    columns = (BLOCK, TILE, LANES)
    hbm = pltpu.HBM

    score, packed, meta, x, y, warm = call(
        first_source_kernel,
        "first_source",
        [
            (matrix, F32),
            ((2 * BLOCK, 1, TILE), F32),
            ((8, LANES), jnp.int32),
            ((BLOCK * TILE, width), bf16),
            ((BLOCK * HALF, width), bf16),
            target_vector,
        ],
        [
            pltpu.SMEM(source_bounds.shape, jnp.int32),
            pltpu.SMEM(target_bounds.shape, jnp.int32),
            pltpu.SMEM(kept_pairs.shape[::-1], jnp.int32),
        ]
        + [pltpu.SemaphoreType.DMA((BLOCK,))] * 4,
        [
            source_emb,
            target_emb,
            warm_start.reshape(2 * BLOCK, 1, HALF),
            source_bounds,
            target_bounds,
            kept_pairs.T,
        ],
        [hbm] * 6,
    )
    parts = spread(packed, over_source)
    n_source = len(parts)
    e, packed = call(
        functools.partial(first_target_kernel, n_source),
        "first_target",
        [(matrix, F32), ((2 * BLOCK, 1, HALF), F32)],
        [pltpu.VMEM(columns, F32)],
        [*parts, score, meta],
    )
    parts = spread(packed, over_target)
    n_target = len(parts)
    sums, q, wq = call(
        functools.partial(second_source_kernel, n_target),
        "second_source",
        [source_vector, target_vector, target_vector],
        [],
        [*parts, warm, e, meta],
    )
    parts = spread(sums, over_source)
    sums, a, a_column = call(
        functools.partial(second_target_kernel, n_source),
        "second_target",
        [target_vector, source_vector, (columns, F32)],
        [],
        [*parts, e, meta, q],
    )
    parts = spread(sums, over_target)
    sums, p = call(
        functools.partial(late_kernel, n_target),
        "late",
        [source_vector, target_vector],
        [],
        [*parts, e, meta, q, target_weight],
    )
    parts = spread(sums, over_source)
    sums, b_column = call(
        functools.partial(mid_kernel, n_source),
        "mid",
        [target_vector, (columns, F32)],
        [],
        [*parts, e, meta, q, a, source_weight],
    )
    parts = spread(sums, over_target)
    sums, h = call(
        functools.partial(early_kernel, n_target),
        "early",
        [source_vector, target_vector],
        [],
        [*parts, e, meta, q],
    )
    parts = spread(sums, over_source)

    rows = sizes["row"]
    per_tile = rows // BLOCK
    piece = HALF // per_tile
    shared = [x, e, meta, a_column, b_column, p, q, h, wq]
    pieces = [None] * rows
    arrived = [None] * rows
    bar = early = None
    for part in (2, 1, 3, 0):
        outs = [((piece, width), bf16 if part or i else F32) for i in range(per_tile)]
        if bar is None:
            bar, early, *results = call(
                functools.partial(target_gradient_kernel, part, n_source),
                f"target_gradient_{part}",
                [(matrix, bf16), (columns, F32)] + outs,
                [],
                [*parts, *shared],
            )
        else:
            bar, *results = call(
                functools.partial(target_gradient_kernel, part, 0),
                f"target_gradient_{part}",
                [(matrix, bf16)] + outs,
                [],
                [*shared, early, bar],
                aliases={len(shared) + 1: 0},
            )
        for i, value in enumerate(results):
            k = part * per_tile + i
            pieces[k] = value
            arrived[k] = swap(value, over_target, k) if k else value
    source_piece = BLOCK * TILE // n_source
    columns_of_chips = sizes["col"]
    halves = (columns_of_chips, source_piece, width)
    near, far = call(
        source_gradient_kernel,
        "source_gradient",
        [(halves, F32), (halves, bf16)],
        [pltpu.VMEM((BLOCK * TILE, width), F32)],
        [bar, y],
    )
    def added(values):
        value = values[0].astype(F32)
        for other in values[1:]:
            value = value + other.astype(F32)
        return value.astype(bf16)

    arrived, far = lax.optimization_barrier((arrived, far))
    target_rows = added(arrived)
    merged = call(
        merge_kernel,
        "merge",
        [((source_piece, width), bf16 if d else F32) for d in range(columns_of_chips)],
        [],
        [near, swap(far, ("rep",), 1)],
    )
    terms = [merged[0]] + [swap(merged[d], ("col",), d) for d in range(1, columns_of_chips)]
    gathered = spread(target_rows, over_target)
    gathered = gathered + [swap(value, ("rep",), 1) for value in gathered]
    source_shape = (source_piece, width)
    return pl.pallas_call(
        functools.partial(finish_kernel, rows),
        name="finish",
        out_shape=[
            jax.ShapeDtypeStruct(source_shape, bf16),
            jax.ShapeDtypeStruct(target_emb.shape, bf16),
        ],
        in_specs=[pl.BlockSpec(memory_space=pltpu.VMEM)] * (len(gathered) + len(terms)),
        out_specs=[pl.BlockSpec(memory_space=pltpu.HBM)] * 2,
        scratch_shapes=[
            pltpu.VMEM(source_shape, bf16),
            pltpu.SemaphoreType.DMA((len(gathered) + 1,)),
        ],
        compiler_params=pltpu.CompilerParams(vmem_limit_bytes=LIMIT),
    )(*gathered, *terms)


def solution(mesh):
    return jax.shard_map(
        functools.partial(shards, dict(mesh.shape)),
        mesh=mesh,
        in_specs=(
            P(("groups", "row"), None),
            P(("groups", "col"), None),
            P(("groups", "col")),
            P(("groups", "row")),
            P(("groups", "col")),
            P("groups"),
            P("groups"),
            P("groups", None),
        ),
        out_specs=(P(("groups", "row", "col", "rep"), None), P(("groups", "col"), None)),
        check_vma=False,
    )
```

time: 98.7 us -> 84.8 us (0.86)
  starting transfers between devices: 43 us -> 32.7 us
  local copies, waits for them, and re-layouts: 5.22 us -> 0.01 us
  waiting for transfers between devices: 31 us -> 33.1 us
    ppermute x34 -> x33, starting transfers between devices: 43 us -> 32.7 us  [swap(): return lax.ppermute(value, axes, [(i, i ^ k) for i in range(count)])]
    unnamed x17 -> x4, local copies, waits for them, and re-layouts: 5.22 us -> 0.01 us
    ppermute x34 -> x33, waiting for transfers between devices: 31 us -> 33.1 us  [swap(): return lax.ppermute(value, axes, [(i, i ^ k) for i in range(count)])]
    pallas_call x8 -> x13, Pallas kernels: 16.7 us -> 16.4 us  [call(): pl.pallas_call(kernel, name=name, out_shape=[pltpu.VMEM(shape, dtype) for...]
  transfers between devices with their start and end apart: 34 -> 33, of which waited for: 21 -> 21; matrix products, arithmetic and copies ran while one was open for 1% -> 0% of each run, Pallas kernels for 0% -> 3%
where the time goes in v2:
time: 84.8 us; the launch traced here: 84.3 us
  waiting for transfers between devices  33.1 us (39%)
  starting transfers between devices  32.7 us (39%)
  Pallas kernels  17.5 us (21%)
  between operations  0.94 us (1%)
    ppermute x33, waiting for transfers between devices, swap(): return lax.ppermute(value, axes, [(i, i ^ k) for i in range(count)])  33.1 us
    ppermute x33, starting transfers between devices, swap(): return lax.ppermute(value, axes, [(i, i ^ k) for i in range(count)])  32.7 us
    pallas_call x13, Pallas kernels, call(): pl.pallas_call(kernel, name=name, out_shape=[pltpu.VMEM(shape, dtype) for...  16.4 us
  transfers between devices with their start and end apart: 33, of which 21 were waited for; matrix products, arithmetic and copies ran while one was open for 0% of the time, Pallas kernels for 3%

profile of v2, /device:TPU:0, one launch (start us, length us, event | category | flops | bytes accessed | tf_op | source)
XLA Modules:
  0.0 84.3 jit_solution(14380190606476798128)
XLA Ops:
  0.6 4.7 %first_source.1 = (f32[4,512,1024]{2,1,0:T(8,128)S(1)}, f32[8,1,512]{2,1,0:T(1,128)S(1)}, s32[8,128]{1,0:T(8,128)S(1)}, bf16[2048,256]{1,0:T(8,128)(2,1)S(1)}, b...) custom-call(bf16[2048,256]{1,0:T(8,128)(2,1)} %x_hbm.1, bf16[2048,256]{1,0:T(8,128)(2,1)} %y_hbm.1, ...), custom_call_target="tpu_custom_call" | custom-call | tf_op jit(solution)/shard_map/first_source/pallas_call | solution.py:429
  5.3 2.8 %collective-permute-start.2 = (f32[8,1,512]{2,1,0:T(1,128)S(1)}, f32[8,1,512]{2,1,0:T(1,128)S(1)}, u32[]{:S(2)}, u32[]{:S(2)}) collective-permute-start(f32[8,1,512]{2,1,0:T(1,128)S(1)} %get-tuple-element.41.args_0_), channel_id=1, source_target_pairs={{0,3},{1,2},{2,1},{3,0},{4,7},{5,6},{6,5},{7,4},{8,11},{9,10},{10,... | collective-permute-start | bytes 49160 | tf_op jit(solution)/shard_map/ppermute | solution.py:457
  9.6 2.3 %collective-permute-done.1.args_2_ = f32[8,1,512]{2,1,0:T(1,128)S(1)} collective-permute-done((f32[8,1,512]{2,1,0:T(1,128)S(1)}, f32[8,1,512]{2,1,0:T(1,128)S(1)}, u32[]{:S(2)}, u32[]{:S(2)}) %collective-permute-start.1) | collective-permute-done | bytes 16416 | tf_op jit(solution)/shard_map/ppermute | solution.py:457
  11.9 1.7 %first_target.1 = (f32[4,512,1024]{2,1,0:T(8,128)S(1)}, f32[8,1,256]{2,1,0:T(1,128)S(1)}) custom-call(f32[8,1,512]{2,1,0:T(1,128)S(1)} %get-tuple-element.41.args_0_, f32[8,1,512]{2,1,0:T(1,128)S(1)} %collective-permute-done.args_1_, f32[8,1,512]{2,1,0:T(1,128)S(1)} %collective-permute-done.1.args_2_, f32[8,1,512]{2,1,0:T(1,128)S(1)} %collective-permute-done.2.args_3_, ...), custom_call_target="tpu_custom_call" | custom-call | tf_op jit(solution)/shard_map/first_target/pallas_call | solution.py:429
  13.5 3.4 %collective-permute-start.5 = (f32[8,1,256]{2,1,0:T(1,128)S(1)}, f32[8,1,256]{2,1,0:T(1,128)S(1)}, u32[]{:S(2)}, u32[]{:S(2)}) collective-permute-start(f32[8,1,256]{2,1,0:T(1,128)S(1)} %get-tuple-element.45.args_0_), channel_id=1, source_target_pairs={{0,12},{4,8},{8,4},{12,0},{1,13},{5,9},{9,5},{13,1},{2,14},{6,10},... | collective-permute-start | bytes 24584 | tf_op jit(solution)/shard_map/ppermute | solution.py:457
  16.9 1.1 %collective-permute-start.3 = (f32[8,1,256]{2,1,0:T(1,128)S(1)}, f32[8,1,256]{2,1,0:T(1,128)S(1)}, u32[]{:S(2)}, u32[]{:S(2)}) collective-permute-start(f32[8,1,256]{2,1,0:T(1,128)S(1)} %get-tuple-element.45.args_0_), channel_id=1, source_target_pairs={{0,4},{4,0},{8,12},{12,8},{1,5},{5,1},{9,13},{13,9},{2,6},{6,2},{1... | collective-permute-start | bytes 24584 | tf_op jit(solution)/shard_map/ppermute | solution.py:457
  18.0 1.1 %collective-permute-done.5.args_3_ = f32[8,1,256]{2,1,0:T(1,128)S(1)} collective-permute-done((f32[8,1,256]{2,1,0:T(1,128)S(1)}, f32[8,1,256]{2,1,0:T(1,128)S(1)}, u32[]{:S(2)}, u32[]{:S(2)}) %collective-permute-start.5) | collective-permute-done | bytes 8224 | tf_op jit(solution)/shard_map/ppermute | solution.py:457
  19.1 2.4 %collective-permute-done.4.args_2_ = f32[8,1,256]{2,1,0:T(1,128)S(1)} collective-permute-done((f32[8,1,256]{2,1,0:T(1,128)S(1)}, f32[8,1,256]{2,1,0:T(1,128)S(1)}, u32[]{:S(2)}, u32[]{:S(2)}) %collective-permute-start.4) | collective-permute-done | bytes 8224 | tf_op jit(solution)/shard_map/ppermute | solution.py:457
  22.8 1.4 %collective-permute-start.6 = (f32[4,1,512]{2,1,0:T(1,128)S(1)}, f32[4,1,512]{2,1,0:T(1,128)S(1)}, u32[]{:S(2)}, u32[]{:S(2)}) collective-permute-start(f32[4,1,512]{2,1,0:T(1,128)S(1)} %get-tuple-element.47.args_0_), channel_id=1, source_target_pairs={{0,1},{1,0},{2,3},{3,2},{4,5},{5,4},{6,7},{7,6},{8,9},{9,8},{10,11... | collective-permute-start | bytes 24584 | tf_op jit(solution)/shard_map/ppermute | solution.py:457
  24.2 1.2 %collective-permute-done.8.args_3_ = f32[4,1,512]{2,1,0:T(1,128)S(1)} collective-permute-done((f32[4,1,512]{2,1,0:T(1,128)S(1)}, f32[4,1,512]{2,1,0:T(1,128)S(1)}, u32[]{:S(2)}, u32[]{:S(2)}) %collective-permute-start.8) | collective-permute-done | bytes 8224 | tf_op jit(solution)/shard_map/ppermute | solution.py:457
  26.9 1.5 %collective-permute-start.11 = (f32[4,1,256]{2,1,0:T(1,128)S(1)}, f32[4,1,256]{2,1,0:T(1,128)S(1)}, u32[]{:S(2)}, u32[]{:S(2)}) collective-permute-start(f32[4,1,256]{2,1,0:T(1,128)S(1)} %get-tuple-element.50.args_0_), channel_id=1, source_target_pairs={{0,12},{4,8},{8,4},{12,0},{1,13},{5,9},{9,5},{13,1},{2,14},{6,10},... | collective-permute-start | bytes 12296 | tf_op jit(solution)/shard_map/ppermute | solution.py:457
  29.1 2.3 %collective-permute-start.9 = (f32[4,1,256]{2,1,0:T(1,128)S(1)}, f32[4,1,256]{2,1,0:T(1,128)S(1)}, u32[]{:S(2)}, u32[]{:S(2)}) collective-permute-start(f32[4,1,256]{2,1,0:T(1,128)S(1)} %get-tuple-element.50.args_0_), channel_id=1, source_target_pairs={{0,4},{4,0},{8,12},{12,8},{1,5},{5,1},{9,13},{13,9},{2,6},{6,2},{1... | collective-permute-start | bytes 12296 | tf_op jit(solution)/shard_map/ppermute | solution.py:457
  35.7 1.2 %collective-permute-done.14.args_3_ = f32[4,1,512]{2,1,0:T(1,128)S(1)} collective-permute-done((f32[4,1,512]{2,1,0:T(1,128)S(1)}, f32[4,1,512]{2,1,0:T(1,128)S(1)}, u32[]{:S(2)}, u32[]{:S(2)}) %collective-permute-start.14) | collective-permute-done | bytes 8224 | tf_op jit(solution)/shard_map/ppermute | solution.py:457
  38.4 2.6 %collective-permute-start.17 = (f32[4,1,256]{2,1,0:T(1,128)S(1)}, f32[4,1,256]{2,1,0:T(1,128)S(1)}, u32[]{:S(2)}, u32[]{:S(2)}) collective-permute-start(f32[4,1,256]{2,1,0:T(1,128)S(1)} %get-tuple-element.55.args_0_), channel_id=1, source_target_pairs={{0,12},{4,8},{8,4},{12,0},{1,13},{5,9},{9,5},{13,1},{2,14},{6,10},... | collective-permute-start | bytes 12296 | tf_op jit(solution)/shard_map/ppermute | solution.py:457
  43.9 1.6 %collective-permute-done.16.args_2_ = f32[4,1,256]{2,1,0:T(1,128)S(1)} collective-permute-done((f32[4,1,256]{2,1,0:T(1,128)S(1)}, f32[4,1,256]{2,1,0:T(1,128)S(1)}, u32[]{:S(2)}, u32[]{:S(2)}) %collective-permute-start.16) | collective-permute-done | bytes 4128 | tf_op jit(solution)/shard_map/ppermute | solution.py:457
  47.1 1.2 %collective-permute-start.18 = (f32[4,1,512]{2,1,0:T(1,128)S(1)}, f32[4,1,512]{2,1,0:T(1,128)S(1)}, u32[]{:S(2)}, u32[]{:S(2)}) collective-permute-start(f32[4,1,512]{2,1,0:T(1,128)S(1)} %get-tuple-element.58.args_0_), channel_id=1, source_target_pairs={{0,1},{1,0},{2,3},{3,2},{4,5},{5,4},{6,7},{7,6},{8,9},{9,8},{10,11... | collective-permute-start | bytes 24584 | tf_op jit(solution)/shard_map/ppermute | solution.py:457
  48.3 1.2 %collective-permute-done.20.args_3_ = f32[4,1,512]{2,1,0:T(1,128)S(1)} collective-permute-done((f32[4,1,512]{2,1,0:T(1,128)S(1)}, f32[4,1,512]{2,1,0:T(1,128)S(1)}, u32[]{:S(2)}, u32[]{:S(2)}) %collective-permute-start.20) | collective-permute-done | bytes 8224 | tf_op jit(solution)/shard_map/ppermute | solution.py:457
  50.2 1.4 %target_gradient_2.1 = (bf16[4,512,1024]{2,1,0:T(8,128)(2,1)S(1)}, f32[4,512,128]{2,1,0:T(8,128)S(1)}, bf16[256,256]{1,0:T(8,128)(2,1)S(1)}) custom-call(f32[4,1,512]{2,1,0:T(1,128)S(1)} %get-tuple-element.58.args_0_, f32[4,1,512]{2,1,0:T(1,128)S(1)} %collective-permute-done.18.args_1_, f32[4,1,512]{2,1,0:T(1,128)S(1)} %collective-permute-done.19.args_2_, ...), custom_call_target="tpu_custom_call" | custom-call | tf_op jit(solution)/shard_map/target_gradient_2/pallas_call | solution.py:429
  52.5 1.1 %target_gradient_3.1 = (bf16[4,512,1024]{2,1,0:T(8,128)(2,1)S(1)}, bf16[256,256]{1,0:T(8,128)(2,1)S(1)}) custom-call(bf16[2048,256]{1,0:T(8,128)(2,1)S(1)} %get-tuple-element.40.args_4_.args_0_, f32[4,512,1024]{2,1,0:T(8,128)S(1)} %get-tuple-element.44.args_5_.args_4_.args_1_, ...), custom_call_target="tpu_custom_call", output_to_operand_aliasing={{0}: (10, {})} | custom-call | tf_op jit(solution)/shard_map/target_gradient_3/pallas_call | solution.py:429
  53.6 1.3 %collective-permute-start.23 = (bf16[256,256]{1,0:T(8,128)(2,1)S(1)}, bf16[256,256]{1,0:T(8,128)(2,1)S(1)}, u32[]{:S(2)}, u32[]{:S(2)}) collective-permute-start(bf16[256,256]{1,0:T(8,128)(2,1)S(1)} %get-tuple-element.66), channel_id=1, source_target_pairs={{0,12},{4,8},{8,4},{12,0},{1,13},{5,9},{9,5},{13,1},{2,14},{6,10},... | collective-permute-start | bytes 393224 | tf_op jit(solution)/shard_map/ppermute | solution.py:457
  54.9 1.3 %collective-permute-start.21 = (bf16[256,256]{1,0:T(8,128)(2,1)S(1)}, bf16[256,256]{1,0:T(8,128)(2,1)S(1)}, u32[]{:S(2)}, u32[]{:S(2)}) collective-permute-start(bf16[256,256]{1,0:T(8,128)(2,1)S(1)} %get-tuple-element.64), channel_id=1, source_target_pairs={{0,4},{4,0},{8,12},{12,8},{1,5},{5,1},{9,13},{13,9},{2,6},{6,2},{1... | collective-permute-start | bytes 393224 | tf_op jit(solution)/shard_map/ppermute | solution.py:457
  56.2 1.9 %collective-permute-start.22 = (bf16[256,256]{1,0:T(8,128)(2,1)S(1)}, bf16[256,256]{1,0:T(8,128)(2,1)S(1)}, u32[]{:S(2)}, u32[]{:S(2)}) collective-permute-start(bf16[256,256]{1,0:T(8,128)(2,1)S(1)} %get-tuple-element.65), channel_id=1, source_target_pairs={{0,8},{4,12},{8,0},{12,4},{1,9},{5,13},{9,1},{13,5},{2,10},{6,14},... | collective-permute-start | bytes 393224 | tf_op jit(solution)/shard_map/ppermute | solution.py:457
  58.0 1.0 %target_gradient_0.1 = (bf16[4,512,1024]{2,1,0:T(8,128)(2,1)S(1)}, f32[256,256]{1,0:T(8,128)S(1)}) custom-call(bf16[2048,256]{1,0:T(8,128)(2,1)S(1)} %get-tuple-element.40.args_4_.args_0_, f32[4,512,1024]{2,1,0:T(8,128)S(1)} %get-tuple-element.44.args_5_.args_4_.args_1_, ...), custom_call_target="tpu_custom_call", output_to_operand_aliasing={{0}: (10, {})} | custom-call | tf_op jit(solution)/shard_map/target_gradient_0/pallas_call | solution.py:429
  59.1 1.4 %source_gradient.1 = (f32[2,512,256]{2,1,0:T(8,128)S(1)}, bf16[2,512,256]{2,1,0:T(8,128)(2,1)S(1)}) custom-call(bf16[4,512,1024]{2,1,0:T(8,128)(2,1)S(1)} %get-tuple-element.67.bar_ref, bf16[1024,256]{1,0:T(8,128)(2,1)S(1)} %get-tuple-element.68.y_ref), custom_call_target="tpu_custom_call" | custom-call | tf_op jit(solution)/shard_map/source_gradient/pallas_call | solution.py:429
  60.5 1.4 %collective-permute-done.23 = bf16[256,256]{1,0:T(8,128)(2,1)S(1)} collective-permute-done((bf16[256,256]{1,0:T(8,128)(2,1)S(1)}, bf16[256,256]{1,0:T(8,128)(2,1)S(1)}, u32[]{:S(2)}, u32[]{:S(2)}) %collective-permute-start.23) | collective-permute-done | bytes 131104 | tf_op jit(solution)/shard_map/ppermute | solution.py:457
  61.9 1.6 %collective-permute-done.21 = bf16[256,256]{1,0:T(8,128)(2,1)S(1)} collective-permute-done((bf16[256,256]{1,0:T(8,128)(2,1)S(1)}, bf16[256,256]{1,0:T(8,128)(2,1)S(1)}, u32[]{:S(2)}, u32[]{:S(2)}) %collective-permute-start.21) | collective-permute-done | bytes 131104 | tf_op jit(solution)/shard_map/ppermute | solution.py:457
  63.5 4.4 %collective-permute-done.22 = bf16[256,256]{1,0:T(8,128)(2,1)S(1)} collective-permute-done((bf16[256,256]{1,0:T(8,128)(2,1)S(1)}, bf16[256,256]{1,0:T(8,128)(2,1)S(1)}, u32[]{:S(2)}, u32[]{:S(2)}) %collective-permute-start.22) | collective-permute-done | bytes 131104 | tf_op jit(solution)/shard_map/ppermute | solution.py:457
  68.0 1.9 %collective-permute-start.26 = (bf16[256,256]{1,0:T(8,128)(2,1)S(1)}, bf16[256,256]{1,0:T(8,128)(2,1)S(1)}, u32[]{:S(2)}, u32[]{:S(2)}) collective-permute-start(bf16[256,256]{1,0:T(8,128)(2,1)S(1)} %add_convert_fusion.args_0_), channel_id=1, source_target_pairs={{0,12},{4,8},{8,4},{12,0},{1,13},{5,9},{9,5},{13,1},{2,14},{6,10},... | collective-permute-start | bytes 393224 | tf_op jit(solution)/shard_map/ppermute | solution.py:457
  70.0 2.5 %collective-permute-start.24 = (bf16[256,256]{1,0:T(8,128)(2,1)S(1)}, bf16[256,256]{1,0:T(8,128)(2,1)S(1)}, u32[]{:S(2)}, u32[]{:S(2)}) collective-permute-start(bf16[256,256]{1,0:T(8,128)(2,1)S(1)} %add_convert_fusion.args_0_), channel_id=1, source_target_pairs={{0,4},{4,0},{8,12},{12,8},{1,5},{5,1},{9,13},{13,9},{2,6},{6,2},{1... | collective-permute-start | bytes 393224 | tf_op jit(solution)/shard_map/ppermute | solution.py:457
  73.3 3.0 %collective-permute-done.26.args_3_ = bf16[256,256]{1,0:T(8,128)(2,1)S(1)} collective-permute-done((bf16[256,256]{1,0:T(8,128)(2,1)S(1)}, bf16[256,256]{1,0:T(8,128)(2,1)S(1)}, u32[]{:S(2)}, u32[]{:S(2)}) %collective-permute-start.26) | collective-permute-done | bytes 131104 | tf_op jit(solution)/shard_map/ppermute | solution.py:457
  76.3 5.1 %collective-permute-done.25.args_2_ = bf16[256,256]{1,0:T(8,128)(2,1)S(1)} collective-permute-done((bf16[256,256]{1,0:T(8,128)(2,1)S(1)}, bf16[256,256]{1,0:T(8,128)(2,1)S(1)}, u32[]{:S(2)}, u32[]{:S(2)}) %collective-permute-start.25) | collective-permute-done | bytes 131104 | tf_op jit(solution)/shard_map/ppermute | solution.py:457
  83.0 1.1 %finish.1 = (bf16[512,256]{1,0:T(8,128)(2,1)}, bf16[2048,256]{1,0:T(8,128)(2,1)}) custom-call(bf16[256,256]{1,0:T(8,128)(2,1)S(1)} %add_convert_fusion.args_0_, bf16[256,256]{1,0:T(8,128)(2,1)S(1)} %collective-permute-done.24.args_1_, bf16[256,256]{1,0:T(8,128)(2,1)S(1)} %collective-permute-done.25.args_2_, ...), custom_call_target="tpu_custom_call" | custom-call | tf_op jit(solution)/shard_map/finish/pallas_call | solution.py:612
  (53 shorter events, 19.1 us)
Async XLA Ops:
  5.3 4.2 %collective-permute-start.2 = (f32[8,1,512]{2,1,0:T(1,128)S(1)}, f32[8,1,512]{2,1,0:T(1,128)S(1)}, u32[]{:S(2)}, u32[]{:S(2)}) collective-permute-start(f32[8,1,512]{2,1,0:T(1,128)S(1)} %get-tuple-element.41.args_0_), channel_id=1, source_target_pairs={{0,3},{1,2},{2,1},{3,0},{4,7},{5,6},{6,5},{7,4},{8,11},{9,10},{10,... | collective-permute-start | bytes 49160 | tf_op jit(solution)/shard_map/ppermute | solution.py:457
  8.1 3.7 %collective-permute-start.1 = (f32[8,1,512]{2,1,0:T(1,128)S(1)}, f32[8,1,512]{2,1,0:T(1,128)S(1)}, u32[]{:S(2)}, u32[]{:S(2)}) collective-permute-start(f32[8,1,512]{2,1,0:T(1,128)S(1)} %get-tuple-element.41.args_0_), channel_id=1, source_target_pairs={{0,2},{1,3},{2,0},{3,1},{4,6},{5,7},{6,4},{7,5},{8,10},{9,11},{10,... | collective-permute-start | bytes 49160 | tf_op jit(solution)/shard_map/ppermute | solution.py:457
  8.7 3.1 %collective-permute-start = (f32[8,1,512]{2,1,0:T(1,128)S(1)}, f32[8,1,512]{2,1,0:T(1,128)S(1)}, u32[]{:S(2)}, u32[]{:S(2)}) collective-permute-start(f32[8,1,512]{2,1,0:T(1,128)S(1)} %get-tuple-element.41.args_0_), channel_id=1, source_target_pairs={{0,1},{1,0},{2,3},{3,2},{4,5},{5,4},{6,7},{7,6},{8,9},{9,8},{10,11... | collective-permute-start | bytes 49160 | tf_op jit(solution)/shard_map/ppermute | solution.py:457
  13.5 5.6 %collective-permute-start.5 = (f32[8,1,256]{2,1,0:T(1,128)S(1)}, f32[8,1,256]{2,1,0:T(1,128)S(1)}, u32[]{:S(2)}, u32[]{:S(2)}) collective-permute-start(f32[8,1,256]{2,1,0:T(1,128)S(1)} %get-tuple-element.45.args_0_), channel_id=1, source_target_pairs={{0,12},{4,8},{8,4},{12,0},{1,13},{5,9},{9,5},{13,1},{2,14},{6,10},... | collective-permute-start | bytes 24584 | tf_op jit(solution)/shard_map/ppermute | solution.py:457
  16.9 4.5 %collective-permute-start.4 = (f32[8,1,256]{2,1,0:T(1,128)S(1)}, f32[8,1,256]{2,1,0:T(1,128)S(1)}, u32[]{:S(2)}, u32[]{:S(2)}) collective-permute-start(f32[8,1,256]{2,1,0:T(1,128)S(1)} %get-tuple-element.45.args_0_), channel_id=1, source_target_pairs={{0,8},{4,12},{8,0},{12,4},{1,9},{5,13},{9,1},{13,5},{2,10},{6,14},... | collective-permute-start | bytes 24584 | tf_op jit(solution)/shard_map/ppermute | solution.py:457
  16.9 4.5 %collective-permute-start.3 = (f32[8,1,256]{2,1,0:T(1,128)S(1)}, f32[8,1,256]{2,1,0:T(1,128)S(1)}, u32[]{:S(2)}, u32[]{:S(2)}) collective-permute-start(f32[8,1,256]{2,1,0:T(1,128)S(1)} %get-tuple-element.45.args_0_), channel_id=1, source_target_pairs={{0,4},{4,0},{8,12},{12,8},{1,5},{5,1},{9,13},{13,9},{2,6},{6,2},{1... | collective-permute-start | bytes 24584 | tf_op jit(solution)/shard_map/ppermute | solution.py:457
  22.2 3.1 %collective-permute-start.8 = (f32[4,1,512]{2,1,0:T(1,128)S(1)}, f32[4,1,512]{2,1,0:T(1,128)S(1)}, u32[]{:S(2)}, u32[]{:S(2)}) collective-permute-start(f32[4,1,512]{2,1,0:T(1,128)S(1)} %get-tuple-element.47.args_0_), channel_id=1, source_target_pairs={{0,3},{1,2},{2,1},{3,0},{4,7},{5,6},{6,5},{7,4},{8,11},{9,10},{10,... | collective-permute-start | bytes 24584 | tf_op jit(solution)/shard_map/ppermute | solution.py:457
  22.3 3.7 %collective-permute-start.7 = (f32[4,1,512]{2,1,0:T(1,128)S(1)}, f32[4,1,512]{2,1,0:T(1,128)S(1)}, u32[]{:S(2)}, u32[]{:S(2)}) collective-permute-start(f32[4,1,512]{2,1,0:T(1,128)S(1)} %get-tuple-element.47.args_0_), channel_id=1, source_target_pairs={{0,2},{1,3},{2,0},{3,1},{4,6},{5,7},{6,4},{7,5},{8,10},{9,11},{10,... | collective-permute-start | bytes 24584 | tf_op jit(solution)/shard_map/ppermute | solution.py:457
  22.8 3.2 %collective-permute-start.6 = (f32[4,1,512]{2,1,0:T(1,128)S(1)}, f32[4,1,512]{2,1,0:T(1,128)S(1)}, u32[]{:S(2)}, u32[]{:S(2)}) collective-permute-start(f32[4,1,512]{2,1,0:T(1,128)S(1)} %get-tuple-element.47.args_0_), channel_id=1, source_target_pairs={{0,1},{1,0},{2,3},{3,2},{4,5},{5,4},{6,7},{7,6},{8,9},{9,8},{10,11... | collective-permute-start | bytes 24584 | tf_op jit(solution)/shard_map/ppermute | solution.py:457
  26.9 5.5 %collective-permute-start.11 = (f32[4,1,256]{2,1,0:T(1,128)S(1)}, f32[4,1,256]{2,1,0:T(1,128)S(1)}, u32[]{:S(2)}, u32[]{:S(2)}) collective-permute-start(f32[4,1,256]{2,1,0:T(1,128)S(1)} %get-tuple-element.50.args_0_), channel_id=1, source_target_pairs={{0,12},{4,8},{8,4},{12,0},{1,13},{5,9},{9,5},{13,1},{2,14},{6,10},... | collective-permute-start | bytes 12296 | tf_op jit(solution)/shard_map/ppermute | solution.py:457
  28.4 4.5 %collective-permute-start.10 = (f32[4,1,256]{2,1,0:T(1,128)S(1)}, f32[4,1,256]{2,1,0:T(1,128)S(1)}, u32[]{:S(2)}, u32[]{:S(2)}) collective-permute-start(f32[4,1,256]{2,1,0:T(1,128)S(1)} %get-tuple-element.50.args_0_), channel_id=1, source_target_pairs={{0,8},{4,12},{8,0},{12,4},{1,9},{5,13},{9,1},{13,5},{2,10},{6,14},... | collective-permute-start | bytes 12296 | tf_op jit(solution)/shard_map/ppermute | solution.py:457
  29.1 3.9 %collective-permute-start.9 = (f32[4,1,256]{2,1,0:T(1,128)S(1)}, f32[4,1,256]{2,1,0:T(1,128)S(1)}, u32[]{:S(2)}, u32[]{:S(2)}) collective-permute-start(f32[4,1,256]{2,1,0:T(1,128)S(1)} %get-tuple-element.50.args_0_), channel_id=1, source_target_pairs={{0,4},{4,0},{8,12},{12,8},{1,5},{5,1},{9,13},{13,9},{2,6},{6,2},{1... | collective-permute-start | bytes 12296 | tf_op jit(solution)/shard_map/ppermute | solution.py:457
  33.8 3.1 %collective-permute-start.14 = (f32[4,1,512]{2,1,0:T(1,128)S(1)}, f32[4,1,512]{2,1,0:T(1,128)S(1)}, u32[]{:S(2)}, u32[]{:S(2)}) collective-permute-start(f32[4,1,512]{2,1,0:T(1,128)S(1)} %get-tuple-element.51.args_0_), channel_id=1, source_target_pairs={{0,3},{1,2},{2,1},{3,0},{4,7},{5,6},{6,5},{7,4},{8,11},{9,10},{10,... | collective-permute-start | bytes 24584 | tf_op jit(solution)/shard_map/ppermute | solution.py:457
  33.9 3.7 %collective-permute-start.13 = (f32[4,1,512]{2,1,0:T(1,128)S(1)}, f32[4,1,512]{2,1,0:T(1,128)S(1)}, u32[]{:S(2)}, u32[]{:S(2)}) collective-permute-start(f32[4,1,512]{2,1,0:T(1,128)S(1)} %get-tuple-element.51.args_0_), channel_id=1, source_target_pairs={{0,2},{1,3},{2,0},{3,1},{4,6},{5,7},{6,4},{7,5},{8,10},{9,11},{10,... | collective-permute-start | bytes 24584 | tf_op jit(solution)/shard_map/ppermute | solution.py:457
  34.7 2.9 %collective-permute-start.12 = (f32[4,1,512]{2,1,0:T(1,128)S(1)}, f32[4,1,512]{2,1,0:T(1,128)S(1)}, u32[]{:S(2)}, u32[]{:S(2)}) collective-permute-start(f32[4,1,512]{2,1,0:T(1,128)S(1)} %get-tuple-element.51.args_0_), channel_id=1, source_target_pairs={{0,1},{1,0},{2,3},{3,2},{4,5},{5,4},{6,7},{7,6},{8,9},{9,8},{10,11... | collective-permute-start | bytes 24584 | tf_op jit(solution)/shard_map/ppermute | solution.py:457
  38.4 5.5 %collective-permute-start.17 = (f32[4,1,256]{2,1,0:T(1,128)S(1)}, f32[4,1,256]{2,1,0:T(1,128)S(1)}, u32[]{:S(2)}, u32[]{:S(2)}) collective-permute-start(f32[4,1,256]{2,1,0:T(1,128)S(1)} %get-tuple-element.55.args_0_), channel_id=1, source_target_pairs={{0,12},{4,8},{8,4},{12,0},{1,13},{5,9},{9,5},{13,1},{2,14},{6,10},... | collective-permute-start | bytes 12296 | tf_op jit(solution)/shard_map/ppermute | solution.py:457
  41.0 4.5 %collective-permute-start.16 = (f32[4,1,256]{2,1,0:T(1,128)S(1)}, f32[4,1,256]{2,1,0:T(1,128)S(1)}, u32[]{:S(2)}, u32[]{:S(2)}) collective-permute-start(f32[4,1,256]{2,1,0:T(1,128)S(1)} %get-tuple-element.55.args_0_), channel_id=1, source_target_pairs={{0,8},{4,12},{8,0},{12,4},{1,9},{5,13},{9,1},{13,5},{2,10},{6,14},... | collective-permute-start | bytes 12296 | tf_op jit(solution)/shard_map/ppermute | solution.py:457
  41.9 3.6 %collective-permute-start.15 = (f32[4,1,256]{2,1,0:T(1,128)S(1)}, f32[4,1,256]{2,1,0:T(1,128)S(1)}, u32[]{:S(2)}, u32[]{:S(2)}) collective-permute-start(f32[4,1,256]{2,1,0:T(1,128)S(1)} %get-tuple-element.55.args_0_), channel_id=1, source_target_pairs={{0,4},{4,0},{8,12},{12,8},{1,5},{5,1},{9,13},{13,9},{2,6},{6,2},{1... | collective-permute-start | bytes 12296 | tf_op jit(solution)/shard_map/ppermute | solution.py:457
  46.4 3.1 %collective-permute-start.20 = (f32[4,1,512]{2,1,0:T(1,128)S(1)}, f32[4,1,512]{2,1,0:T(1,128)S(1)}, u32[]{:S(2)}, u32[]{:S(2)}) collective-permute-start(f32[4,1,512]{2,1,0:T(1,128)S(1)} %get-tuple-element.58.args_0_), channel_id=1, source_target_pairs={{0,3},{1,2},{2,1},{3,0},{4,7},{5,6},{6,5},{7,4},{8,11},{9,10},{10,... | collective-permute-start | bytes 24584 | tf_op jit(solution)/shard_map/ppermute | solution.py:457
  46.5 3.7 %collective-permute-start.19 = (f32[4,1,512]{2,1,0:T(1,128)S(1)}, f32[4,1,512]{2,1,0:T(1,128)S(1)}, u32[]{:S(2)}, u32[]{:S(2)}) collective-permute-start(f32[4,1,512]{2,1,0:T(1,128)S(1)} %get-tuple-element.58.args_0_), channel_id=1, source_target_pairs={{0,2},{1,3},{2,0},{3,1},{4,6},{5,7},{6,4},{7,5},{8,10},{9,11},{10,... | collective-permute-start | bytes 24584 | tf_op jit(solution)/shard_map/ppermute | solution.py:457
  47.1 3.1 %collective-permute-start.18 = (f32[4,1,512]{2,1,0:T(1,128)S(1)}, f32[4,1,512]{2,1,0:T(1,128)S(1)}, u32[]{:S(2)}, u32[]{:S(2)}) collective-permute-start(f32[4,1,512]{2,1,0:T(1,128)S(1)} %get-tuple-element.58.args_0_), channel_id=1, source_target_pairs={{0,1},{1,0},{2,3},{3,2},{4,5},{5,4},{6,7},{7,6},{8,9},{9,8},{10,11... | collective-permute-start | bytes 24584 | tf_op jit(solution)/shard_map/ppermute | solution.py:457
  53.6 8.3 %collective-permute-start.23 = (bf16[256,256]{1,0:T(8,128)(2,1)S(1)}, bf16[256,256]{1,0:T(8,128)(2,1)S(1)}, u32[]{:S(2)}, u32[]{:S(2)}) collective-permute-start(bf16[256,256]{1,0:T(8,128)(2,1)S(1)} %get-tuple-element.66), channel_id=1, source_target_pairs={{0,12},{4,8},{8,4},{12,0},{1,13},{5,9},{9,5},{13,1},{2,14},{6,10},... | collective-permute-start | bytes 393224 | tf_op jit(solution)/shard_map/ppermute | solution.py:457
  54.9 8.6 %collective-permute-start.21 = (bf16[256,256]{1,0:T(8,128)(2,1)S(1)}, bf16[256,256]{1,0:T(8,128)(2,1)S(1)}, u32[]{:S(2)}, u32[]{:S(2)}) collective-permute-start(bf16[256,256]{1,0:T(8,128)(2,1)S(1)} %get-tuple-element.64), channel_id=1, source_target_pairs={{0,4},{4,0},{8,12},{12,8},{1,5},{5,1},{9,13},{13,9},{2,6},{6,2},{1... | collective-permute-start | bytes 393224 | tf_op jit(solution)/shard_map/ppermute | solution.py:457
  56.2 11.8 %collective-permute-start.22 = (bf16[256,256]{1,0:T(8,128)(2,1)S(1)}, bf16[256,256]{1,0:T(8,128)(2,1)S(1)}, u32[]{:S(2)}, u32[]{:S(2)}) collective-permute-start(bf16[256,256]{1,0:T(8,128)(2,1)S(1)} %get-tuple-element.65), channel_id=1, source_target_pairs={{0,8},{4,12},{8,0},{12,4},{1,9},{5,13},{9,1},{13,5},{2,10},{6,14},... | collective-permute-start | bytes 393224 | tf_op jit(solution)/shard_map/ppermute | solution.py:457
  68.0 4.5 %collective-permute-start.31 = (bf16[2,512,256]{2,1,0:T(8,128)(2,1)S(1)}, bf16[2,512,256]{2,1,0:T(8,128)(2,1)S(1)}, u32[]{:S(2)}, u32[]{:S(2)}) collective-permute-start(bf16[2,512,256]{2,1,0:T(8,128)(2,1)S(1)} %get-tuple-element.75), channel_id=1, source_target_pairs={{0,1},{1,0},{2,3},{3,2},{4,5},{5,4},{6,7},{7,6},{8,9},{9,8},{10,11... | collective-permute-start | bytes 1572872 | tf_op jit(solution)/shard_map/ppermute | solution.py:457
  68.0 8.3 %collective-permute-start.26 = (bf16[256,256]{1,0:T(8,128)(2,1)S(1)}, bf16[256,256]{1,0:T(8,128)(2,1)S(1)}, u32[]{:S(2)}, u32[]{:S(2)}) collective-permute-start(bf16[256,256]{1,0:T(8,128)(2,1)S(1)} %add_convert_fusion.args_0_), channel_id=1, source_target_pairs={{0,12},{4,8},{8,4},{12,0},{1,13},{5,9},{9,5},{13,1},{2,14},{6,10},... | collective-permute-start | bytes 393224 | tf_op jit(solution)/shard_map/ppermute | solution.py:457
  70.0 11.5 %collective-permute-start.25 = (bf16[256,256]{1,0:T(8,128)(2,1)S(1)}, bf16[256,256]{1,0:T(8,128)(2,1)S(1)}, u32[]{:S(2)}, u32[]{:S(2)}) collective-permute-start(bf16[256,256]{1,0:T(8,128)(2,1)S(1)} %add_convert_fusion.args_0_), channel_id=1, source_target_pairs={{0,8},{4,12},{8,0},{12,4},{1,9},{5,13},{9,1},{13,5},{2,10},{6,14},... | collective-permute-start | bytes 393224 | tf_op jit(solution)/shard_map/ppermute | solution.py:457
  70.0 11.6 %collective-permute-start.24 = (bf16[256,256]{1,0:T(8,128)(2,1)S(1)}, bf16[256,256]{1,0:T(8,128)(2,1)S(1)}, u32[]{:S(2)}, u32[]{:S(2)}) collective-permute-start(bf16[256,256]{1,0:T(8,128)(2,1)S(1)} %add_convert_fusion.args_0_), channel_id=1, source_target_pairs={{0,4},{4,0},{8,12},{12,8},{1,5},{5,1},{9,13},{13,9},{2,6},{6,2},{1... | collective-permute-start | bytes 393224 | tf_op jit(solution)/shard_map/ppermute | solution.py:457
  72.6 10.4 %collective-permute-start.32 = (bf16[512,256]{1,0:T(8,128)(2,1)S(1)}, bf16[512,256]{1,0:T(8,128)(2,1)S(1)}, u32[]{:S(2)}, u32[]{:S(2)}) collective-permute-start(bf16[512,256]{1,0:T(8,128)(2,1)S(1)} %get-tuple-element.77), channel_id=1, source_target_pairs={{0,2},{2,0},{1,3},{3,1},{4,6},{6,4},{5,7},{7,5},{8,10},{10,8},{9,1... | collective-permute-start | bytes 786440 | tf_op jit(solution)/shard_map/ppermute | solution.py:457
  73.3 8.7 %collective-permute-start.27 = (bf16[256,256]{1,0:T(8,128)(2,1)S(1)}, bf16[256,256]{1,0:T(8,128)(2,1)S(1)}, u32[]{:S(2)}, u32[]{:S(2)}) collective-permute-start(bf16[256,256]{1,0:T(8,128)(2,1)S(1)} %add_convert_fusion.args_0_), channel_id=1, source_target_pairs={{0,1},{1,0},{2,3},{3,2},{4,5},{5,4},{6,7},{7,6},{8,9},{9,8},{10,11... | collective-permute-start | bytes 393224 | tf_op jit(solution)/shard_map/ppermute | solution.py:457
  76.3 5.7 %collective-permute-start.30 = (bf16[256,256]{1,0:T(8,128)(2,1)S(1)}, bf16[256,256]{1,0:T(8,128)(2,1)S(1)}, u32[]{:S(2)}, u32[]{:S(2)}) collective-permute-start(bf16[256,256]{1,0:T(8,128)(2,1)S(1)} %collective-permute-done.26.args_3_), channel_id=1, source_target_pairs={{0,1},{1,0},{2,3},{3,2},{4,5},{5,4},{6,7},{7,6},{8,9},{9,8},{10,11... | collective-permute-start | bytes 393224 | tf_op jit(solution)/shard_map/ppermute | solution.py:457
  81.5 1.5 %collective-permute-start.28 = (bf16[256,256]{1,0:T(8,128)(2,1)S(1)}, bf16[256,256]{1,0:T(8,128)(2,1)S(1)}, u32[]{:S(2)}, u32[]{:S(2)}) collective-permute-start(bf16[256,256]{1,0:T(8,128)(2,1)S(1)} %collective-permute-done.24.args_1_), channel_id=1, source_target_pairs={{0,1},{1,0},{2,3},{3,2},{4,5},{5,4},{6,7},{7,6},{8,9},{9,8},{10,11... | collective-permute-start | bytes 393224 | tf_op jit(solution)/shard_map/ppermute | solution.py:457
  (3 other events, 12.9 us)

commit v3 on v2

--- a/solution.py
+++ b/solution.py
@@ -124,6 +124,8 @@
     sb_ref,
     tb_ref,
     kp_ref,
+    even_ref,
+    odd_ref,
     x_sems,
     y_sems,
     warm_sems,
@@ -172,26 +174,35 @@
     inv_root = x_ref.shape[1] ** (-0.5)
     for copy in y_copies:
         copy.wait()
-    for s in range(BLOCK):
-        x_copies[s].wait()
-        score_ref[s] = inv_root * lax.dot_general(
+
+    def scores(s):
+        buffers[s % 2][...] = inv_root * lax.dot_general(
             x_ref[s * TILE : (s + 1) * TILE, :],
             y_ref[...],
             NT_DIMS,
             preferred_element_type=F32,
         )
+
+    buffers = (even_ref, odd_ref)
+    x_copies[0].wait()
+    scores(0)
     for copy in warm_copies:
         copy.wait()
-
-    def one(s, carry):
+    for s in range(BLOCK):
         low, high = kept_targets(meta, s)
+        buffer = buffers[s % 2]
+        if s + 1 < BLOCK:
+            x_copies[s + 1].wait()
 
         def body(n):
             warm = [warm_ref[low + i] for i in range(n)]
+            if s + 1 < BLOCK:
+                scores(s + 1)
             for at in range(0, TILE, LANES):
                 largest = None
                 for i in range(n):
-                    e = score_ref[s, at : at + LANES, tile_lanes(low + i)]
+                    e = buffer[at : at + LANES, tile_lanes(low + i)]
+                    score_ref[s, at : at + LANES, tile_lanes(low + i)] = e
                     term = jnp.maximum(
                         e[:, :LANES] + warm[i][:, :LANES], e[:, LANES:] + warm[i][:, LANES:]
                     )
@@ -200,7 +211,7 @@
                 largest = jnp.broadcast_to(largest, (LANES, LANES))
                 acc = None
                 for i in range(n):
-                    e = score_ref[s, at : at + LANES, tile_lanes(low + i)]
+                    e = buffer[at : at + LANES, tile_lanes(low + i)]
                     term = jnp.exp(e[:, :LANES] + warm[i][:, :LANES] - largest) + jnp.exp(
                         e[:, LANES:] + warm[i][:, LANES:] - largest
                     )
@@ -209,9 +220,6 @@
                 out_ref[BLOCK + s, :, at : at + LANES] = lane_sums(acc)
 
         for_widths(low, high, body)
-        return carry
-
-    lax.fori_loop(0, BLOCK, one, 0)
 
 
 def combine(refs, at, offset):
@@ -333,49 +341,54 @@
     t = (row_pos // per_tile) ^ part
     low, high = kept_sources(read_meta(meta_ref), t)
     p, q, h, wq = p_ref[t], q_ref[t], h_ref[t], wq_ref[t]
-    for s in range(BLOCK):
-
-        @pl.when((s >= low) & (s < high))
-        def _():
-            for at in range(0, TILE, ROWS):
-                e = e_ref[s, at : at + ROWS, tile_lanes(t)]
-                a = a_ref[s, at : at + ROWS, :]
-                b = b_ref[s, at : at + ROWS, :]
-                early = early_ref[s, at : at + ROWS, :]
-                sides = []
-                for side in (slice(0, LANES), slice(LANES, HALF)):
-                    factor = a * p[:, side] + b * q[:, side] + (h[:, side] + early * wq[:, side])
-                    sides.append((e[:, side] * factor).astype(jnp.bfloat16))
-                bar_ref[s, at : at + ROWS, tile_lanes(t)] = jnp.concatenate(sides, axis=1)
-
-        @pl.when((s < low) | (s >= high))
-        def _():
-            bar_ref[s, :, tile_lanes(t)] = jnp.zeros((TILE, HALF), jnp.bfloat16)
-
-    bar = bar_ref[:, :, tile_lanes(t)].reshape(BLOCK * TILE, HALF)
     inv_root = x_ref.shape[1] ** (-0.5)
-    result = -inv_root * lax.dot_general(bar, x_ref[...], TN_DIMS, preferred_element_type=F32)
-    if per_tile == 1:
-        out_refs[0][...] = result.astype(out_refs[0].dtype)
-        return
     piece = HALF // per_tile
-    for i, ref in enumerate(out_refs):
-        at = (row_pos % per_tile) ^ i
-        for j in range(per_tile):
-
-            @pl.when(at == j)
-            def _():
-                ref[...] = result[j * piece : (j + 1) * piece, :].astype(ref.dtype)
-
-
-def source_gradient_kernel(bar_ref, y_ref, near_ref, far_ref, acc_ref):
+
+    def term(s):
+        for at in range(0, TILE, ROWS):
+            e = e_ref[s, at : at + ROWS, tile_lanes(t)]
+            a = a_ref[s, at : at + ROWS, :]
+            b = b_ref[s, at : at + ROWS, :]
+            early = early_ref[s, at : at + ROWS, :]
+            sides = []
+            for side in (slice(0, LANES), slice(LANES, HALF)):
+                factor = a * p[:, side] + b * q[:, side] + (h[:, side] + early * wq[:, side])
+                sides.append((e[:, side] * factor).astype(jnp.bfloat16))
+            bar_ref[s, at : at + ROWS, tile_lanes(t)] = jnp.concatenate(sides, axis=1)
+        x = x_ref[pl.ds(pl.multiple_of(s * TILE, TILE), TILE), :]
+        bar = bar_ref[s, :, tile_lanes(t)]
+        return lax.dot_general(bar, x, TN_DIMS, preferred_element_type=F32)
+
+    def body(n):
+        result = term(low)
+        for i in range(1, n):
+            result = result + term(low + i)
+        result = -inv_root * result
+        for i, ref in enumerate(out_refs):
+            for j in range(per_tile):
+
+                @pl.when(((row_pos % per_tile) ^ i) == j)
+                def _():
+                    ref[...] = result[j * piece : (j + 1) * piece, :].astype(ref.dtype)
+
+    for_widths(low, high, body)
+
+
+def source_gradient_kernel(bar_ref, y_ref, meta_ref, near_ref, far_ref, acc_ref):
     inv_root = y_ref.shape[1] ** (-0.5)
     col_pos = lax.axis_index("col")
     rep_pos = lax.axis_index("rep")
+    meta = read_meta(meta_ref)
     for s in range(BLOCK):
-        acc_ref[s * TILE : (s + 1) * TILE, :] = -inv_root * lax.dot_general(
-            bar_ref[s], y_ref[...], NN_DIMS, preferred_element_type=F32
-        )
+        low, high = kept_targets(meta, s)
+
+        def body(n):
+            kept = pl.ds(pl.multiple_of(low * HALF, HALF), n * HALF)
+            acc_ref[s * TILE : (s + 1) * TILE, :] = -inv_root * lax.dot_general(
+                bar_ref[s, :, kept], y_ref[kept, :], NN_DIMS, preferred_element_type=F32
+            )
+
+        for_widths(low, high, body)
     piece = near_ref.shape[1]
     for d in range(near_ref.shape[0]):
         at = 2 * (col_pos ^ d)
@@ -486,6 +499,8 @@
             pltpu.SMEM(source_bounds.shape, jnp.int32),
             pltpu.SMEM(target_bounds.shape, jnp.int32),
             pltpu.SMEM(kept_pairs.shape[::-1], jnp.int32),
+            pltpu.VMEM(matrix[1:], F32),
+            pltpu.VMEM(matrix[1:], F32),
         ]
         + [pltpu.SemaphoreType.DMA((BLOCK,))] * 4,
         [
@@ -557,7 +572,7 @@
     pieces = [None] * rows
     arrived = [None] * rows
     bar = early = None
-    for part in (2, 1, 3, 0):
+    for part in (3, 2, 1, 0):
         outs = [((piece, width), bf16 if part or i else F32) for i in range(per_tile)]
         if bar is None:
             bar, early, *results = call(
@@ -568,6 +583,9 @@
                 [*parts, *shared],
             )
         else:
+            if part == 0:
+                first = slice((3, 2, 1, 0)[0] * per_tile, ((3, 2, 1, 0)[0] + 1) * per_tile)
+                bar, arrived[first] = lax.optimization_barrier((bar, arrived[first]))
             bar, *results = call(
                 functools.partial(target_gradient_kernel, part, 0),
                 f"target_gradient_{part}",
@@ -588,7 +606,7 @@
         "source_gradient",
         [(halves, F32), (halves, bf16)],
         [pltpu.VMEM((BLOCK * TILE, width), F32)],
-        [bar, y],
+        [bar, y, meta],
     )
     def added(values):
         value = values[0].astype(F32)

time: 84.8 us -> 82.1 us (0.968)
  Pallas kernels: 17.5 us -> 14.7 us
  starting transfers between devices: 32.7 us -> 34.1 us
  waiting for transfers between devices: 33.1 us -> 31.9 us
    pallas_call x13, Pallas kernels: 16.4 us -> 13.6 us  [call(): pl.pallas_call(kernel, name=name, out_shape=[pltpu.VMEM(shape, dtype) for...]
    ppermute x33, starting transfers between devices: 32.7 us -> 34.1 us  [swap(): return lax.ppermute(value, axes, [(i, i ^ k) for i in range(count)])]
    ppermute x33, waiting for transfers between devices: 33.1 us -> 31.9 us  [swap(): return lax.ppermute(value, axes, [(i, i ^ k) for i in range(count)])]
  transfers between devices with their start and end apart: 33 -> 33, of which waited for: 21 -> 21; matrix products, arithmetic and copies ran while one was open for 0% -> 0% of each run, Pallas kernels for 3% -> 4%
where the time goes in v3:
time: 82.1 us; the launch traced here: 81.8 us
  starting transfers between devices  34.1 us (42%)
  waiting for transfers between devices  31.9 us (39%)
  Pallas kernels  14.7 us (18%)
  between operations  0.94 us (1%)
    ppermute x33, starting transfers between devices, swap(): return lax.ppermute(value, axes, [(i, i ^ k) for i in range(count)])  34.1 us
    ppermute x33, waiting for transfers between devices, swap(): return lax.ppermute(value, axes, [(i, i ^ k) for i in range(count)])  31.9 us
    pallas_call x13, Pallas kernels, call(): pl.pallas_call(kernel, name=name, out_shape=[pltpu.VMEM(shape, dtype) for...  13.6 us
  transfers between devices with their start and end apart: 33, of which 21 were waited for; matrix products, arithmetic and copies ran while one was open for 0% of the time, Pallas kernels for 4%

profile of v3, /device:TPU:0, one launch (start us, length us, event | category | flops | bytes accessed | tf_op | source)
XLA Modules:
  0.0 81.8 jit_solution(16073139052930388338)
XLA Ops:
  0.6 4.0 %first_source.1 = (f32[4,512,1024]{2,1,0:T(8,128)S(1)}, f32[8,1,512]{2,1,0:T(1,128)S(1)}, s32[8,128]{1,0:T(8,128)S(1)}, bf16[2048,256]{1,0:T(8,128)(2,1)S(1)}, b...) custom-call(bf16[2048,256]{1,0:T(8,128)(2,1)} %x_hbm.1, bf16[2048,256]{1,0:T(8,128)(2,1)} %y_hbm.1, ...), custom_call_target="tpu_custom_call" | custom-call | tf_op jit(solution)/shard_map/first_source/pallas_call | solution.py:442
  4.6 2.8 %collective-permute-start.2 = (f32[8,1,512]{2,1,0:T(1,128)S(1)}, f32[8,1,512]{2,1,0:T(1,128)S(1)}, u32[]{:S(2)}, u32[]{:S(2)}) collective-permute-start(f32[8,1,512]{2,1,0:T(1,128)S(1)} %get-tuple-element.43.args_0_), channel_id=1, source_target_pairs={{0,3},{1,2},{2,1},{3,0},{4,7},{5,6},{6,5},{7,4},{8,11},{9,10},{10,... | collective-permute-start | bytes 49160 | tf_op jit(solution)/shard_map/ppermute | solution.py:470
  8.9 2.3 %collective-permute-done.1.args_2_ = f32[8,1,512]{2,1,0:T(1,128)S(1)} collective-permute-done((f32[8,1,512]{2,1,0:T(1,128)S(1)}, f32[8,1,512]{2,1,0:T(1,128)S(1)}, u32[]{:S(2)}, u32[]{:S(2)}) %collective-permute-start.1) | collective-permute-done | bytes 16416 | tf_op jit(solution)/shard_map/ppermute | solution.py:470
  11.2 1.3 %first_target.1 = (f32[4,512,1024]{2,1,0:T(8,128)S(1)}, f32[8,1,256]{2,1,0:T(1,128)S(1)}) custom-call(f32[8,1,512]{2,1,0:T(1,128)S(1)} %get-tuple-element.43.args_0_, f32[8,1,512]{2,1,0:T(1,128)S(1)} %collective-permute-done.args_1_, f32[8,1,512]{2,1,0:T(1,128)S(1)} %collective-permute-done.1.args_2_, f32[8,1,512]{2,1,0:T(1,128)S(1)} %collective-permute-done.2.args_3_, ...), custom_call_target="tpu_custom_call" | custom-call | tf_op jit(solution)/shard_map/first_target/pallas_call | solution.py:442
  12.6 3.9 %collective-permute-start.5 = (f32[8,1,256]{2,1,0:T(1,128)S(1)}, f32[8,1,256]{2,1,0:T(1,128)S(1)}, u32[]{:S(2)}, u32[]{:S(2)}) collective-permute-start(f32[8,1,256]{2,1,0:T(1,128)S(1)} %get-tuple-element.47.args_0_), channel_id=1, source_target_pairs={{0,12},{4,8},{8,4},{12,0},{1,13},{5,9},{9,5},{13,1},{2,14},{6,10},... | collective-permute-start | bytes 24584 | tf_op jit(solution)/shard_map/ppermute | solution.py:470
  17.1 1.0 %collective-permute-done.5.args_3_ = f32[8,1,256]{2,1,0:T(1,128)S(1)} collective-permute-done((f32[8,1,256]{2,1,0:T(1,128)S(1)}, f32[8,1,256]{2,1,0:T(1,128)S(1)}, u32[]{:S(2)}, u32[]{:S(2)}) %collective-permute-start.5) | collective-permute-done | bytes 8224 | tf_op jit(solution)/shard_map/ppermute | solution.py:470
  18.1 2.9 %collective-permute-done.4.args_2_ = f32[8,1,256]{2,1,0:T(1,128)S(1)} collective-permute-done((f32[8,1,256]{2,1,0:T(1,128)S(1)}, f32[8,1,256]{2,1,0:T(1,128)S(1)}, u32[]{:S(2)}, u32[]{:S(2)}) %collective-permute-start.4) | collective-permute-done | bytes 8224 | tf_op jit(solution)/shard_map/ppermute | solution.py:470
  22.4 1.4 %collective-permute-start.6 = (f32[4,1,512]{2,1,0:T(1,128)S(1)}, f32[4,1,512]{2,1,0:T(1,128)S(1)}, u32[]{:S(2)}, u32[]{:S(2)}) collective-permute-start(f32[4,1,512]{2,1,0:T(1,128)S(1)} %get-tuple-element.49.args_0_), channel_id=1, source_target_pairs={{0,1},{1,0},{2,3},{3,2},{4,5},{5,4},{6,7},{7,6},{8,9},{9,8},{10,11... | collective-permute-start | bytes 24584 | tf_op jit(solution)/shard_map/ppermute | solution.py:470
  23.8 1.2 %collective-permute-done.8.args_3_ = f32[4,1,512]{2,1,0:T(1,128)S(1)} collective-permute-done((f32[4,1,512]{2,1,0:T(1,128)S(1)}, f32[4,1,512]{2,1,0:T(1,128)S(1)}, u32[]{:S(2)}, u32[]{:S(2)}) %collective-permute-start.8) | collective-permute-done | bytes 8224 | tf_op jit(solution)/shard_map/ppermute | solution.py:470
  26.4 1.8 %collective-permute-start.11 = (f32[4,1,256]{2,1,0:T(1,128)S(1)}, f32[4,1,256]{2,1,0:T(1,128)S(1)}, u32[]{:S(2)}, u32[]{:S(2)}) collective-permute-start(f32[4,1,256]{2,1,0:T(1,128)S(1)} %get-tuple-element.52.args_0_), channel_id=1, source_target_pairs={{0,12},{4,8},{8,4},{12,0},{1,13},{5,9},{9,5},{13,1},{2,14},{6,10},... | collective-permute-start | bytes 12296 | tf_op jit(solution)/shard_map/ppermute | solution.py:470
  28.9 2.0 %collective-permute-start.9 = (f32[4,1,256]{2,1,0:T(1,128)S(1)}, f32[4,1,256]{2,1,0:T(1,128)S(1)}, u32[]{:S(2)}, u32[]{:S(2)}) collective-permute-start(f32[4,1,256]{2,1,0:T(1,128)S(1)} %get-tuple-element.52.args_0_), channel_id=1, source_target_pairs={{0,4},{4,0},{8,12},{12,8},{1,5},{5,1},{9,13},{13,9},{2,6},{6,2},{1... | collective-permute-start | bytes 12296 | tf_op jit(solution)/shard_map/ppermute | solution.py:470
  30.9 1.0 %collective-permute-done.11.args_3_ = f32[4,1,256]{2,1,0:T(1,128)S(1)} collective-permute-done((f32[4,1,256]{2,1,0:T(1,128)S(1)}, f32[4,1,256]{2,1,0:T(1,128)S(1)}, u32[]{:S(2)}, u32[]{:S(2)}) %collective-permute-start.11) | collective-permute-done | bytes 4128 | tf_op jit(solution)/shard_map/ppermute | solution.py:470
  34.1 1.4 %collective-permute-start.12 = (f32[4,1,512]{2,1,0:T(1,128)S(1)}, f32[4,1,512]{2,1,0:T(1,128)S(1)}, u32[]{:S(2)}, u32[]{:S(2)}) collective-permute-start(f32[4,1,512]{2,1,0:T(1,128)S(1)} %get-tuple-element.53.args_0_), channel_id=1, source_target_pairs={{0,1},{1,0},{2,3},{3,2},{4,5},{5,4},{6,7},{7,6},{8,9},{9,8},{10,11... | collective-permute-start | bytes 24584 | tf_op jit(solution)/shard_map/ppermute | solution.py:470
  35.5 1.2 %collective-permute-done.14.args_3_ = f32[4,1,512]{2,1,0:T(1,128)S(1)} collective-permute-done((f32[4,1,512]{2,1,0:T(1,128)S(1)}, f32[4,1,512]{2,1,0:T(1,128)S(1)}, u32[]{:S(2)}, u32[]{:S(2)}) %collective-permute-start.14) | collective-permute-done | bytes 8224 | tf_op jit(solution)/shard_map/ppermute | solution.py:470
  38.2 2.9 %collective-permute-start.17 = (f32[4,1,256]{2,1,0:T(1,128)S(1)}, f32[4,1,256]{2,1,0:T(1,128)S(1)}, u32[]{:S(2)}, u32[]{:S(2)}) collective-permute-start(f32[4,1,256]{2,1,0:T(1,128)S(1)} %get-tuple-element.57.args_0_), channel_id=1, source_target_pairs={{0,12},{4,8},{8,4},{12,0},{1,13},{5,9},{9,5},{13,1},{2,14},{6,10},... | collective-permute-start | bytes 12296 | tf_op jit(solution)/shard_map/ppermute | solution.py:470
  41.5 1.1 %collective-permute-start.15 = (f32[4,1,256]{2,1,0:T(1,128)S(1)}, f32[4,1,256]{2,1,0:T(1,128)S(1)}, u32[]{:S(2)}, u32[]{:S(2)}) collective-permute-start(f32[4,1,256]{2,1,0:T(1,128)S(1)} %get-tuple-element.57.args_0_), channel_id=1, source_target_pairs={{0,4},{4,0},{8,12},{12,8},{1,5},{5,1},{9,13},{13,9},{2,6},{6,2},{1... | collective-permute-start | bytes 12296 | tf_op jit(solution)/shard_map/ppermute | solution.py:470
  42.6 1.0 %collective-permute-done.17.args_3_ = f32[4,1,256]{2,1,0:T(1,128)S(1)} collective-permute-done((f32[4,1,256]{2,1,0:T(1,128)S(1)}, f32[4,1,256]{2,1,0:T(1,128)S(1)}, u32[]{:S(2)}, u32[]{:S(2)}) %collective-permute-start.17) | collective-permute-done | bytes 4128 | tf_op jit(solution)/shard_map/ppermute | solution.py:470
  43.6 1.9 %collective-permute-done.16.args_2_ = f32[4,1,256]{2,1,0:T(1,128)S(1)} collective-permute-done((f32[4,1,256]{2,1,0:T(1,128)S(1)}, f32[4,1,256]{2,1,0:T(1,128)S(1)}, u32[]{:S(2)}, u32[]{:S(2)}) %collective-permute-start.16) | collective-permute-done | bytes 4128 | tf_op jit(solution)/shard_map/ppermute | solution.py:470
  46.8 1.6 %collective-permute-start.18 = (f32[4,1,512]{2,1,0:T(1,128)S(1)}, f32[4,1,512]{2,1,0:T(1,128)S(1)}, u32[]{:S(2)}, u32[]{:S(2)}) collective-permute-start(f32[4,1,512]{2,1,0:T(1,128)S(1)} %get-tuple-element.60.args_0_), channel_id=1, source_target_pairs={{0,1},{1,0},{2,3},{3,2},{4,5},{5,4},{6,7},{7,6},{8,9},{9,8},{10,11... | collective-permute-start | bytes 24584 | tf_op jit(solution)/shard_map/ppermute | solution.py:470
  48.3 1.2 %collective-permute-done.20.args_3_ = f32[4,1,512]{2,1,0:T(1,128)S(1)} collective-permute-done((f32[4,1,512]{2,1,0:T(1,128)S(1)}, f32[4,1,512]{2,1,0:T(1,128)S(1)}, u32[]{:S(2)}, u32[]{:S(2)}) %collective-permute-start.20) | collective-permute-done | bytes 8224 | tf_op jit(solution)/shard_map/ppermute | solution.py:470
  51.2 1.6 %collective-permute-start.21 = (bf16[256,256]{1,0:T(8,128)(2,1)S(1)}, bf16[256,256]{1,0:T(8,128)(2,1)S(1)}, u32[]{:S(2)}, u32[]{:S(2)}) collective-permute-start(bf16[256,256]{1,0:T(8,128)(2,1)S(1)} %get-tuple-element.65), channel_id=1, source_target_pairs={{0,12},{4,8},{8,4},{12,0},{1,13},{5,9},{9,5},{13,1},{2,14},{6,10},... | collective-permute-start | bytes 393224 | tf_op jit(solution)/shard_map/ppermute | solution.py:470
  53.8 1.9 %collective-permute-start.22 = (bf16[256,256]{1,0:T(8,128)(2,1)S(1)}, bf16[256,256]{1,0:T(8,128)(2,1)S(1)}, u32[]{:S(2)}, u32[]{:S(2)}) collective-permute-start(bf16[256,256]{1,0:T(8,128)(2,1)S(1)} %get-tuple-element.68), channel_id=1, source_target_pairs={{0,4},{4,0},{8,12},{12,8},{1,5},{5,1},{9,13},{13,9},{2,6},{6,2},{1... | collective-permute-start | bytes 393224 | tf_op jit(solution)/shard_map/ppermute | solution.py:470
  55.7 1.8 %collective-permute-start.23 = (bf16[256,256]{1,0:T(8,128)(2,1)S(1)}, bf16[256,256]{1,0:T(8,128)(2,1)S(1)}, u32[]{:S(2)}, u32[]{:S(2)}) collective-permute-start(bf16[256,256]{1,0:T(8,128)(2,1)S(1)} %get-tuple-element.69), channel_id=1, source_target_pairs={{0,8},{4,12},{8,0},{12,4},{1,9},{5,13},{9,1},{13,5},{2,10},{6,14},... | collective-permute-start | bytes 393224 | tf_op jit(solution)/shard_map/ppermute | solution.py:470
  57.5 1.7 %collective-permute-done.21 = bf16[256,256]{1,0:T(8,128)(2,1)S(1)} collective-permute-done((bf16[256,256]{1,0:T(8,128)(2,1)S(1)}, bf16[256,256]{1,0:T(8,128)(2,1)S(1)}, u32[]{:S(2)}, u32[]{:S(2)}) %collective-permute-start.21) | collective-permute-done | bytes 131104 | tf_op jit(solution)/shard_map/ppermute | solution.py:470
  60.0 1.3 %source_gradient.1 = (f32[2,512,256]{2,1,0:T(8,128)S(1)}, bf16[2,512,256]{2,1,0:T(8,128)(2,1)S(1)}) custom-call(bf16[4,512,1024]{2,1,0:T(8,128)(2,1)S(1)} %get-tuple-element.71.bar_ref, bf16[1024,256]{1,0:T(8,128)(2,1)S(1)} %get-tuple-element.72.y_ref, s32[8,128]{1,0:T(8,128)S(1)} %get-tuple-element.45.args_5_.args_6_.args_2_.meta_ref), custom_call_target="tpu_custom_call" | custom-call | tf_op jit(solution)/shard_map/source_gradient/pallas_call | solution.py:442
  62.1 3.1 %collective-permute-done.23 = bf16[256,256]{1,0:T(8,128)(2,1)S(1)} collective-permute-done((bf16[256,256]{1,0:T(8,128)(2,1)S(1)}, bf16[256,256]{1,0:T(8,128)(2,1)S(1)}, u32[]{:S(2)}, u32[]{:S(2)}) %collective-permute-start.23) | collective-permute-done | bytes 131104 | tf_op jit(solution)/shard_map/ppermute | solution.py:470
  65.3 2.7 %collective-permute-start.26 = (bf16[256,256]{1,0:T(8,128)(2,1)S(1)}, bf16[256,256]{1,0:T(8,128)(2,1)S(1)}, u32[]{:S(2)}, u32[]{:S(2)}) collective-permute-start(bf16[256,256]{1,0:T(8,128)(2,1)S(1)} %add_convert_fusion.args_0_), channel_id=1, source_target_pairs={{0,12},{4,8},{8,4},{12,0},{1,13},{5,9},{9,5},{13,1},{2,14},{6,10},... | collective-permute-start | bytes 393224 | tf_op jit(solution)/shard_map/ppermute | solution.py:470
  68.0 1.8 %collective-permute-start.24 = (bf16[256,256]{1,0:T(8,128)(2,1)S(1)}, bf16[256,256]{1,0:T(8,128)(2,1)S(1)}, u32[]{:S(2)}, u32[]{:S(2)}) collective-permute-start(bf16[256,256]{1,0:T(8,128)(2,1)S(1)} %add_convert_fusion.args_0_), channel_id=1, source_target_pairs={{0,4},{4,0},{8,12},{12,8},{1,5},{5,1},{9,13},{13,9},{2,6},{6,2},{1... | collective-permute-start | bytes 393224 | tf_op jit(solution)/shard_map/ppermute | solution.py:470
  69.9 1.1 %collective-permute-start.32 = (bf16[512,256]{1,0:T(8,128)(2,1)S(1)}, bf16[512,256]{1,0:T(8,128)(2,1)S(1)}, u32[]{:S(2)}, u32[]{:S(2)}) collective-permute-start(bf16[512,256]{1,0:T(8,128)(2,1)S(1)} %get-tuple-element.81), channel_id=1, source_target_pairs={{0,2},{2,0},{1,3},{3,1},{4,6},{6,4},{5,7},{7,5},{8,10},{10,8},{9,1... | collective-permute-start | bytes 786440 | tf_op jit(solution)/shard_map/ppermute | solution.py:470
  71.0 2.6 %collective-permute-done.26.args_3_ = bf16[256,256]{1,0:T(8,128)(2,1)S(1)} collective-permute-done((bf16[256,256]{1,0:T(8,128)(2,1)S(1)}, bf16[256,256]{1,0:T(8,128)(2,1)S(1)}, u32[]{:S(2)}, u32[]{:S(2)}) %collective-permute-start.26) | collective-permute-done | bytes 131104 | tf_op jit(solution)/shard_map/ppermute | solution.py:470
  73.6 5.3 %collective-permute-done.25.args_2_ = bf16[256,256]{1,0:T(8,128)(2,1)S(1)} collective-permute-done((bf16[256,256]{1,0:T(8,128)(2,1)S(1)}, bf16[256,256]{1,0:T(8,128)(2,1)S(1)}, u32[]{:S(2)}, u32[]{:S(2)}) %collective-permute-start.25) | collective-permute-done | bytes 131104 | tf_op jit(solution)/shard_map/ppermute | solution.py:470
  80.5 1.1 %finish.1 = (bf16[512,256]{1,0:T(8,128)(2,1)}, bf16[2048,256]{1,0:T(8,128)(2,1)}) custom-call(bf16[256,256]{1,0:T(8,128)(2,1)S(1)} %add_convert_fusion.args_0_, bf16[256,256]{1,0:T(8,128)(2,1)S(1)} %collective-permute-done.24.args_1_, bf16[256,256]{1,0:T(8,128)(2,1)S(1)} %collective-permute-done.25.args_2_, ...), custom_call_target="tpu_custom_call" | custom-call | tf_op jit(solution)/shard_map/finish/pallas_call | solution.py:630
  (53 shorter events, 16.6 us)
Async XLA Ops:
  4.6 4.3 %collective-permute-start.2 = (f32[8,1,512]{2,1,0:T(1,128)S(1)}, f32[8,1,512]{2,1,0:T(1,128)S(1)}, u32[]{:S(2)}, u32[]{:S(2)}) collective-permute-start(f32[8,1,512]{2,1,0:T(1,128)S(1)} %get-tuple-element.43.args_0_), channel_id=1, source_target_pairs={{0,3},{1,2},{2,1},{3,0},{4,7},{5,6},{6,5},{7,4},{8,11},{9,10},{10,... | collective-permute-start | bytes 49160 | tf_op jit(solution)/shard_map/ppermute | solution.py:470
  7.5 3.7 %collective-permute-start.1 = (f32[8,1,512]{2,1,0:T(1,128)S(1)}, f32[8,1,512]{2,1,0:T(1,128)S(1)}, u32[]{:S(2)}, u32[]{:S(2)}) collective-permute-start(f32[8,1,512]{2,1,0:T(1,128)S(1)} %get-tuple-element.43.args_0_), channel_id=1, source_target_pairs={{0,2},{1,3},{2,0},{3,1},{4,6},{5,7},{6,4},{7,5},{8,10},{9,11},{10,... | collective-permute-start | bytes 49160 | tf_op jit(solution)/shard_map/ppermute | solution.py:470
  8.1 3.1 %collective-permute-start = (f32[8,1,512]{2,1,0:T(1,128)S(1)}, f32[8,1,512]{2,1,0:T(1,128)S(1)}, u32[]{:S(2)}, u32[]{:S(2)}) collective-permute-start(f32[8,1,512]{2,1,0:T(1,128)S(1)} %get-tuple-element.43.args_0_), channel_id=1, source_target_pairs={{0,1},{1,0},{2,3},{3,2},{4,5},{5,4},{6,7},{7,6},{8,9},{9,8},{10,11... | collective-permute-start | bytes 49160 | tf_op jit(solution)/shard_map/ppermute | solution.py:470
  12.6 5.5 %collective-permute-start.5 = (f32[8,1,256]{2,1,0:T(1,128)S(1)}, f32[8,1,256]{2,1,0:T(1,128)S(1)}, u32[]{:S(2)}, u32[]{:S(2)}) collective-permute-start(f32[8,1,256]{2,1,0:T(1,128)S(1)} %get-tuple-element.47.args_0_), channel_id=1, source_target_pairs={{0,12},{4,8},{8,4},{12,0},{1,13},{5,9},{9,5},{13,1},{2,14},{6,10},... | collective-permute-start | bytes 24584 | tf_op jit(solution)/shard_map/ppermute | solution.py:470
  16.5 4.5 %collective-permute-start.4 = (f32[8,1,256]{2,1,0:T(1,128)S(1)}, f32[8,1,256]{2,1,0:T(1,128)S(1)}, u32[]{:S(2)}, u32[]{:S(2)}) collective-permute-start(f32[8,1,256]{2,1,0:T(1,128)S(1)} %get-tuple-element.47.args_0_), channel_id=1, source_target_pairs={{0,8},{4,12},{8,0},{12,4},{1,9},{5,13},{9,1},{13,5},{2,10},{6,14},... | collective-permute-start | bytes 24584 | tf_op jit(solution)/shard_map/ppermute | solution.py:470
  16.5 4.5 %collective-permute-start.3 = (f32[8,1,256]{2,1,0:T(1,128)S(1)}, f32[8,1,256]{2,1,0:T(1,128)S(1)}, u32[]{:S(2)}, u32[]{:S(2)}) collective-permute-start(f32[8,1,256]{2,1,0:T(1,128)S(1)} %get-tuple-element.47.args_0_), channel_id=1, source_target_pairs={{0,4},{4,0},{8,12},{12,8},{1,5},{5,1},{9,13},{13,9},{2,6},{6,2},{1... | collective-permute-start | bytes 24584 | tf_op jit(solution)/shard_map/ppermute | solution.py:470
  21.9 3.1 %collective-permute-start.8 = (f32[4,1,512]{2,1,0:T(1,128)S(1)}, f32[4,1,512]{2,1,0:T(1,128)S(1)}, u32[]{:S(2)}, u32[]{:S(2)}) collective-permute-start(f32[4,1,512]{2,1,0:T(1,128)S(1)} %get-tuple-element.49.args_0_), channel_id=1, source_target_pairs={{0,3},{1,2},{2,1},{3,0},{4,7},{5,6},{6,5},{7,4},{8,11},{9,10},{10,... | collective-permute-start | bytes 24584 | tf_op jit(solution)/shard_map/ppermute | solution.py:470
  21.9 3.7 %collective-permute-start.7 = (f32[4,1,512]{2,1,0:T(1,128)S(1)}, f32[4,1,512]{2,1,0:T(1,128)S(1)}, u32[]{:S(2)}, u32[]{:S(2)}) collective-permute-start(f32[4,1,512]{2,1,0:T(1,128)S(1)} %get-tuple-element.49.args_0_), channel_id=1, source_target_pairs={{0,2},{1,3},{2,0},{3,1},{4,6},{5,7},{6,4},{7,5},{8,10},{9,11},{10,... | collective-permute-start | bytes 24584 | tf_op jit(solution)/shard_map/ppermute | solution.py:470
  22.4 3.3 %collective-permute-start.6 = (f32[4,1,512]{2,1,0:T(1,128)S(1)}, f32[4,1,512]{2,1,0:T(1,128)S(1)}, u32[]{:S(2)}, u32[]{:S(2)}) collective-permute-start(f32[4,1,512]{2,1,0:T(1,128)S(1)} %get-tuple-element.49.args_0_), channel_id=1, source_target_pairs={{0,1},{1,0},{2,3},{3,2},{4,5},{5,4},{6,7},{7,6},{8,9},{9,8},{10,11... | collective-permute-start | bytes 24584 | tf_op jit(solution)/shard_map/ppermute | solution.py:470
  26.4 5.5 %collective-permute-start.11 = (f32[4,1,256]{2,1,0:T(1,128)S(1)}, f32[4,1,256]{2,1,0:T(1,128)S(1)}, u32[]{:S(2)}, u32[]{:S(2)}) collective-permute-start(f32[4,1,256]{2,1,0:T(1,128)S(1)} %get-tuple-element.52.args_0_), channel_id=1, source_target_pairs={{0,12},{4,8},{8,4},{12,0},{1,13},{5,9},{9,5},{13,1},{2,14},{6,10},... | collective-permute-start | bytes 12296 | tf_op jit(solution)/shard_map/ppermute | solution.py:470
  28.2 4.5 %collective-permute-start.10 = (f32[4,1,256]{2,1,0:T(1,128)S(1)}, f32[4,1,256]{2,1,0:T(1,128)S(1)}, u32[]{:S(2)}, u32[]{:S(2)}) collective-permute-start(f32[4,1,256]{2,1,0:T(1,128)S(1)} %get-tuple-element.52.args_0_), channel_id=1, source_target_pairs={{0,8},{4,12},{8,0},{12,4},{1,9},{5,13},{9,1},{13,5},{2,10},{6,14},... | collective-permute-start | bytes 12296 | tf_op jit(solution)/shard_map/ppermute | solution.py:470
  28.9 3.9 %collective-permute-start.9 = (f32[4,1,256]{2,1,0:T(1,128)S(1)}, f32[4,1,256]{2,1,0:T(1,128)S(1)}, u32[]{:S(2)}, u32[]{:S(2)}) collective-permute-start(f32[4,1,256]{2,1,0:T(1,128)S(1)} %get-tuple-element.52.args_0_), channel_id=1, source_target_pairs={{0,4},{4,0},{8,12},{12,8},{1,5},{5,1},{9,13},{13,9},{2,6},{6,2},{1... | collective-permute-start | bytes 12296 | tf_op jit(solution)/shard_map/ppermute | solution.py:470
  33.6 3.1 %collective-permute-start.14 = (f32[4,1,512]{2,1,0:T(1,128)S(1)}, f32[4,1,512]{2,1,0:T(1,128)S(1)}, u32[]{:S(2)}, u32[]{:S(2)}) collective-permute-start(f32[4,1,512]{2,1,0:T(1,128)S(1)} %get-tuple-element.53.args_0_), channel_id=1, source_target_pairs={{0,3},{1,2},{2,1},{3,0},{4,7},{5,6},{6,5},{7,4},{8,11},{9,10},{10,... | collective-permute-start | bytes 24584 | tf_op jit(solution)/shard_map/ppermute | solution.py:470
  33.7 3.7 %collective-permute-start.13 = (f32[4,1,512]{2,1,0:T(1,128)S(1)}, f32[4,1,512]{2,1,0:T(1,128)S(1)}, u32[]{:S(2)}, u32[]{:S(2)}) collective-permute-start(f32[4,1,512]{2,1,0:T(1,128)S(1)} %get-tuple-element.53.args_0_), channel_id=1, source_target_pairs={{0,2},{1,3},{2,0},{3,1},{4,6},{5,7},{6,4},{7,5},{8,10},{9,11},{10,... | collective-permute-start | bytes 24584 | tf_op jit(solution)/shard_map/ppermute | solution.py:470
  34.1 3.3 %collective-permute-start.12 = (f32[4,1,512]{2,1,0:T(1,128)S(1)}, f32[4,1,512]{2,1,0:T(1,128)S(1)}, u32[]{:S(2)}, u32[]{:S(2)}) collective-permute-start(f32[4,1,512]{2,1,0:T(1,128)S(1)} %get-tuple-element.53.args_0_), channel_id=1, source_target_pairs={{0,1},{1,0},{2,3},{3,2},{4,5},{5,4},{6,7},{7,6},{8,9},{9,8},{10,11... | collective-permute-start | bytes 24584 | tf_op jit(solution)/shard_map/ppermute | solution.py:470
  38.2 5.5 %collective-permute-start.17 = (f32[4,1,256]{2,1,0:T(1,128)S(1)}, f32[4,1,256]{2,1,0:T(1,128)S(1)}, u32[]{:S(2)}, u32[]{:S(2)}) collective-permute-start(f32[4,1,256]{2,1,0:T(1,128)S(1)} %get-tuple-element.57.args_0_), channel_id=1, source_target_pairs={{0,12},{4,8},{8,4},{12,0},{1,13},{5,9},{9,5},{13,1},{2,14},{6,10},... | collective-permute-start | bytes 12296 | tf_op jit(solution)/shard_map/ppermute | solution.py:470
  41.1 4.5 %collective-permute-start.16 = (f32[4,1,256]{2,1,0:T(1,128)S(1)}, f32[4,1,256]{2,1,0:T(1,128)S(1)}, u32[]{:S(2)}, u32[]{:S(2)}) collective-permute-start(f32[4,1,256]{2,1,0:T(1,128)S(1)} %get-tuple-element.57.args_0_), channel_id=1, source_target_pairs={{0,8},{4,12},{8,0},{12,4},{1,9},{5,13},{9,1},{13,5},{2,10},{6,14},... | collective-permute-start | bytes 12296 | tf_op jit(solution)/shard_map/ppermute | solution.py:470
  41.5 4.1 %collective-permute-start.15 = (f32[4,1,256]{2,1,0:T(1,128)S(1)}, f32[4,1,256]{2,1,0:T(1,128)S(1)}, u32[]{:S(2)}, u32[]{:S(2)}) collective-permute-start(f32[4,1,256]{2,1,0:T(1,128)S(1)} %get-tuple-element.57.args_0_), channel_id=1, source_target_pairs={{0,4},{4,0},{8,12},{12,8},{1,5},{5,1},{9,13},{13,9},{2,6},{6,2},{1... | collective-permute-start | bytes 12296 | tf_op jit(solution)/shard_map/ppermute | solution.py:470
  46.4 3.1 %collective-permute-start.20 = (f32[4,1,512]{2,1,0:T(1,128)S(1)}, f32[4,1,512]{2,1,0:T(1,128)S(1)}, u32[]{:S(2)}, u32[]{:S(2)}) collective-permute-start(f32[4,1,512]{2,1,0:T(1,128)S(1)} %get-tuple-element.60.args_0_), channel_id=1, source_target_pairs={{0,3},{1,2},{2,1},{3,0},{4,7},{5,6},{6,5},{7,4},{8,11},{9,10},{10,... | collective-permute-start | bytes 24584 | tf_op jit(solution)/shard_map/ppermute | solution.py:470
  46.5 3.7 %collective-permute-start.19 = (f32[4,1,512]{2,1,0:T(1,128)S(1)}, f32[4,1,512]{2,1,0:T(1,128)S(1)}, u32[]{:S(2)}, u32[]{:S(2)}) collective-permute-start(f32[4,1,512]{2,1,0:T(1,128)S(1)} %get-tuple-element.60.args_0_), channel_id=1, source_target_pairs={{0,2},{1,3},{2,0},{3,1},{4,6},{5,7},{6,4},{7,5},{8,10},{9,11},{10,... | collective-permute-start | bytes 24584 | tf_op jit(solution)/shard_map/ppermute | solution.py:470
  46.8 3.4 %collective-permute-start.18 = (f32[4,1,512]{2,1,0:T(1,128)S(1)}, f32[4,1,512]{2,1,0:T(1,128)S(1)}, u32[]{:S(2)}, u32[]{:S(2)}) collective-permute-start(f32[4,1,512]{2,1,0:T(1,128)S(1)} %get-tuple-element.60.args_0_), channel_id=1, source_target_pairs={{0,1},{1,0},{2,3},{3,2},{4,5},{5,4},{6,7},{7,6},{8,9},{9,8},{10,11... | collective-permute-start | bytes 24584 | tf_op jit(solution)/shard_map/ppermute | solution.py:470
  51.2 8.0 %collective-permute-start.21 = (bf16[256,256]{1,0:T(8,128)(2,1)S(1)}, bf16[256,256]{1,0:T(8,128)(2,1)S(1)}, u32[]{:S(2)}, u32[]{:S(2)}) collective-permute-start(bf16[256,256]{1,0:T(8,128)(2,1)S(1)} %get-tuple-element.65), channel_id=1, source_target_pairs={{0,12},{4,8},{8,4},{12,0},{1,13},{5,9},{9,5},{13,1},{2,14},{6,10},... | collective-permute-start | bytes 393224 | tf_op jit(solution)/shard_map/ppermute | solution.py:470
  53.8 8.3 %collective-permute-start.22 = (bf16[256,256]{1,0:T(8,128)(2,1)S(1)}, bf16[256,256]{1,0:T(8,128)(2,1)S(1)}, u32[]{:S(2)}, u32[]{:S(2)}) collective-permute-start(bf16[256,256]{1,0:T(8,128)(2,1)S(1)} %get-tuple-element.68), channel_id=1, source_target_pairs={{0,4},{4,0},{8,12},{12,8},{1,5},{5,1},{9,13},{13,9},{2,6},{6,2},{1... | collective-permute-start | bytes 393224 | tf_op jit(solution)/shard_map/ppermute | solution.py:470
  55.7 9.5 %collective-permute-start.23 = (bf16[256,256]{1,0:T(8,128)(2,1)S(1)}, bf16[256,256]{1,0:T(8,128)(2,1)S(1)}, u32[]{:S(2)}, u32[]{:S(2)}) collective-permute-start(bf16[256,256]{1,0:T(8,128)(2,1)S(1)} %get-tuple-element.69), channel_id=1, source_target_pairs={{0,8},{4,12},{8,0},{12,4},{1,9},{5,13},{9,1},{13,5},{2,10},{6,14},... | collective-permute-start | bytes 393224 | tf_op jit(solution)/shard_map/ppermute | solution.py:470
  65.2 4.5 %collective-permute-start.31 = (bf16[2,512,256]{2,1,0:T(8,128)(2,1)S(1)}, bf16[2,512,256]{2,1,0:T(8,128)(2,1)S(1)}, u32[]{:S(2)}, u32[]{:S(2)}) collective-permute-start(bf16[2,512,256]{2,1,0:T(8,128)(2,1)S(1)} %get-tuple-element.79), channel_id=1, source_target_pairs={{0,1},{1,0},{2,3},{3,2},{4,5},{5,4},{6,7},{7,6},{8,9},{9,8},{10,11... | collective-permute-start | bytes 1572872 | tf_op jit(solution)/shard_map/ppermute | solution.py:470
  65.3 8.3 %collective-permute-start.26 = (bf16[256,256]{1,0:T(8,128)(2,1)S(1)}, bf16[256,256]{1,0:T(8,128)(2,1)S(1)}, u32[]{:S(2)}, u32[]{:S(2)}) collective-permute-start(bf16[256,256]{1,0:T(8,128)(2,1)S(1)} %add_convert_fusion.args_0_), channel_id=1, source_target_pairs={{0,12},{4,8},{8,4},{12,0},{1,13},{5,9},{9,5},{13,1},{2,14},{6,10},... | collective-permute-start | bytes 393224 | tf_op jit(solution)/shard_map/ppermute | solution.py:470
  68.0 11.0 %collective-permute-start.25 = (bf16[256,256]{1,0:T(8,128)(2,1)S(1)}, bf16[256,256]{1,0:T(8,128)(2,1)S(1)}, u32[]{:S(2)}, u32[]{:S(2)}) collective-permute-start(bf16[256,256]{1,0:T(8,128)(2,1)S(1)} %add_convert_fusion.args_0_), channel_id=1, source_target_pairs={{0,8},{4,12},{8,0},{12,4},{1,9},{5,13},{9,1},{13,5},{2,10},{6,14},... | collective-permute-start | bytes 393224 | tf_op jit(solution)/shard_map/ppermute | solution.py:470
  68.0 11.0 %collective-permute-start.24 = (bf16[256,256]{1,0:T(8,128)(2,1)S(1)}, bf16[256,256]{1,0:T(8,128)(2,1)S(1)}, u32[]{:S(2)}, u32[]{:S(2)}) collective-permute-start(bf16[256,256]{1,0:T(8,128)(2,1)S(1)} %add_convert_fusion.args_0_), channel_id=1, source_target_pairs={{0,4},{4,0},{8,12},{12,8},{1,5},{5,1},{9,13},{13,9},{2,6},{6,2},{1... | collective-permute-start | bytes 393224 | tf_op jit(solution)/shard_map/ppermute | solution.py:470
  69.9 10.6 %collective-permute-start.32 = (bf16[512,256]{1,0:T(8,128)(2,1)S(1)}, bf16[512,256]{1,0:T(8,128)(2,1)S(1)}, u32[]{:S(2)}, u32[]{:S(2)}) collective-permute-start(bf16[512,256]{1,0:T(8,128)(2,1)S(1)} %get-tuple-element.81), channel_id=1, source_target_pairs={{0,2},{2,0},{1,3},{3,1},{4,6},{6,4},{5,7},{7,5},{8,10},{10,8},{9,1... | collective-permute-start | bytes 786440 | tf_op jit(solution)/shard_map/ppermute | solution.py:470
  71.0 8.4 %collective-permute-start.27 = (bf16[256,256]{1,0:T(8,128)(2,1)S(1)}, bf16[256,256]{1,0:T(8,128)(2,1)S(1)}, u32[]{:S(2)}, u32[]{:S(2)}) collective-permute-start(bf16[256,256]{1,0:T(8,128)(2,1)S(1)} %add_convert_fusion.args_0_), channel_id=1, source_target_pairs={{0,1},{1,0},{2,3},{3,2},{4,5},{5,4},{6,7},{7,6},{8,9},{9,8},{10,11... | collective-permute-start | bytes 393224 | tf_op jit(solution)/shard_map/ppermute | solution.py:470
  73.6 5.8 %collective-permute-start.30 = (bf16[256,256]{1,0:T(8,128)(2,1)S(1)}, bf16[256,256]{1,0:T(8,128)(2,1)S(1)}, u32[]{:S(2)}, u32[]{:S(2)}) collective-permute-start(bf16[256,256]{1,0:T(8,128)(2,1)S(1)} %collective-permute-done.26.args_3_), channel_id=1, source_target_pairs={{0,1},{1,0},{2,3},{3,2},{4,5},{5,4},{6,7},{7,6},{8,9},{9,8},{10,11... | collective-permute-start | bytes 393224 | tf_op jit(solution)/shard_map/ppermute | solution.py:470
  79.0 1.5 %collective-permute-start.28 = (bf16[256,256]{1,0:T(8,128)(2,1)S(1)}, bf16[256,256]{1,0:T(8,128)(2,1)S(1)}, u32[]{:S(2)}, u32[]{:S(2)}) collective-permute-start(bf16[256,256]{1,0:T(8,128)(2,1)S(1)} %collective-permute-done.24.args_1_), channel_id=1, source_target_pairs={{0,1},{1,0},{2,3},{3,2},{4,5},{5,4},{6,7},{7,6},{8,9},{9,8},{10,11... | collective-permute-start | bytes 393224 | tf_op jit(solution)/shard_map/ppermute | solution.py:470
  (3 other events, 13.1 us)

commit v4 on v2

v4 whole, which is shorter than its diff:
```python
import functools
import math

import jax
import jax.numpy as jnp
from jax import lax
from jax.experimental import pallas as pl
from jax.experimental.pallas import tpu as pltpu
from jax.sharding import PartitionSpec as P

TILE = 512
HALF = 256
BLOCK = 4
LANES = 128
ROWS = 64
LIMIT = 24 * 1024 * 1024
LOWEST = -1e30
F32 = jnp.float32
NT_DIMS = (((1,), (1,)), ((), ()))
NN_DIMS = (((1,), (0,)), ((), ()))
TN_DIMS = (((0,), (0,)), ((), ()))


def kept_targets(meta, s):
    first_cut, second_cut, straight = meta
    is_low = (s < first_cut).astype(jnp.int32) == straight
    return jnp.where(is_low, 0, second_cut), jnp.where(is_low, second_cut, BLOCK)


def kept_sources(meta, t):
    first_cut, second_cut, straight = meta
    is_low = (t < second_cut).astype(jnp.int32) == straight
    return jnp.where(is_low, 0, first_cut), jnp.where(is_low, first_cut, BLOCK)


def tile_lanes(t):
    return pl.ds(pl.multiple_of(t * HALF, HALF), HALF)


def read_meta(meta_ref):
    return meta_ref[0, 0], meta_ref[0, 1], meta_ref[0, 2]


def to_column(row):
    return jnp.broadcast_to(row, (LANES, row.shape[1])).T


def lane_sums(values):
    return jnp.sum(values.T, axis=0, keepdims=True)


def total(refs, index):
    value = refs[0][index]
    for ref in refs[1:]:
        value = value + ref[index]
    return value


def tile_biases(meta, s):
    low, high = kept_targets(meta, s)
    return [jnp.where((low <= t) & (t < high), 0.0, LOWEST) for t in range(BLOCK)]


def lane_groups():
    return [(i // 2, slice(i * LANES, (i + 1) * LANES)) for i in range(2 * BLOCK)]


def half_of(i):
    return slice((i % 2) * LANES, (i % 2 + 1) * LANES)


def weighted_rows(e_ref, vector_ref, out_ref):
    for s in range(BLOCK):
        for at in range(0, TILE, LANES):
            acc = None
            for i, (t, lanes) in enumerate(lane_groups()):
                term = e_ref[s, at : at + LANES, lanes] * vector_ref[t, :, half_of(i)]
                acc = term if acc is None else acc + term
            out_ref[s, :, at : at + LANES] = lane_sums(acc)


def eight_rows(values, reduce):
    return reduce(values.reshape(-1, 8, LANES), axis=0)


def weighted_columns(e_ref, column_ref, scale_ref, out_ref):
    acc = [None] * (2 * BLOCK)
    for s in range(BLOCK):
        for at in range(0, TILE, LANES):
            u = column_ref[s, at : at + LANES, :]
            for i, (t, lanes) in enumerate(lane_groups()):
                term = eight_rows(e_ref[s, at : at + LANES, lanes] * u, jnp.sum)
                acc[i] = term if acc[i] is None else acc[i] + term
    for i, (t, lanes) in enumerate(lane_groups()):
        half = half_of(i)
        out_ref[t, :, half] = scale_ref[t, :, half] * jnp.sum(acc[i], axis=0, keepdims=True)


def first_source_kernel(
    x_hbm,
    y_hbm,
    warm_hbm,
    sb_hbm,
    tb_hbm,
    kp_hbm,
    score_ref,
    out_ref,
    meta_ref,
    x_ref,
    y_ref,
    warm_ref,
    sb_ref,
    tb_ref,
    kp_ref,
    sems,
    bound_sems,
):
    row_pos = lax.axis_index("row")
    col_pos = lax.axis_index("col")
    rep_pos = lax.axis_index("rep")
    bounds = [
        pltpu.make_async_copy(source, target, bound_sems.at[i])
        for i, (source, target) in enumerate(
            ((sb_hbm, sb_ref), (tb_hbm, tb_ref), (kp_hbm, kp_ref))
        )
    ]
    y_copy = pltpu.make_async_copy(y_hbm.at[:, rep_pos], y_ref, sems.at[0])
    x_copy = pltpu.make_async_copy(x_hbm.at[:1], x_ref.at[:1], sems.at[1])
    rest_copy = pltpu.make_async_copy(x_hbm.at[1:], x_ref.at[1:], sems.at[2])
    warm_copy = pltpu.make_async_copy(warm_hbm.at[:, rep_pos], warm_ref, sems.at[3])
    copies = [y_copy, x_copy, *bounds, warm_copy, rest_copy]
    for copy in copies:
        copy.start()
    for copy in bounds:
        copy.wait()
    first_cut = sb_ref[2 * row_pos + 1] - BLOCK * row_pos
    second_cut = tb_ref[2 * col_pos + 1] - BLOCK * col_pos

    def look(i, found):
        here = (kp_ref[0, i] == 2 * row_pos) & (kp_ref[1, i] == 2 * col_pos)
        return found | here.astype(jnp.int32)

    straight = lax.fori_loop(0, kp_ref.shape[1], look, jnp.int32(0))
    lanes = lax.broadcasted_iota(jnp.int32, meta_ref.shape, 1)
    meta_ref[...] = jnp.where(lanes == 0, first_cut, jnp.where(lanes == 1, second_cut, straight))
    meta = (first_cut, second_cut, straight)
    width = x_ref.shape[2]
    scale = width ** (-0.5) * math.log2(math.e)

    def scores(s):
        score_ref[s] = scale * lax.dot_general(
            x_ref[s],
            y_ref[...].reshape(BLOCK * HALF, width),
            NT_DIMS,
            preferred_element_type=F32,
        )

    def passes(s):
        biases = tile_biases(meta, s)
        warm = [
            warm_ref[t, :, half_of(i)] * math.log2(math.e) + biases[t]
            for i, (t, _) in enumerate(lane_groups())
        ]
        for at in range(0, TILE, LANES):
            largest = None
            for i, (_, lanes) in enumerate(lane_groups()):
                term = score_ref[s, at : at + LANES, lanes] + warm[i]
                largest = term if largest is None else jnp.maximum(largest, term)
            largest = jnp.max(largest, axis=1, keepdims=True)
            largest = jnp.broadcast_to(largest, (LANES, LANES))
            acc = None
            for i, (_, lanes) in enumerate(lane_groups()):
                term = jnp.exp2(score_ref[s, at : at + LANES, lanes] + warm[i] - largest)
                acc = term if acc is None else acc + term
            out_ref[s, :, at : at + LANES] = largest.T[:1]
            out_ref[BLOCK + s, :, at : at + LANES] = lane_sums(acc)

    y_copy.wait()
    x_copy.wait()
    scores(0)
    warm_copy.wait()
    rest_copy.wait()
    for s in range(BLOCK):
        if s + 1 < BLOCK:
            scores(s + 1)
        passes(s)


def combine(refs, at, offset):
    largest = refs[0][at]
    for ref in refs[1:]:
        largest = jnp.maximum(largest, ref[at])
    sums = refs[0][offset + at] * jnp.exp2(refs[0][at] - largest)
    for ref in refs[1:]:
        sums = sums + ref[offset + at] * jnp.exp2(ref[at] - largest)
    return -(largest + jnp.log2(sums))


def first_target_kernel(count, *args):
    parts = args[:count]
    score_ref, meta_ref, e_ref, out_ref, column_ref = args[count:]
    meta = read_meta(meta_ref)
    biases = [tile_biases(meta, s) for s in range(BLOCK)]
    largest = [None] * (2 * BLOCK)
    for s in range(BLOCK):
        column_ref[s] = to_column(combine(parts, s, BLOCK))
        here = [None] * (2 * BLOCK)
        for at in range(0, TILE, LANES):
            u = column_ref[s, at : at + LANES, :]
            for i, (t, lanes) in enumerate(lane_groups()):
                term = eight_rows(score_ref[s, at : at + LANES, lanes] + u, jnp.max)
                here[i] = term if here[i] is None else jnp.maximum(here[i], term)
        for i, (t, _) in enumerate(lane_groups()):
            term = here[i] + biases[s][t]
            largest[i] = term if s == 0 else jnp.maximum(largest[i], term)
    sums = [None] * (2 * BLOCK)
    for i, (t, _) in enumerate(lane_groups()):
        largest[i] = jnp.max(largest[i], axis=0, keepdims=True)
        out_ref[t, :, half_of(i)] = largest[i]
    for s in range(BLOCK):
        shifts = [largest[i] - biases[s][t] for i, (t, _) in enumerate(lane_groups())]
        for at in range(0, TILE, LANES):
            u = column_ref[s, at : at + LANES, :]
            for i, (t, lanes) in enumerate(lane_groups()):
                e = jnp.exp2(score_ref[s, at : at + LANES, lanes] + u - shifts[i])
                e_ref[s, at : at + LANES, lanes] = e
                term = eight_rows(e, jnp.sum)
                sums[i] = term if sums[i] is None else sums[i] + term
    for i, (t, _) in enumerate(lane_groups()):
        out_ref[BLOCK + t, :, half_of(i)] = jnp.sum(sums[i], axis=0, keepdims=True)


def second_source_kernel(count, *args):
    parts = args[:count]
    warm_ref, e_ref, out_ref, q_ref, wq_ref = args[count:]
    for t in range(BLOCK):
        potential = combine(parts, t, BLOCK)
        q = jnp.exp2(parts[0][t] + potential)
        q_ref[t] = q
        wq_ref[t] = q * jnp.exp2(warm_ref[t] * math.log2(math.e) - potential)
    weighted_rows(e_ref, q_ref, out_ref)


def second_target_kernel(count, *args):
    parts = args[:count]
    e_ref, q_ref, out_ref, a_ref, column_ref = args[count:]
    for s in range(BLOCK):
        a = 1.0 / total(parts, s)
        a_ref[s] = a
        column_ref[s] = to_column(a)
    weighted_columns(e_ref, column_ref, q_ref, out_ref)


def late_kernel(count, *args):
    parts = args[:count]
    e_ref, q_ref, weight_ref, out_ref, p_ref = args[count:]
    rep_pos = lax.axis_index("rep")
    for t in range(BLOCK):
        p_ref[t] = weight_ref[2 * t + rep_pos] * q_ref[t] / total(parts, t)
    weighted_rows(e_ref, p_ref, out_ref)


def mid_kernel(count, *args):
    parts = args[:count]
    e_ref, q_ref, a_ref, weight_ref, out_ref, column_ref = args[count:]
    for s in range(BLOCK):
        a = a_ref[s]
        column_ref[s] = to_column(a * (weight_ref[s] - a * total(parts, s)))
    weighted_columns(e_ref, column_ref, q_ref, out_ref)


def early_kernel(count, *args):
    parts = args[:count]
    e_ref, q_ref, out_ref, h_ref = args[count:]
    for t in range(BLOCK):
        h_ref[t] = -q_ref[t] * total(parts, t)
    weighted_rows(e_ref, h_ref, out_ref)


def target_gradient_kernel(part, count, *args):
    if count:
        parts = args[:count]
        x_ref, e_ref, a_ref, b_ref, p_ref, q_ref, h_ref, wq_ref = args[count : count + 8]
        bar_ref, early_ref, *out_refs = args[count + 8 :]
        for s in range(BLOCK):
            early_ref[s] = to_column(-total(parts, s))
    else:
        x_ref, e_ref, a_ref, b_ref, p_ref, q_ref, h_ref, wq_ref = args[:8]
        early_ref, _, bar_ref, *out_refs = args[8:]
    row_pos = lax.axis_index("row")
    per_tile = len(out_refs)
    t = (row_pos // per_tile) ^ part
    p, q, h, wq = p_ref[t], q_ref[t], h_ref[t], wq_ref[t]
    width = x_ref.shape[2]
    result = None
    for s in range(BLOCK):
        bars = []
        for at in range(0, TILE, ROWS):
            e = e_ref[s, at : at + ROWS, tile_lanes(t)]
            a = a_ref[s, at : at + ROWS, :]
            b = b_ref[s, at : at + ROWS, :]
            early = early_ref[s, at : at + ROWS, :]
            sides = []
            for side in (slice(0, LANES), slice(LANES, HALF)):
                factor = a * p[:, side] + b * q[:, side] + (h[:, side] + early * wq[:, side])
                sides.append((e[:, side] * factor).astype(jnp.bfloat16))
            bars.append(jnp.concatenate(sides, axis=1))
        bar = jnp.concatenate(bars, axis=0)
        bar_ref[s, :, tile_lanes(t)] = bar
        term = lax.dot_general(bar, x_ref[s], TN_DIMS, preferred_element_type=F32)
        result = term if result is None else result + term
    result = -(width ** (-0.5)) * result
    if per_tile == 1:
        out_refs[0][...] = result.astype(out_refs[0].dtype)
        return
    piece = HALF // per_tile
    for i, ref in enumerate(out_refs):
        for j in range(per_tile):

            @pl.when(((row_pos % per_tile) ^ i) == j)
            def _():
                ref[...] = result[j * piece : (j + 1) * piece, :].astype(ref.dtype)


def source_gradient_kernel(bar_ref, y_ref, near_ref, far_ref, acc_ref):
    width = y_ref.shape[2]
    col_pos = lax.axis_index("col")
    rep_pos = lax.axis_index("rep")
    y = y_ref[...].reshape(BLOCK * HALF, width)
    for s in range(BLOCK):
        acc_ref[s * TILE : (s + 1) * TILE, :] = -(width ** (-0.5)) * lax.dot_general(
            bar_ref[s], y, NN_DIMS, preferred_element_type=F32
        )
    piece = near_ref.shape[1]
    for d in range(near_ref.shape[0]):
        at = 2 * (col_pos ^ d)
        for ref, rep in ((near_ref, rep_pos), (far_ref, 1 - rep_pos)):
            begin = pl.multiple_of((at + rep) * piece, piece)
            ref[d] = acc_ref[pl.ds(begin, piece), :].astype(ref.dtype)


def merge_kernel(near_ref, far_ref, *out_refs):
    for d, ref in enumerate(out_refs):
        ref[...] = (near_ref[d] + far_ref[d].astype(F32)).astype(ref.dtype)


def finish_kernel(ranks, count, *args):
    pieces, args = args[: len(ranks)], args[len(ranks) :]
    terms, args = args[:count], args[count:]
    if terms:
        source_out, target_out, sum_ref, sems = args
    else:
        _, target_out, sems = args
    rep_pos = lax.axis_index("rep")
    row_pos = lax.axis_index("row")
    piece = pieces[0].shape[0]
    per_tile = HALF // piece
    copies = []
    for i, ((k, crossed), ref) in enumerate(zip(ranks, pieces)):
        at = row_pos ^ k
        rep = 1 - rep_pos if crossed else rep_pos
        begin = (at // per_tile) * TILE + rep * HALF + (at % per_tile) * piece
        begin = pl.multiple_of(begin, piece)
        copies.append(
            pltpu.make_async_copy(ref, target_out.at[pl.ds(begin, piece)], sems.at[i])
        )
    for copy in copies:
        copy.start()
    if terms:
        value = terms[0][...]
        for term in terms[1:]:
            value = value + term[...].astype(F32)
        sum_ref[...] = value.astype(sum_ref.dtype)
        copies.append(pltpu.make_async_copy(sum_ref, source_out, sems.at[len(ranks)]))
        copies[-1].start()
    for copy in copies:
        copy.wait()


def call(kernel, name, outs, scratch, args, spaces=None, aliases=None, cost=None):
    spaces = spaces or [pltpu.VMEM] * len(args)
    args = [
        pltpu.with_memory_space_constraint(value, space)
        for value, space in zip(args, spaces)
    ]
    return pl.pallas_call(
        kernel,
        name=name,
        out_shape=[pltpu.VMEM(shape, dtype) for shape, dtype in outs],
        in_specs=[pl.BlockSpec(memory_space=space) for space in spaces],
        out_specs=[pl.BlockSpec(memory_space=pltpu.VMEM) for _ in outs],
        scratch_shapes=scratch,
        input_output_aliases=aliases or {},
        cost_estimate=cost,
        compiler_params=pltpu.CompilerParams(vmem_limit_bytes=LIMIT),
    )(*args)


def shards(
    sizes,
    source_emb,
    target_emb,
    warm_start,
    source_weight,
    target_weight,
    source_bounds,
    target_bounds,
    kept_pairs,
):
    width = source_emb.shape[1]

    def swap(value, axes, k):
        count = math.prod(sizes[axis] for axis in axes)
        return lax.ppermute(value, axes, [(i, i ^ k) for i in range(count)])

    def spread(value, axes):
        count = math.prod(sizes[axis] for axis in axes)
        return [value] + [swap(value, axes, k) for k in range(1, count)]

    bf16 = jnp.bfloat16
    over_source = ("col", "rep")
    over_target = ("row",)
    target_weight = target_weight.reshape(2 * BLOCK, 1, HALF)
    source_weight = source_weight.reshape(BLOCK, 1, TILE)
    source_vector = ((BLOCK, 1, TILE), F32)
    target_vector = ((BLOCK, 1, HALF), F32)
    matrix = (BLOCK, TILE, BLOCK * HALF)
    columns = (BLOCK, TILE, LANES)
    hbm = pltpu.HBM

    score, packed, meta, x, y, warm = call(
        first_source_kernel,
        "first_source",
        [
            (matrix, F32),
            ((2 * BLOCK, 1, TILE), F32),
            ((8, LANES), jnp.int32),
            ((BLOCK, TILE, width), bf16),
            ((BLOCK, HALF, width), bf16),
            target_vector,
        ],
        [
            pltpu.SMEM(source_bounds.shape, jnp.int32),
            pltpu.SMEM(target_bounds.shape, jnp.int32),
            pltpu.SMEM(kept_pairs.shape[::-1], jnp.int32),
            pltpu.SemaphoreType.DMA((4,)),
            pltpu.SemaphoreType.DMA((3,)),
        ],
        [
            source_emb.reshape(BLOCK, TILE, width),
            target_emb.reshape(BLOCK, 2, HALF, width),
            warm_start.reshape(BLOCK, 2, 1, HALF),
            source_bounds,
            target_bounds,
            kept_pairs.T,
        ],
        [hbm] * 6,
    )
    parts = spread(packed, over_source)
    n_source = len(parts)
    e, packed = call(
        functools.partial(first_target_kernel, n_source),
        "first_target",
        [(matrix, F32), ((2 * BLOCK, 1, HALF), F32)],
        [pltpu.VMEM(columns, F32)],
        [*parts, score, meta],
    )
    parts = spread(packed, over_target)
    n_target = len(parts)
    sums, q, wq = call(
        functools.partial(second_source_kernel, n_target),
        "second_source",
        [source_vector, target_vector, target_vector],
        [],
        [*parts, warm, e],
    )
    parts = spread(sums, over_source)
    sums, a, a_column = call(
        functools.partial(second_target_kernel, n_source),
        "second_target",
        [target_vector, source_vector, (columns, F32)],
        [],
        [*parts, e, q],
    )
    parts = spread(sums, over_target)
    sums, p = call(
        functools.partial(late_kernel, n_target),
        "late",
        [source_vector, target_vector],
        [],
        [*parts, e, q, target_weight],
    )
    parts = spread(sums, over_source)
    sums, b_column = call(
        functools.partial(mid_kernel, n_source),
        "mid",
        [target_vector, (columns, F32)],
        [],
        [*parts, e, q, a, source_weight],
    )
    parts = spread(sums, over_target)
    sums, h = call(
        functools.partial(early_kernel, n_target),
        "early",
        [source_vector, target_vector],
        [],
        [*parts, e, q],
    )
    parts = spread(sums, over_source)

    rows = sizes["row"]
    per_tile = rows // BLOCK
    piece = HALF // per_tile
    shared = [x, e, a_column, b_column, p, q, h, wq]
    pieces = [None] * rows
    arrived = [None] * rows
    bar = early = None
    for part in (3, 2, 1, 0):
        outs = [((piece, width), bf16 if part or i else F32) for i in range(per_tile)]
        if bar is None:
            bar, early, *results = call(
                functools.partial(target_gradient_kernel, part, n_source),
                f"target_gradient_{part}",
                [(matrix, bf16), (columns, F32)] + outs,
                [],
                [*parts, *shared],
            )
        else:
            if part == 0:
                first = slice((3, 2, 1, 0)[0] * per_tile, ((3, 2, 1, 0)[0] + 1) * per_tile)
                bar, arrived[first] = lax.optimization_barrier((bar, arrived[first]))
            bar, *results = call(
                functools.partial(target_gradient_kernel, part, 0),
                f"target_gradient_{part}",
                [(matrix, bf16)] + outs,
                [],
                [*shared, early, bar],
                aliases={len(shared) + 1: 0},
            )
        for i, value in enumerate(results):
            k = part * per_tile + i
            pieces[k] = value
            arrived[k] = swap(value, over_target, k) if k else value
    source_piece = BLOCK * TILE // n_source
    columns_of_chips = sizes["col"]
    halves = (columns_of_chips, source_piece, width)
    near, far = call(
        source_gradient_kernel,
        "source_gradient",
        [(halves, F32), (halves, bf16)],
        [pltpu.VMEM((BLOCK * TILE, width), F32)],
        [bar, y],
    )
    def added(values):
        value = values[0].astype(F32)
        for other in values[1:]:
            value = value + other.astype(F32)
        return value.astype(bf16)

    arrived, far = lax.optimization_barrier((arrived, far))
    target_rows = added(arrived)
    merged = call(
        merge_kernel,
        "merge",
        [((source_piece, width), bf16 if d else F32) for d in range(columns_of_chips)],
        [],
        [near, swap(far, ("rep",), 1)],
    )
    terms = [merged[0]] + [swap(merged[d], ("col",), d) for d in range(1, columns_of_chips)]
    gathered = spread(target_rows, over_target)
    crossed = [swap(value, ("rep",), 1) for value in gathered]
    late_ones = [k for k in range(rows) if k // per_tile in (1, 2)]
    ranks = [(k, 0) for k in range(rows)]
    ranks += [(k, 1) for k in range(rows) if k not in late_ones]
    source_shape = (source_piece, width)
    on_vmem = pl.BlockSpec(memory_space=pltpu.VMEM)
    on_hbm = pl.BlockSpec(memory_space=pltpu.HBM)
    target_out = jax.ShapeDtypeStruct(target_emb.shape, bf16)
    params = pltpu.CompilerParams(vmem_limit_bytes=LIMIT)
    grad_source, grad_target = pl.pallas_call(
        functools.partial(finish_kernel, ranks, len(terms)),
        name="finish",
        out_shape=[jax.ShapeDtypeStruct(source_shape, bf16), target_out],
        in_specs=[on_vmem] * (len(ranks) + len(terms)),
        out_specs=[on_hbm] * 2,
        scratch_shapes=[
            pltpu.VMEM(source_shape, bf16),
            pltpu.SemaphoreType.DMA((len(ranks) + 1,)),
        ],
        compiler_params=params,
    )(*[(crossed if c else gathered)[k] for k, c in ranks], *terms)
    ranks = [(k, 1) for k in late_ones]
    grad_target = pl.pallas_call(
        functools.partial(finish_kernel, ranks, 0),
        name="finish_last",
        out_shape=target_out,
        in_specs=[on_vmem] * len(ranks) + [on_hbm],
        out_specs=on_hbm,
        scratch_shapes=[pltpu.SemaphoreType.DMA((len(ranks),))],
        input_output_aliases={len(ranks): 0},
        compiler_params=params,
    )(*[crossed[k] for k in late_ones], grad_target)
    return grad_source, grad_target


def solution(mesh):
    return jax.shard_map(
        functools.partial(shards, dict(mesh.shape)),
        mesh=mesh,
        in_specs=(
            P(("groups", "row"), None),
            P(("groups", "col"), None),
            P(("groups", "col")),
            P(("groups", "row")),
            P(("groups", "col")),
            P("groups"),
            P("groups"),
            P("groups", None),
        ),
        out_specs=(P(("groups", "row", "col", "rep"), None), P(("groups", "col"), None)),
        check_vma=False,
    )
```

time: 84.8 us -> 80.1 us (0.945)
  waiting for transfers between devices: 33.1 us -> 28.3 us
  starting transfers between devices: 32.7 us -> 33.8 us
    ppermute x33, waiting for transfers between devices: 33.1 us -> 28.3 us  [swap(): return lax.ppermute(value, axes, [(i, i ^ k) for i in range(count)])]
    pallas_call x13, Pallas kernels: 16.4 us -> 14.9 us  [call(): pl.pallas_call(kernel, name=name, out_shape=[pltpu.VMEM(shape, dtype) for...]
    ppermute x33, starting transfers between devices: 32.7 us -> 33.8 us  [swap(): return lax.ppermute(value, axes, [(i, i ^ k) for i in range(count)])]
    pallas_call x1 -> x2, Pallas kernels: 1.14 us -> 1.77 us  [the longest x1 1.03 us: shards(): pl.pallas_call(functools.partial(finish_kernel, ranks, len(terms)), name=...]
  transfers between devices with their start and end apart: 33 -> 33, of which waited for: 21 -> 19; matrix products, arithmetic and copies ran while one was open for 0% -> 0% of each run, Pallas kernels for 3% -> 7%
where the time goes in v4:
time: 80.1 us; the launch traced here: 79.9 us
  starting transfers between devices  33.8 us (42%)
  waiting for transfers between devices  28.3 us (35%)
  Pallas kernels  16.7 us (21%)
  between operations  0.95 us (1%)
    ppermute x33, starting transfers between devices, swap(): return lax.ppermute(value, axes, [(i, i ^ k) for i in range(count)])  33.8 us
    ppermute x33, waiting for transfers between devices, swap(): return lax.ppermute(value, axes, [(i, i ^ k) for i in range(count)])  28.3 us
    pallas_call x13, Pallas kernels, call(): pl.pallas_call(kernel, name=name, out_shape=[pltpu.VMEM(shape, dtype) for...  14.9 us
  transfers between devices with their start and end apart: 33, of which 19 were waited for; matrix products, arithmetic and copies ran while one was open for 0% of the time, Pallas kernels for 7%

profile of v4, /device:TPU:0, one launch (start us, length us, event | category | flops | bytes accessed | tf_op | source)
XLA Modules:
  0.0 79.9 jit_solution(15611546364521605039)
XLA Ops:
  0.6 4.0 %first_source.1 = (f32[4,512,1024]{2,1,0:T(8,128)S(1)}, f32[8,1,512]{2,1,0:T(1,128)S(1)}, s32[8,128]{1,0:T(8,128)S(1)}, bf16[4,512,256]{2,1,0:T(8,128)(2,1)S(1)}...) custom-call(bf16[4,512,256]{2,1,0:T(8,128)(2,1)} %bitcast.8, bf16[4,2,256,256]{3,2,1,0:T(8,128)(2,1)} %bitcast.9, ...), custom_call_target="tpu_custom_call" | custom-call | tf_op jit(solution)/shard_map/first_source/pallas_call | solution.py:386
  4.6 2.4 %collective-permute-start.2 = (f32[8,1,512]{2,1,0:T(1,128)S(1)}, f32[8,1,512]{2,1,0:T(1,128)S(1)}, u32[]{:S(2)}, u32[]{:S(2)}) collective-permute-start(f32[8,1,512]{2,1,0:T(1,128)S(1)} %get-tuple-element.45.args_0_), channel_id=1, source_target_pairs={{0,3},{1,2},{2,1},{3,0},{4,7},{5,6},{6,5},{7,4},{8,11},{9,10},{10,... | collective-permute-start | bytes 49160 | tf_op jit(solution)/shard_map/ppermute | solution.py:414
  8.5 2.3 %collective-permute-done.1.args_2_ = f32[8,1,512]{2,1,0:T(1,128)S(1)} collective-permute-done((f32[8,1,512]{2,1,0:T(1,128)S(1)}, f32[8,1,512]{2,1,0:T(1,128)S(1)}, u32[]{:S(2)}, u32[]{:S(2)}) %collective-permute-start.1) | collective-permute-done | bytes 16416 | tf_op jit(solution)/shard_map/ppermute | solution.py:414
  10.8 1.9 %first_target.1 = (f32[4,512,1024]{2,1,0:T(8,128)S(1)}, f32[8,1,256]{2,1,0:T(1,128)S(1)}) custom-call(f32[8,1,512]{2,1,0:T(1,128)S(1)} %get-tuple-element.45.args_0_, f32[8,1,512]{2,1,0:T(1,128)S(1)} %collective-permute-done.args_1_, f32[8,1,512]{2,1,0:T(1,128)S(1)} %collective-permute-done.1.args_2_, f32[8,1,512]{2,1,0:T(1,128)S(1)} %collective-permute-done.2.args_3_, ...), custom_call_target="tpu_custom_call" | custom-call | tf_op jit(solution)/shard_map/first_target/pallas_call | solution.py:386
  12.7 3.7 %collective-permute-start.5 = (f32[8,1,256]{2,1,0:T(1,128)S(1)}, f32[8,1,256]{2,1,0:T(1,128)S(1)}, u32[]{:S(2)}, u32[]{:S(2)}) collective-permute-start(f32[8,1,256]{2,1,0:T(1,128)S(1)} %get-tuple-element.49.args_0_), channel_id=1, source_target_pairs={{0,12},{4,8},{8,4},{12,0},{1,13},{5,9},{9,5},{13,1},{2,14},{6,10},... | collective-permute-start | bytes 24584 | tf_op jit(solution)/shard_map/ppermute | solution.py:414
  17.2 1.2 %collective-permute-done.5.args_3_ = f32[8,1,256]{2,1,0:T(1,128)S(1)} collective-permute-done((f32[8,1,256]{2,1,0:T(1,128)S(1)}, f32[8,1,256]{2,1,0:T(1,128)S(1)}, u32[]{:S(2)}, u32[]{:S(2)}) %collective-permute-start.5) | collective-permute-done | bytes 8224 | tf_op jit(solution)/shard_map/ppermute | solution.py:414
  18.4 2.6 %collective-permute-done.4.args_2_ = f32[8,1,256]{2,1,0:T(1,128)S(1)} collective-permute-done((f32[8,1,256]{2,1,0:T(1,128)S(1)}, f32[8,1,256]{2,1,0:T(1,128)S(1)}, u32[]{:S(2)}, u32[]{:S(2)}) %collective-permute-start.4) | collective-permute-done | bytes 8224 | tf_op jit(solution)/shard_map/ppermute | solution.py:414
  22.4 1.1 %collective-permute-start.6 = (f32[4,1,512]{2,1,0:T(1,128)S(1)}, f32[4,1,512]{2,1,0:T(1,128)S(1)}, u32[]{:S(2)}, u32[]{:S(2)}) collective-permute-start(f32[4,1,512]{2,1,0:T(1,128)S(1)} %get-tuple-element.51.args_0_), channel_id=1, source_target_pairs={{0,1},{1,0},{2,3},{3,2},{4,5},{5,4},{6,7},{7,6},{8,9},{9,8},{10,11... | collective-permute-start | bytes 24584 | tf_op jit(solution)/shard_map/ppermute | solution.py:414
  23.5 1.2 %collective-permute-done.8.args_3_ = f32[4,1,512]{2,1,0:T(1,128)S(1)} collective-permute-done((f32[4,1,512]{2,1,0:T(1,128)S(1)}, f32[4,1,512]{2,1,0:T(1,128)S(1)}, u32[]{:S(2)}, u32[]{:S(2)}) %collective-permute-start.8) | collective-permute-done | bytes 8224 | tf_op jit(solution)/shard_map/ppermute | solution.py:414
  26.1 1.5 %collective-permute-start.11 = (f32[4,1,256]{2,1,0:T(1,128)S(1)}, f32[4,1,256]{2,1,0:T(1,128)S(1)}, u32[]{:S(2)}, u32[]{:S(2)}) collective-permute-start(f32[4,1,256]{2,1,0:T(1,128)S(1)} %get-tuple-element.54.args_0_), channel_id=1, source_target_pairs={{0,12},{4,8},{8,4},{12,0},{1,13},{5,9},{9,5},{13,1},{2,14},{6,10},... | collective-permute-start | bytes 12296 | tf_op jit(solution)/shard_map/ppermute | solution.py:414
  28.2 2.3 %collective-permute-start.9 = (f32[4,1,256]{2,1,0:T(1,128)S(1)}, f32[4,1,256]{2,1,0:T(1,128)S(1)}, u32[]{:S(2)}, u32[]{:S(2)}) collective-permute-start(f32[4,1,256]{2,1,0:T(1,128)S(1)} %get-tuple-element.54.args_0_), channel_id=1, source_target_pairs={{0,4},{4,0},{8,12},{12,8},{1,5},{5,1},{9,13},{13,9},{2,6},{6,2},{1... | collective-permute-start | bytes 12296 | tf_op jit(solution)/shard_map/ppermute | solution.py:414
  30.5 1.0 %collective-permute-done.11.args_3_ = f32[4,1,256]{2,1,0:T(1,128)S(1)} collective-permute-done((f32[4,1,256]{2,1,0:T(1,128)S(1)}, f32[4,1,256]{2,1,0:T(1,128)S(1)}, u32[]{:S(2)}, u32[]{:S(2)}) %collective-permute-start.11) | collective-permute-done | bytes 4128 | tf_op jit(solution)/shard_map/ppermute | solution.py:414
  33.5 1.1 %collective-permute-start.12 = (f32[4,1,512]{2,1,0:T(1,128)S(1)}, f32[4,1,512]{2,1,0:T(1,128)S(1)}, u32[]{:S(2)}, u32[]{:S(2)}) collective-permute-start(f32[4,1,512]{2,1,0:T(1,128)S(1)} %get-tuple-element.55.args_0_), channel_id=1, source_target_pairs={{0,1},{1,0},{2,3},{3,2},{4,5},{5,4},{6,7},{7,6},{8,9},{9,8},{10,11... | collective-permute-start | bytes 24584 | tf_op jit(solution)/shard_map/ppermute | solution.py:414
  34.7 1.2 %collective-permute-done.14.args_3_ = f32[4,1,512]{2,1,0:T(1,128)S(1)} collective-permute-done((f32[4,1,512]{2,1,0:T(1,128)S(1)}, f32[4,1,512]{2,1,0:T(1,128)S(1)}, u32[]{:S(2)}, u32[]{:S(2)}) %collective-permute-start.14) | collective-permute-done | bytes 8224 | tf_op jit(solution)/shard_map/ppermute | solution.py:414
  37.3 2.6 %collective-permute-start.17 = (f32[4,1,256]{2,1,0:T(1,128)S(1)}, f32[4,1,256]{2,1,0:T(1,128)S(1)}, u32[]{:S(2)}, u32[]{:S(2)}) collective-permute-start(f32[4,1,256]{2,1,0:T(1,128)S(1)} %get-tuple-element.59.args_0_), channel_id=1, source_target_pairs={{0,12},{4,8},{8,4},{12,0},{1,13},{5,9},{9,5},{13,1},{2,14},{6,10},... | collective-permute-start | bytes 12296 | tf_op jit(solution)/shard_map/ppermute | solution.py:414
  42.7 1.6 %collective-permute-done.16.args_2_ = f32[4,1,256]{2,1,0:T(1,128)S(1)} collective-permute-done((f32[4,1,256]{2,1,0:T(1,128)S(1)}, f32[4,1,256]{2,1,0:T(1,128)S(1)}, u32[]{:S(2)}, u32[]{:S(2)}) %collective-permute-start.16) | collective-permute-done | bytes 4128 | tf_op jit(solution)/shard_map/ppermute | solution.py:414
  45.9 1.1 %collective-permute-start.18 = (f32[4,1,512]{2,1,0:T(1,128)S(1)}, f32[4,1,512]{2,1,0:T(1,128)S(1)}, u32[]{:S(2)}, u32[]{:S(2)}) collective-permute-start(f32[4,1,512]{2,1,0:T(1,128)S(1)} %get-tuple-element.62.args_0_), channel_id=1, source_target_pairs={{0,1},{1,0},{2,3},{3,2},{4,5},{5,4},{6,7},{7,6},{8,9},{9,8},{10,11... | collective-permute-start | bytes 24584 | tf_op jit(solution)/shard_map/ppermute | solution.py:414
  47.0 1.2 %collective-permute-done.20.args_3_ = f32[4,1,512]{2,1,0:T(1,128)S(1)} collective-permute-done((f32[4,1,512]{2,1,0:T(1,128)S(1)}, f32[4,1,512]{2,1,0:T(1,128)S(1)}, u32[]{:S(2)}, u32[]{:S(2)}) %collective-permute-start.20) | collective-permute-done | bytes 8224 | tf_op jit(solution)/shard_map/ppermute | solution.py:414
  48.9 1.1 %target_gradient_3.1 = (bf16[4,512,1024]{2,1,0:T(8,128)(2,1)S(1)}, f32[4,512,128]{2,1,0:T(8,128)S(1)}, bf16[256,256]{1,0:T(8,128)(2,1)S(1)}) custom-call(f32[4,1,512]{2,1,0:T(1,128)S(1)} %get-tuple-element.62.args_0_, f32[4,1,512]{2,1,0:T(1,128)S(1)} %collective-permute-done.18.args_1_, f32[4,1,512]{2,1,0:T(1,128)S(1)} %collective-permute-done.19.args_2_, ...), custom_call_target="tpu_custom_call" | custom-call | tf_op jit(solution)/shard_map/target_gradient_3/pallas_call | solution.py:386
  50.0 1.4 %collective-permute-start.21 = (bf16[256,256]{1,0:T(8,128)(2,1)S(1)}, bf16[256,256]{1,0:T(8,128)(2,1)S(1)}, u32[]{:S(2)}, u32[]{:S(2)}) collective-permute-start(bf16[256,256]{1,0:T(8,128)(2,1)S(1)} %get-tuple-element.67), channel_id=1, source_target_pairs={{0,12},{4,8},{8,4},{12,0},{1,13},{5,9},{9,5},{13,1},{2,14},{6,10},... | collective-permute-start | bytes 393224 | tf_op jit(solution)/shard_map/ppermute | solution.py:414
  52.5 1.1 %target_gradient_1.1 = (bf16[4,512,1024]{2,1,0:T(8,128)(2,1)S(1)}, bf16[256,256]{1,0:T(8,128)(2,1)S(1)}) custom-call(bf16[4,512,256]{2,1,0:T(8,128)(2,1)S(1)} %get-tuple-element.44.args_4_.args_0_, f32[4,512,1024]{2,1,0:T(8,128)S(1)} %get-tuple-element.48.args_5_.args_4_.args_1_, ...), custom_call_target="tpu_custom_call", output_to_operand_aliasing={{0}: (9, {})} | custom-call | tf_op jit(solution)/shard_map/target_gradient_1/pallas_call | solution.py:386
  53.5 1.4 %collective-permute-start.22 = (bf16[256,256]{1,0:T(8,128)(2,1)S(1)}, bf16[256,256]{1,0:T(8,128)(2,1)S(1)}, u32[]{:S(2)}, u32[]{:S(2)}) collective-permute-start(bf16[256,256]{1,0:T(8,128)(2,1)S(1)} %get-tuple-element.70), channel_id=1, source_target_pairs={{0,4},{4,0},{8,12},{12,8},{1,5},{5,1},{9,13},{13,9},{2,6},{6,2},{1... | collective-permute-start | bytes 393224 | tf_op jit(solution)/shard_map/ppermute | solution.py:414
  55.0 1.8 %collective-permute-start.23 = (bf16[256,256]{1,0:T(8,128)(2,1)S(1)}, bf16[256,256]{1,0:T(8,128)(2,1)S(1)}, u32[]{:S(2)}, u32[]{:S(2)}) collective-permute-start(bf16[256,256]{1,0:T(8,128)(2,1)S(1)} %get-tuple-element.71), channel_id=1, source_target_pairs={{0,8},{4,12},{8,0},{12,4},{1,9},{5,13},{9,1},{13,5},{2,10},{6,14},... | collective-permute-start | bytes 393224 | tf_op jit(solution)/shard_map/ppermute | solution.py:414
  58.4 1.4 %source_gradient.1 = (f32[2,512,256]{2,1,0:T(8,128)S(1)}, bf16[2,512,256]{2,1,0:T(8,128)(2,1)S(1)}) custom-call(bf16[4,512,1024]{2,1,0:T(8,128)(2,1)S(1)} %get-tuple-element.73.bar_ref, bf16[4,256,256]{2,1,0:T(8,128)(2,1)S(1)} %get-tuple-element.74.y_ref), custom_call_target="tpu_custom_call" | custom-call | tf_op jit(solution)/shard_map/source_gradient/pallas_call | solution.py:386
  59.9 1.5 %collective-permute-done.22 = bf16[256,256]{1,0:T(8,128)(2,1)S(1)} collective-permute-done((bf16[256,256]{1,0:T(8,128)(2,1)S(1)}, bf16[256,256]{1,0:T(8,128)(2,1)S(1)}, u32[]{:S(2)}, u32[]{:S(2)}) %collective-permute-start.22) | collective-permute-done | bytes 131104 | tf_op jit(solution)/shard_map/ppermute | solution.py:414
  61.3 2.4 %collective-permute-done.23 = bf16[256,256]{1,0:T(8,128)(2,1)S(1)} collective-permute-done((bf16[256,256]{1,0:T(8,128)(2,1)S(1)}, bf16[256,256]{1,0:T(8,128)(2,1)S(1)}, u32[]{:S(2)}, u32[]{:S(2)}) %collective-permute-start.23) | collective-permute-done | bytes 131104 | tf_op jit(solution)/shard_map/ppermute | solution.py:414
  63.8 2.6 %collective-permute-start.26 = (bf16[256,256]{1,0:T(8,128)(2,1)S(1)}, bf16[256,256]{1,0:T(8,128)(2,1)S(1)}, u32[]{:S(2)}, u32[]{:S(2)}) collective-permute-start(bf16[256,256]{1,0:T(8,128)(2,1)S(1)} %add_convert_fusion.args_0_), channel_id=1, source_target_pairs={{0,12},{4,8},{8,4},{12,0},{1,13},{5,9},{9,5},{13,1},{2,14},{6,10},... | collective-permute-start | bytes 393224 | tf_op jit(solution)/shard_map/ppermute | solution.py:414
  66.6 1.5 %collective-permute-start.30 = (bf16[512,256]{1,0:T(8,128)(2,1)S(1)}, bf16[512,256]{1,0:T(8,128)(2,1)S(1)}, u32[]{:S(2)}, u32[]{:S(2)}) collective-permute-start(bf16[512,256]{1,0:T(8,128)(2,1)S(1)} %get-tuple-element.83), channel_id=1, source_target_pairs={{0,2},{2,0},{1,3},{3,1},{4,6},{6,4},{5,7},{7,5},{8,10},{10,8},{9,1... | collective-permute-start | bytes 786440 | tf_op jit(solution)/shard_map/ppermute | solution.py:414
  68.0 2.3 %collective-permute-start.24 = (bf16[256,256]{1,0:T(8,128)(2,1)S(1)}, bf16[256,256]{1,0:T(8,128)(2,1)S(1)}, u32[]{:S(2)}, u32[]{:S(2)}) collective-permute-start(bf16[256,256]{1,0:T(8,128)(2,1)S(1)} %add_convert_fusion.args_0_), channel_id=1, source_target_pairs={{0,4},{4,0},{8,12},{12,8},{1,5},{5,1},{9,13},{13,9},{2,6},{6,2},{1... | collective-permute-start | bytes 393224 | tf_op jit(solution)/shard_map/ppermute | solution.py:414
  70.3 1.8 %collective-permute-done.26.args_3_ = bf16[256,256]{1,0:T(8,128)(2,1)S(1)} collective-permute-done((bf16[256,256]{1,0:T(8,128)(2,1)S(1)}, bf16[256,256]{1,0:T(8,128)(2,1)S(1)}, u32[]{:S(2)}, u32[]{:S(2)}) %collective-permute-start.26) | collective-permute-done | bytes 131104 | tf_op jit(solution)/shard_map/ppermute | solution.py:414
  72.1 5.3 %collective-permute-done.25.args_2_ = bf16[256,256]{1,0:T(8,128)(2,1)S(1)} collective-permute-done((bf16[256,256]{1,0:T(8,128)(2,1)S(1)}, bf16[256,256]{1,0:T(8,128)(2,1)S(1)}, u32[]{:S(2)}, u32[]{:S(2)}) %collective-permute-start.25) | collective-permute-done | bytes 131104 | tf_op jit(solution)/shard_map/ppermute | solution.py:414
  77.9 1.0 %finish.1 = (bf16[512,256]{1,0:T(8,128)(2,1)}, bf16[2048,256]{1,0:T(8,128)(2,1)}) custom-call(bf16[256,256]{1,0:T(8,128)(2,1)S(1)} %add_convert_fusion.args_0_, bf16[256,256]{1,0:T(8,128)(2,1)S(1)} %collective-permute-done.24.args_1_, bf16[256,256]{1,0:T(8,128)(2,1)S(1)} %collective-permute-done.25.args_2_, ...), custom_call_target="tpu_custom_call" | custom-call | tf_op jit(solution)/shard_map/finish/pallas_call | solution.py:580
  (54 shorter events, 18.0 us)
Async XLA Ops:
  4.6 3.9 %collective-permute-start.2 = (f32[8,1,512]{2,1,0:T(1,128)S(1)}, f32[8,1,512]{2,1,0:T(1,128)S(1)}, u32[]{:S(2)}, u32[]{:S(2)}) collective-permute-start(f32[8,1,512]{2,1,0:T(1,128)S(1)} %get-tuple-element.45.args_0_), channel_id=1, source_target_pairs={{0,3},{1,2},{2,1},{3,0},{4,7},{5,6},{6,5},{7,4},{8,11},{9,10},{10,... | collective-permute-start | bytes 49160 | tf_op jit(solution)/shard_map/ppermute | solution.py:414
  7.1 3.7 %collective-permute-start.1 = (f32[8,1,512]{2,1,0:T(1,128)S(1)}, f32[8,1,512]{2,1,0:T(1,128)S(1)}, u32[]{:S(2)}, u32[]{:S(2)}) collective-permute-start(f32[8,1,512]{2,1,0:T(1,128)S(1)} %get-tuple-element.45.args_0_), channel_id=1, source_target_pairs={{0,2},{1,3},{2,0},{3,1},{4,6},{5,7},{6,4},{7,5},{8,10},{9,11},{10,... | collective-permute-start | bytes 49160 | tf_op jit(solution)/shard_map/ppermute | solution.py:414
  7.7 3.1 %collective-permute-start = (f32[8,1,512]{2,1,0:T(1,128)S(1)}, f32[8,1,512]{2,1,0:T(1,128)S(1)}, u32[]{:S(2)}, u32[]{:S(2)}) collective-permute-start(f32[8,1,512]{2,1,0:T(1,128)S(1)} %get-tuple-element.45.args_0_), channel_id=1, source_target_pairs={{0,1},{1,0},{2,3},{3,2},{4,5},{5,4},{6,7},{7,6},{8,9},{9,8},{10,11... | collective-permute-start | bytes 49160 | tf_op jit(solution)/shard_map/ppermute | solution.py:414
  12.7 5.6 %collective-permute-start.5 = (f32[8,1,256]{2,1,0:T(1,128)S(1)}, f32[8,1,256]{2,1,0:T(1,128)S(1)}, u32[]{:S(2)}, u32[]{:S(2)}) collective-permute-start(f32[8,1,256]{2,1,0:T(1,128)S(1)} %get-tuple-element.49.args_0_), channel_id=1, source_target_pairs={{0,12},{4,8},{8,4},{12,0},{1,13},{5,9},{9,5},{13,1},{2,14},{6,10},... | collective-permute-start | bytes 24584 | tf_op jit(solution)/shard_map/ppermute | solution.py:414
  16.4 4.5 %collective-permute-start.4 = (f32[8,1,256]{2,1,0:T(1,128)S(1)}, f32[8,1,256]{2,1,0:T(1,128)S(1)}, u32[]{:S(2)}, u32[]{:S(2)}) collective-permute-start(f32[8,1,256]{2,1,0:T(1,128)S(1)} %get-tuple-element.49.args_0_), channel_id=1, source_target_pairs={{0,8},{4,12},{8,0},{12,4},{1,9},{5,13},{9,1},{13,5},{2,10},{6,14},... | collective-permute-start | bytes 24584 | tf_op jit(solution)/shard_map/ppermute | solution.py:414
  16.4 4.5 %collective-permute-start.3 = (f32[8,1,256]{2,1,0:T(1,128)S(1)}, f32[8,1,256]{2,1,0:T(1,128)S(1)}, u32[]{:S(2)}, u32[]{:S(2)}) collective-permute-start(f32[8,1,256]{2,1,0:T(1,128)S(1)} %get-tuple-element.49.args_0_), channel_id=1, source_target_pairs={{0,4},{4,0},{8,12},{12,8},{1,5},{5,1},{9,13},{13,9},{2,6},{6,2},{1... | collective-permute-start | bytes 24584 | tf_op jit(solution)/shard_map/ppermute | solution.py:414
  21.6 3.1 %collective-permute-start.8 = (f32[4,1,512]{2,1,0:T(1,128)S(1)}, f32[4,1,512]{2,1,0:T(1,128)S(1)}, u32[]{:S(2)}, u32[]{:S(2)}) collective-permute-start(f32[4,1,512]{2,1,0:T(1,128)S(1)} %get-tuple-element.51.args_0_), channel_id=1, source_target_pairs={{0,3},{1,2},{2,1},{3,0},{4,7},{5,6},{6,5},{7,4},{8,11},{9,10},{10,... | collective-permute-start | bytes 24584 | tf_op jit(solution)/shard_map/ppermute | solution.py:414
  21.7 3.7 %collective-permute-start.7 = (f32[4,1,512]{2,1,0:T(1,128)S(1)}, f32[4,1,512]{2,1,0:T(1,128)S(1)}, u32[]{:S(2)}, u32[]{:S(2)}) collective-permute-start(f32[4,1,512]{2,1,0:T(1,128)S(1)} %get-tuple-element.51.args_0_), channel_id=1, source_target_pairs={{0,2},{1,3},{2,0},{3,1},{4,6},{5,7},{6,4},{7,5},{8,10},{9,11},{10,... | collective-permute-start | bytes 24584 | tf_op jit(solution)/shard_map/ppermute | solution.py:414
  22.4 3.0 %collective-permute-start.6 = (f32[4,1,512]{2,1,0:T(1,128)S(1)}, f32[4,1,512]{2,1,0:T(1,128)S(1)}, u32[]{:S(2)}, u32[]{:S(2)}) collective-permute-start(f32[4,1,512]{2,1,0:T(1,128)S(1)} %get-tuple-element.51.args_0_), channel_id=1, source_target_pairs={{0,1},{1,0},{2,3},{3,2},{4,5},{5,4},{6,7},{7,6},{8,9},{9,8},{10,11... | collective-permute-start | bytes 24584 | tf_op jit(solution)/shard_map/ppermute | solution.py:414
  26.1 5.5 %collective-permute-start.11 = (f32[4,1,256]{2,1,0:T(1,128)S(1)}, f32[4,1,256]{2,1,0:T(1,128)S(1)}, u32[]{:S(2)}, u32[]{:S(2)}) collective-permute-start(f32[4,1,256]{2,1,0:T(1,128)S(1)} %get-tuple-element.54.args_0_), channel_id=1, source_target_pairs={{0,12},{4,8},{8,4},{12,0},{1,13},{5,9},{9,5},{13,1},{2,14},{6,10},... | collective-permute-start | bytes 12296 | tf_op jit(solution)/shard_map/ppermute | solution.py:414
  27.6 4.5 %collective-permute-start.10 = (f32[4,1,256]{2,1,0:T(1,128)S(1)}, f32[4,1,256]{2,1,0:T(1,128)S(1)}, u32[]{:S(2)}, u32[]{:S(2)}) collective-permute-start(f32[4,1,256]{2,1,0:T(1,128)S(1)} %get-tuple-element.54.args_0_), channel_id=1, source_target_pairs={{0,8},{4,12},{8,0},{12,4},{1,9},{5,13},{9,1},{13,5},{2,10},{6,14},... | collective-permute-start | bytes 12296 | tf_op jit(solution)/shard_map/ppermute | solution.py:414
  28.2 3.9 %collective-permute-start.9 = (f32[4,1,256]{2,1,0:T(1,128)S(1)}, f32[4,1,256]{2,1,0:T(1,128)S(1)}, u32[]{:S(2)}, u32[]{:S(2)}) collective-permute-start(f32[4,1,256]{2,1,0:T(1,128)S(1)} %get-tuple-element.54.args_0_), channel_id=1, source_target_pairs={{0,4},{4,0},{8,12},{12,8},{1,5},{5,1},{9,13},{13,9},{2,6},{6,2},{1... | collective-permute-start | bytes 12296 | tf_op jit(solution)/shard_map/ppermute | solution.py:414
  32.8 3.1 %collective-permute-start.14 = (f32[4,1,512]{2,1,0:T(1,128)S(1)}, f32[4,1,512]{2,1,0:T(1,128)S(1)}, u32[]{:S(2)}, u32[]{:S(2)}) collective-permute-start(f32[4,1,512]{2,1,0:T(1,128)S(1)} %get-tuple-element.55.args_0_), channel_id=1, source_target_pairs={{0,3},{1,2},{2,1},{3,0},{4,7},{5,6},{6,5},{7,4},{8,11},{9,10},{10,... | collective-permute-start | bytes 24584 | tf_op jit(solution)/shard_map/ppermute | solution.py:414
  32.8 3.7 %collective-permute-start.13 = (f32[4,1,512]{2,1,0:T(1,128)S(1)}, f32[4,1,512]{2,1,0:T(1,128)S(1)}, u32[]{:S(2)}, u32[]{:S(2)}) collective-permute-start(f32[4,1,512]{2,1,0:T(1,128)S(1)} %get-tuple-element.55.args_0_), channel_id=1, source_target_pairs={{0,2},{1,3},{2,0},{3,1},{4,6},{5,7},{6,4},{7,5},{8,10},{9,11},{10,... | collective-permute-start | bytes 24584 | tf_op jit(solution)/shard_map/ppermute | solution.py:414
  33.5 3.0 %collective-permute-start.12 = (f32[4,1,512]{2,1,0:T(1,128)S(1)}, f32[4,1,512]{2,1,0:T(1,128)S(1)}, u32[]{:S(2)}, u32[]{:S(2)}) collective-permute-start(f32[4,1,512]{2,1,0:T(1,128)S(1)} %get-tuple-element.55.args_0_), channel_id=1, source_target_pairs={{0,1},{1,0},{2,3},{3,2},{4,5},{5,4},{6,7},{7,6},{8,9},{9,8},{10,11... | collective-permute-start | bytes 24584 | tf_op jit(solution)/shard_map/ppermute | solution.py:414
  37.3 5.5 %collective-permute-start.17 = (f32[4,1,256]{2,1,0:T(1,128)S(1)}, f32[4,1,256]{2,1,0:T(1,128)S(1)}, u32[]{:S(2)}, u32[]{:S(2)}) collective-permute-start(f32[4,1,256]{2,1,0:T(1,128)S(1)} %get-tuple-element.59.args_0_), channel_id=1, source_target_pairs={{0,12},{4,8},{8,4},{12,0},{1,13},{5,9},{9,5},{13,1},{2,14},{6,10},... | collective-permute-start | bytes 12296 | tf_op jit(solution)/shard_map/ppermute | solution.py:414
  39.9 4.5 %collective-permute-start.16 = (f32[4,1,256]{2,1,0:T(1,128)S(1)}, f32[4,1,256]{2,1,0:T(1,128)S(1)}, u32[]{:S(2)}, u32[]{:S(2)}) collective-permute-start(f32[4,1,256]{2,1,0:T(1,128)S(1)} %get-tuple-element.59.args_0_), channel_id=1, source_target_pairs={{0,8},{4,12},{8,0},{12,4},{1,9},{5,13},{9,1},{13,5},{2,10},{6,14},... | collective-permute-start | bytes 12296 | tf_op jit(solution)/shard_map/ppermute | solution.py:414
  40.8 3.6 %collective-permute-start.15 = (f32[4,1,256]{2,1,0:T(1,128)S(1)}, f32[4,1,256]{2,1,0:T(1,128)S(1)}, u32[]{:S(2)}, u32[]{:S(2)}) collective-permute-start(f32[4,1,256]{2,1,0:T(1,128)S(1)} %get-tuple-element.59.args_0_), channel_id=1, source_target_pairs={{0,4},{4,0},{8,12},{12,8},{1,5},{5,1},{9,13},{13,9},{2,6},{6,2},{1... | collective-permute-start | bytes 12296 | tf_op jit(solution)/shard_map/ppermute | solution.py:414
  45.1 3.1 %collective-permute-start.20 = (f32[4,1,512]{2,1,0:T(1,128)S(1)}, f32[4,1,512]{2,1,0:T(1,128)S(1)}, u32[]{:S(2)}, u32[]{:S(2)}) collective-permute-start(f32[4,1,512]{2,1,0:T(1,128)S(1)} %get-tuple-element.62.args_0_), channel_id=1, source_target_pairs={{0,3},{1,2},{2,1},{3,0},{4,7},{5,6},{6,5},{7,4},{8,11},{9,10},{10,... | collective-permute-start | bytes 24584 | tf_op jit(solution)/shard_map/ppermute | solution.py:414
  45.2 3.7 %collective-permute-start.19 = (f32[4,1,512]{2,1,0:T(1,128)S(1)}, f32[4,1,512]{2,1,0:T(1,128)S(1)}, u32[]{:S(2)}, u32[]{:S(2)}) collective-permute-start(f32[4,1,512]{2,1,0:T(1,128)S(1)} %get-tuple-element.62.args_0_), channel_id=1, source_target_pairs={{0,2},{1,3},{2,0},{3,1},{4,6},{5,7},{6,4},{7,5},{8,10},{9,11},{10,... | collective-permute-start | bytes 24584 | tf_op jit(solution)/shard_map/ppermute | solution.py:414
  45.9 3.0 %collective-permute-start.18 = (f32[4,1,512]{2,1,0:T(1,128)S(1)}, f32[4,1,512]{2,1,0:T(1,128)S(1)}, u32[]{:S(2)}, u32[]{:S(2)}) collective-permute-start(f32[4,1,512]{2,1,0:T(1,128)S(1)} %get-tuple-element.62.args_0_), channel_id=1, source_target_pairs={{0,1},{1,0},{2,3},{3,2},{4,5},{5,4},{6,7},{7,6},{8,9},{9,8},{10,11... | collective-permute-start | bytes 24584 | tf_op jit(solution)/shard_map/ppermute | solution.py:414
  50.0 7.4 %collective-permute-start.21 = (bf16[256,256]{1,0:T(8,128)(2,1)S(1)}, bf16[256,256]{1,0:T(8,128)(2,1)S(1)}, u32[]{:S(2)}, u32[]{:S(2)}) collective-permute-start(bf16[256,256]{1,0:T(8,128)(2,1)S(1)} %get-tuple-element.67), channel_id=1, source_target_pairs={{0,12},{4,8},{8,4},{12,0},{1,13},{5,9},{9,5},{13,1},{2,14},{6,10},... | collective-permute-start | bytes 393224 | tf_op jit(solution)/shard_map/ppermute | solution.py:414
  53.5 7.8 %collective-permute-start.22 = (bf16[256,256]{1,0:T(8,128)(2,1)S(1)}, bf16[256,256]{1,0:T(8,128)(2,1)S(1)}, u32[]{:S(2)}, u32[]{:S(2)}) collective-permute-start(bf16[256,256]{1,0:T(8,128)(2,1)S(1)} %get-tuple-element.70), channel_id=1, source_target_pairs={{0,4},{4,0},{8,12},{12,8},{1,5},{5,1},{9,13},{13,9},{2,6},{6,2},{1... | collective-permute-start | bytes 393224 | tf_op jit(solution)/shard_map/ppermute | solution.py:414
  55.0 8.8 %collective-permute-start.23 = (bf16[256,256]{1,0:T(8,128)(2,1)S(1)}, bf16[256,256]{1,0:T(8,128)(2,1)S(1)}, u32[]{:S(2)}, u32[]{:S(2)}) collective-permute-start(bf16[256,256]{1,0:T(8,128)(2,1)S(1)} %get-tuple-element.71), channel_id=1, source_target_pairs={{0,8},{4,12},{8,0},{12,4},{1,9},{5,13},{9,1},{13,5},{2,10},{6,14},... | collective-permute-start | bytes 393224 | tf_op jit(solution)/shard_map/ppermute | solution.py:414
  63.8 2.7 %collective-permute-start.29 = (bf16[2,512,256]{2,1,0:T(8,128)(2,1)S(1)}, bf16[2,512,256]{2,1,0:T(8,128)(2,1)S(1)}, u32[]{:S(2)}, u32[]{:S(2)}) collective-permute-start(bf16[2,512,256]{2,1,0:T(8,128)(2,1)S(1)} %get-tuple-element.81), channel_id=1, source_target_pairs={{0,1},{1,0},{2,3},{3,2},{4,5},{5,4},{6,7},{7,6},{8,9},{9,8},{10,11... | collective-permute-start | bytes 1572872 | tf_op jit(solution)/shard_map/ppermute | solution.py:414
  63.8 8.3 %collective-permute-start.26 = (bf16[256,256]{1,0:T(8,128)(2,1)S(1)}, bf16[256,256]{1,0:T(8,128)(2,1)S(1)}, u32[]{:S(2)}, u32[]{:S(2)}) collective-permute-start(bf16[256,256]{1,0:T(8,128)(2,1)S(1)} %add_convert_fusion.args_0_), channel_id=1, source_target_pairs={{0,12},{4,8},{8,4},{12,0},{1,13},{5,9},{9,5},{13,1},{2,14},{6,10},... | collective-permute-start | bytes 393224 | tf_op jit(solution)/shard_map/ppermute | solution.py:414
  66.6 11.4 %collective-permute-start.30 = (bf16[512,256]{1,0:T(8,128)(2,1)S(1)}, bf16[512,256]{1,0:T(8,128)(2,1)S(1)}, u32[]{:S(2)}, u32[]{:S(2)}) collective-permute-start(bf16[512,256]{1,0:T(8,128)(2,1)S(1)} %get-tuple-element.83), channel_id=1, source_target_pairs={{0,2},{2,0},{1,3},{3,1},{4,6},{6,4},{5,7},{7,5},{8,10},{10,8},{9,1... | collective-permute-start | bytes 786440 | tf_op jit(solution)/shard_map/ppermute | solution.py:414
  68.0 9.4 %collective-permute-start.25 = (bf16[256,256]{1,0:T(8,128)(2,1)S(1)}, bf16[256,256]{1,0:T(8,128)(2,1)S(1)}, u32[]{:S(2)}, u32[]{:S(2)}) collective-permute-start(bf16[256,256]{1,0:T(8,128)(2,1)S(1)} %add_convert_fusion.args_0_), channel_id=1, source_target_pairs={{0,8},{4,12},{8,0},{12,4},{1,9},{5,13},{9,1},{13,5},{2,10},{6,14},... | collective-permute-start | bytes 393224 | tf_op jit(solution)/shard_map/ppermute | solution.py:414
  68.0 9.5 %collective-permute-start.24 = (bf16[256,256]{1,0:T(8,128)(2,1)S(1)}, bf16[256,256]{1,0:T(8,128)(2,1)S(1)}, u32[]{:S(2)}, u32[]{:S(2)}) collective-permute-start(bf16[256,256]{1,0:T(8,128)(2,1)S(1)} %add_convert_fusion.args_0_), channel_id=1, source_target_pairs={{0,4},{4,0},{8,12},{12,8},{1,5},{5,1},{9,13},{13,9},{2,6},{6,2},{1... | collective-permute-start | bytes 393224 | tf_op jit(solution)/shard_map/ppermute | solution.py:414
  70.3 7.6 %collective-permute-start.27 = (bf16[256,256]{1,0:T(8,128)(2,1)S(1)}, bf16[256,256]{1,0:T(8,128)(2,1)S(1)}, u32[]{:S(2)}, u32[]{:S(2)}) collective-permute-start(bf16[256,256]{1,0:T(8,128)(2,1)S(1)} %add_convert_fusion.args_0_), channel_id=1, source_target_pairs={{0,1},{1,0},{2,3},{3,2},{4,5},{5,4},{6,7},{7,6},{8,9},{9,8},{10,11... | collective-permute-start | bytes 393224 | tf_op jit(solution)/shard_map/ppermute | solution.py:414
  72.1 5.8 %collective-permute-start.28 = (bf16[256,256]{1,0:T(8,128)(2,1)S(1)}, bf16[256,256]{1,0:T(8,128)(2,1)S(1)}, u32[]{:S(2)}, u32[]{:S(2)}) collective-permute-start(bf16[256,256]{1,0:T(8,128)(2,1)S(1)} %collective-permute-done.26.args_3_), channel_id=1, source_target_pairs={{0,1},{1,0},{2,3},{3,2},{4,5},{5,4},{6,7},{7,6},{8,9},{9,8},{10,11... | collective-permute-start | bytes 393224 | tf_op jit(solution)/shard_map/ppermute | solution.py:414
  77.4 1.6 %collective-permute-start.32 = (bf16[256,256]{1,0:T(8,128)(2,1)S(1)}, bf16[256,256]{1,0:T(8,128)(2,1)S(1)}, u32[]{:S(2)}, u32[]{:S(2)}) collective-permute-start(bf16[256,256]{1,0:T(8,128)(2,1)S(1)} %collective-permute-done.25.args_2_), channel_id=1, source_target_pairs={{0,1},{1,0},{2,3},{3,2},{4,5},{5,4},{6,7},{7,6},{8,9},{9,8},{10,11... | collective-permute-start | bytes 393224 | tf_op jit(solution)/shard_map/ppermute | solution.py:414
  (3 other events, 12.6 us)

commit v5 on v4

--- a/solution.py
+++ b/solution.py
@@ -15,6 +15,7 @@
 ROWS = 64
 LIMIT = 24 * 1024 * 1024
 LOWEST = -1e30
+NEAR = 60.0
 F32 = jnp.float32
 NT_DIMS = (((1,), (1,)), ((), ()))
 NN_DIMS = (((1,), (0,)), ((), ()))
@@ -27,18 +28,8 @@
     return jnp.where(is_low, 0, second_cut), jnp.where(is_low, second_cut, BLOCK)
 
 
-def kept_sources(meta, t):
-    first_cut, second_cut, straight = meta
-    is_low = (t < second_cut).astype(jnp.int32) == straight
-    return jnp.where(is_low, 0, first_cut), jnp.where(is_low, first_cut, BLOCK)
-
-
 def tile_lanes(t):
     return pl.ds(pl.multiple_of(t * HALF, HALF), HALF)
-
-
-def read_meta(meta_ref):
-    return meta_ref[0, 0], meta_ref[0, 1], meta_ref[0, 2]
 
 
 def to_column(row):
@@ -105,13 +96,12 @@
     kp_hbm,
     score_ref,
     out_ref,
-    meta_ref,
     x_ref,
     y_ref,
-    warm_ref,
     sb_ref,
     tb_ref,
     kp_ref,
+    warm_ref,
     sems,
     bound_sems,
 ):
@@ -141,44 +131,41 @@
         return found | here.astype(jnp.int32)
 
     straight = lax.fori_loop(0, kp_ref.shape[1], look, jnp.int32(0))
-    lanes = lax.broadcasted_iota(jnp.int32, meta_ref.shape, 1)
-    meta_ref[...] = jnp.where(lanes == 0, first_cut, jnp.where(lanes == 1, second_cut, straight))
     meta = (first_cut, second_cut, straight)
     width = x_ref.shape[2]
     scale = width ** (-0.5) * math.log2(math.e)
 
     def scores(s):
-        score_ref[s] = scale * lax.dot_general(
+        biases = tile_biases(meta, s)
+        row = jnp.concatenate(
+            [warm_ref[t] * math.log2(math.e) + biases[t] for t in range(BLOCK)], axis=1
+        )
+        product = lax.dot_general(
             x_ref[s],
             y_ref[...].reshape(BLOCK * HALF, width),
             NT_DIMS,
             preferred_element_type=F32,
         )
+        score_ref[s] = scale * product + row
 
     def passes(s):
-        biases = tile_biases(meta, s)
-        warm = [
-            warm_ref[t, :, half_of(i)] * math.log2(math.e) + biases[t]
-            for i, (t, _) in enumerate(lane_groups())
-        ]
         for at in range(0, TILE, LANES):
             largest = None
-            for i, (_, lanes) in enumerate(lane_groups()):
-                term = score_ref[s, at : at + LANES, lanes] + warm[i]
+            for _, lanes in lane_groups():
+                term = score_ref[s, at : at + LANES, lanes]
                 largest = term if largest is None else jnp.maximum(largest, term)
             largest = jnp.max(largest, axis=1, keepdims=True)
             largest = jnp.broadcast_to(largest, (LANES, LANES))
             acc = None
-            for i, (_, lanes) in enumerate(lane_groups()):
-                term = jnp.exp2(score_ref[s, at : at + LANES, lanes] + warm[i] - largest)
+            for _, lanes in lane_groups():
+                term = jnp.exp2(score_ref[s, at : at + LANES, lanes] - largest)
                 acc = term if acc is None else acc + term
-            out_ref[s, :, at : at + LANES] = largest.T[:1]
-            out_ref[BLOCK + s, :, at : at + LANES] = lane_sums(acc)
-
+            out_ref[s, :, at : at + LANES] = largest.T[:1] + jnp.log2(lane_sums(acc))
+
+    warm_copy.wait()
     y_copy.wait()
     x_copy.wait()
     scores(0)
-    warm_copy.wait()
     rest_copy.wait()
     for s in range(BLOCK):
         if s + 1 < BLOCK:
@@ -186,58 +173,76 @@
         passes(s)
 
 
-def combine(refs, at, offset):
+def combine(refs, at):
     largest = refs[0][at]
     for ref in refs[1:]:
         largest = jnp.maximum(largest, ref[at])
-    sums = refs[0][offset + at] * jnp.exp2(refs[0][at] - largest)
+    sums = jnp.exp2(refs[0][at] - largest)
     for ref in refs[1:]:
-        sums = sums + ref[offset + at] * jnp.exp2(ref[at] - largest)
+        sums = sums + jnp.exp2(ref[at] - largest)
     return -(largest + jnp.log2(sums))
+
+
+def peaks(score_ref, column_ref, out_ref):
+    largest = [None] * (2 * BLOCK)
+    for s in range(BLOCK):
+        for at in range(0, TILE, LANES):
+            u = column_ref[s, at : at + LANES, :]
+            for i, (_, lanes) in enumerate(lane_groups()):
+                term = eight_rows(score_ref[s, at : at + LANES, lanes] + u, jnp.max)
+                largest[i] = term if largest[i] is None else jnp.maximum(largest[i], term)
+    for i, (t, _) in enumerate(lane_groups()):
+        out_ref[t, :, half_of(i)] = jnp.max(largest[i], axis=0, keepdims=True)
+
+
+def own_peaks_kernel(own_ref, score_ref, out_ref, column_ref):
+    for s in range(BLOCK):
+        column_ref[s] = to_column(-own_ref[s])
+    peaks(score_ref, column_ref, out_ref)
 
 
 def first_target_kernel(count, *args):
     parts = args[:count]
-    score_ref, meta_ref, e_ref, out_ref, column_ref = args[count:]
-    meta = read_meta(meta_ref)
-    biases = [tile_biases(meta, s) for s in range(BLOCK)]
-    largest = [None] * (2 * BLOCK)
-    for s in range(BLOCK):
-        column_ref[s] = to_column(combine(parts, s, BLOCK))
-        here = [None] * (2 * BLOCK)
+    score_ref, own_peaks_ref, e_ref, out_ref, shift_ref, column_ref = args[count:]
+    gap = None
+    for s in range(BLOCK):
+        potential = combine(parts, s)
+        column_ref[s] = to_column(potential)
+        term = -potential - parts[0][s]
+        gap = term if gap is None else jnp.maximum(gap, term)
+    is_near = jnp.max(gap) <= NEAR
+
+    @pl.when(is_near)
+    def _():
+        shift_ref[...] = own_peaks_ref[...]
+
+    @pl.when(jnp.logical_not(is_near))
+    def _():
+        peaks(score_ref, column_ref, shift_ref)
+
+    sums = [None] * (2 * BLOCK)
+    shifts = [shift_ref[t, :, half_of(i)] for i, (t, _) in enumerate(lane_groups())]
+    for s in range(BLOCK):
         for at in range(0, TILE, LANES):
             u = column_ref[s, at : at + LANES, :]
-            for i, (t, lanes) in enumerate(lane_groups()):
-                term = eight_rows(score_ref[s, at : at + LANES, lanes] + u, jnp.max)
-                here[i] = term if here[i] is None else jnp.maximum(here[i], term)
-        for i, (t, _) in enumerate(lane_groups()):
-            term = here[i] + biases[s][t]
-            largest[i] = term if s == 0 else jnp.maximum(largest[i], term)
-    sums = [None] * (2 * BLOCK)
-    for i, (t, _) in enumerate(lane_groups()):
-        largest[i] = jnp.max(largest[i], axis=0, keepdims=True)
-        out_ref[t, :, half_of(i)] = largest[i]
-    for s in range(BLOCK):
-        shifts = [largest[i] - biases[s][t] for i, (t, _) in enumerate(lane_groups())]
-        for at in range(0, TILE, LANES):
-            u = column_ref[s, at : at + LANES, :]
-            for i, (t, lanes) in enumerate(lane_groups()):
+            for i, (_, lanes) in enumerate(lane_groups()):
                 e = jnp.exp2(score_ref[s, at : at + LANES, lanes] + u - shifts[i])
                 e_ref[s, at : at + LANES, lanes] = e
                 term = eight_rows(e, jnp.sum)
                 sums[i] = term if sums[i] is None else sums[i] + term
     for i, (t, _) in enumerate(lane_groups()):
-        out_ref[BLOCK + t, :, half_of(i)] = jnp.sum(sums[i], axis=0, keepdims=True)
+        value = jnp.sum(sums[i], axis=0, keepdims=True)
+        out_ref[t, :, half_of(i)] = shifts[i] + jnp.log2(value)
 
 
 def second_source_kernel(count, *args):
     parts = args[:count]
-    warm_ref, e_ref, out_ref, q_ref, wq_ref = args[count:]
+    shift_ref, e_ref, out_ref, q_ref, wq_ref = args[count:]
     for t in range(BLOCK):
-        potential = combine(parts, t, BLOCK)
-        q = jnp.exp2(parts[0][t] + potential)
+        potential = combine(parts, t)
+        q = jnp.exp2(shift_ref[t] + potential)
         q_ref[t] = q
-        wq_ref[t] = q * jnp.exp2(warm_ref[t] * math.log2(math.e) - potential)
+        wq_ref[t] = q * jnp.exp2(-potential)
     weighted_rows(e_ref, q_ref, out_ref)
 
 
@@ -415,7 +420,10 @@
 
     def spread(value, axes):
         count = math.prod(sizes[axis] for axis in axes)
-        return [value] + [swap(value, axes, k) for k in range(1, count)]
+        order = list(range(1, count))
+        if "rep" not in axes:
+            order.sort(key=lambda k: (k % 4 == 2, k))
+        return [value] + [swap(value, axes, k) for k in order]
 
     bf16 = jnp.bfloat16
     over_source = ("col", "rep")
@@ -428,21 +436,20 @@
     columns = (BLOCK, TILE, LANES)
     hbm = pltpu.HBM
 
-    score, packed, meta, x, y, warm = call(
+    score, sums, x, y = call(
         first_source_kernel,
         "first_source",
         [
             (matrix, F32),
-            ((2 * BLOCK, 1, TILE), F32),
-            ((8, LANES), jnp.int32),
+            source_vector,
             ((BLOCK, TILE, width), bf16),
             ((BLOCK, HALF, width), bf16),
-            target_vector,
         ],
         [
             pltpu.SMEM(source_bounds.shape, jnp.int32),
             pltpu.SMEM(target_bounds.shape, jnp.int32),
             pltpu.SMEM(kept_pairs.shape[::-1], jnp.int32),
+            pltpu.VMEM(target_vector[0], F32),
             pltpu.SemaphoreType.DMA((4,)),
             pltpu.SemaphoreType.DMA((3,)),
         ],
@@ -456,23 +463,30 @@
         ],
         [hbm] * 6,
     )
-    parts = spread(packed, over_source)
+    parts = spread(sums, over_source)
     n_source = len(parts)
-    e, packed = call(
+    (own_peaks,) = call(
+        own_peaks_kernel,
+        "own_peaks",
+        [target_vector],
+        [pltpu.VMEM(columns, F32)],
+        [sums, score],
+    )
+    e, sums, shift = call(
         functools.partial(first_target_kernel, n_source),
         "first_target",
-        [(matrix, F32), ((2 * BLOCK, 1, HALF), F32)],
+        [(matrix, F32), target_vector, target_vector],
         [pltpu.VMEM(columns, F32)],
-        [*parts, score, meta],
-    )
-    parts = spread(packed, over_target)
+        [*parts, score, own_peaks],
+    )
+    parts = spread(sums, over_target)
     n_target = len(parts)
     sums, q, wq = call(
         functools.partial(second_source_kernel, n_target),
         "second_source",
         [source_vector, target_vector, target_vector],
         [],
-        [*parts, warm, e],
+        [*parts, shift, e],
     )
     parts = spread(sums, over_source)
     sums, a, a_column = call(
@@ -567,7 +581,7 @@
         [near, swap(far, ("rep",), 1)],
     )
     terms = [merged[0]] + [swap(merged[d], ("col",), d) for d in range(1, columns_of_chips)]
-    gathered = spread(target_rows, over_target)
+    gathered = [swap(target_rows, over_target, k) if k else target_rows for k in range(rows)]
     crossed = [swap(value, ("rep",), 1) for value in gathered]
     late_ones = [k for k in range(rows) if k // per_tile in (1, 2)]
     ranks = [(k, 0) for k in range(rows)]

time: 80.1 us -> 80.5 us (level)
  starting transfers between devices: 33.8 us -> 31.1 us
  Pallas kernels: 16.7 us -> 18.4 us
  waiting for transfers between devices: 28.3 us -> 29.8 us
    ppermute x33, starting transfers between devices: 33.8 us -> 31.1 us  [swap(): return lax.ppermute(value, axes, [(i, i ^ k) for i in range(count)])]
    pallas_call x13 -> x14, Pallas kernels: 14.9 us -> 16.6 us  [call(): pl.pallas_call(kernel, name=name, out_shape=[pltpu.VMEM(shape, dtype) for...]
    ppermute x33, waiting for transfers between devices: 28.3 us -> 29.8 us  [swap(): return lax.ppermute(value, axes, [(i, i ^ k) for i in range(count)])]
  transfers between devices with their start and end apart: 33 -> 33, of which waited for: 19 -> 19; matrix products, arithmetic and copies ran while one was open for 0% -> 0% of each run, Pallas kernels for 7% -> 8%
where the time goes in v5:
time: 80.5 us; the launch traced here: 80.4 us
  starting transfers between devices  31.1 us (39%)
  waiting for transfers between devices  29.8 us (37%)
  Pallas kernels  18.4 us (23%)
  between operations  0.97 us (1%)
    ppermute x33, starting transfers between devices, swap(): return lax.ppermute(value, axes, [(i, i ^ k) for i in range(count)])  31.1 us
    ppermute x33, waiting for transfers between devices, swap(): return lax.ppermute(value, axes, [(i, i ^ k) for i in range(count)])  29.8 us
    pallas_call x14, Pallas kernels, call(): pl.pallas_call(kernel, name=name, out_shape=[pltpu.VMEM(shape, dtype) for...  16.6 us
  transfers between devices with their start and end apart: 33, of which 19 were waited for; matrix products, arithmetic and copies ran while one was open for 0% of the time, Pallas kernels for 8%

profile of v5, /device:TPU:0, one launch (start us, length us, event | category | flops | bytes accessed | tf_op | source)
XLA Modules:
  0.0 80.4 jit_solution(10888536815162604753)
XLA Ops:
  0.6 3.8 %first_source.1 = (f32[4,512,1024]{2,1,0:T(8,128)S(1)}, f32[4,1,512]{2,1,0:T(1,128)S(1)}, bf16[4,512,256]{2,1,0:T(8,128)(2,1)S(1)}, bf16[4,256,256]{2,1,0:T(8,128)(2,1)S(1)}) custom-call(bf16[4,512,256]{2,1,0:T(8,128)(2,1)} %bitcast.8, bf16[4,2,256,256]{3,2,1,0:T(8,128)(2,1)} %bitcast.9, f32[4,2,1,256]{3,2,1,0:T(1,128)} %bitcast.10, s32[9]{0:T(128)} %sb_hbm.1, ...), custom_call_target="tpu_custom_call" | custom-call | tf_op jit(solution)/shard_map/first_source/pallas_call | solution.py:391
  4.5 2.4 %collective-permute-start.2 = (f32[4,1,512]{2,1,0:T(1,128)S(1)}, f32[4,1,512]{2,1,0:T(1,128)S(1)}, u32[]{:S(2)}, u32[]{:S(2)}) collective-permute-start(f32[4,1,512]{2,1,0:T(1,128)S(1)} %get-tuple-element.44.own_ref.args_0_), channel_id=1, source_target_pairs={{0,3},{1,2},{2,1},{3,0},{4,7},{5,6},{6,5},{7,4},{8,11},{9,10},{10,... | collective-permute-start | bytes 24584 | tf_op jit(solution)/shard_map/ppermute | solution.py:419
  8.3 2.3 %collective-permute-done.1.args_2_ = f32[4,1,512]{2,1,0:T(1,128)S(1)} collective-permute-done((f32[4,1,512]{2,1,0:T(1,128)S(1)}, f32[4,1,512]{2,1,0:T(1,128)S(1)}, u32[]{:S(2)}, u32[]{:S(2)}) %collective-permute-start.1) | collective-permute-done | bytes 8224 | tf_op jit(solution)/shard_map/ppermute | solution.py:419
  10.6 3.1 %first_target.1 = (f32[4,512,1024]{2,1,0:T(8,128)S(1)}, f32[4,1,256]{2,1,0:T(1,128)S(1)}, f32[4,1,256]{2,1,0:T(1,128)S(1)}) custom-call(f32[4,1,512]{2,1,0:T(1,128)S(1)} %get-tuple-element.44.own_ref.args_0_, f32[4,1,512]{2,1,0:T(1,128)S(1)} %collective-permute-done.args_1_, f32[4,1,512]{2,1,0:T(1,128)S(1)} %collective-permute-done.1.args_2_, ...), custom_call_target="tpu_custom_call" | custom-call | tf_op jit(solution)/shard_map/first_target/pallas_call | solution.py:391
  13.7 2.7 %collective-permute-start.5 = (f32[4,1,256]{2,1,0:T(1,128)S(1)}, f32[4,1,256]{2,1,0:T(1,128)S(1)}, u32[]{:S(2)}, u32[]{:S(2)}) collective-permute-start(f32[4,1,256]{2,1,0:T(1,128)S(1)} %get-tuple-element.47.args_0_), channel_id=1, source_target_pairs={{0,8},{4,12},{8,0},{12,4},{1,9},{5,13},{9,1},{13,5},{2,10},{6,14},... | collective-permute-start | bytes 12296 | tf_op jit(solution)/shard_map/ppermute | solution.py:419
  16.3 1.3 %collective-permute-start.4 = (f32[4,1,256]{2,1,0:T(1,128)S(1)}, f32[4,1,256]{2,1,0:T(1,128)S(1)}, u32[]{:S(2)}, u32[]{:S(2)}) collective-permute-start(f32[4,1,256]{2,1,0:T(1,128)S(1)} %get-tuple-element.47.args_0_), channel_id=1, source_target_pairs={{0,12},{4,8},{8,4},{12,0},{1,13},{5,9},{9,5},{13,1},{2,14},{6,10},... | collective-permute-start | bytes 12296 | tf_op jit(solution)/shard_map/ppermute | solution.py:419
  18.3 3.5 %collective-permute-done.4.args_2_ = f32[4,1,256]{2,1,0:T(1,128)S(1)} collective-permute-done((f32[4,1,256]{2,1,0:T(1,128)S(1)}, f32[4,1,256]{2,1,0:T(1,128)S(1)}, u32[]{:S(2)}, u32[]{:S(2)}) %collective-permute-start.4) | collective-permute-done | bytes 4128 | tf_op jit(solution)/shard_map/ppermute | solution.py:419
  23.2 1.1 %collective-permute-start.6 = (f32[4,1,512]{2,1,0:T(1,128)S(1)}, f32[4,1,512]{2,1,0:T(1,128)S(1)}, u32[]{:S(2)}, u32[]{:S(2)}) collective-permute-start(f32[4,1,512]{2,1,0:T(1,128)S(1)} %get-tuple-element.49.args_0_), channel_id=1, source_target_pairs={{0,1},{1,0},{2,3},{3,2},{4,5},{5,4},{6,7},{7,6},{8,9},{9,8},{10,11... | collective-permute-start | bytes 24584 | tf_op jit(solution)/shard_map/ppermute | solution.py:419
  24.3 1.2 %collective-permute-done.8.args_3_ = f32[4,1,512]{2,1,0:T(1,128)S(1)} collective-permute-done((f32[4,1,512]{2,1,0:T(1,128)S(1)}, f32[4,1,512]{2,1,0:T(1,128)S(1)}, u32[]{:S(2)}, u32[]{:S(2)}) %collective-permute-start.8) | collective-permute-done | bytes 8224 | tf_op jit(solution)/shard_map/ppermute | solution.py:419
  26.9 1.3 %collective-permute-start.11 = (f32[4,1,256]{2,1,0:T(1,128)S(1)}, f32[4,1,256]{2,1,0:T(1,128)S(1)}, u32[]{:S(2)}, u32[]{:S(2)}) collective-permute-start(f32[4,1,256]{2,1,0:T(1,128)S(1)} %get-tuple-element.52.args_0_), channel_id=1, source_target_pairs={{0,8},{4,12},{8,0},{12,4},{1,9},{5,13},{9,1},{13,5},{2,10},{6,14},... | collective-permute-start | bytes 12296 | tf_op jit(solution)/shard_map/ppermute | solution.py:419
  29.1 1.3 %collective-permute-start.9 = (f32[4,1,256]{2,1,0:T(1,128)S(1)}, f32[4,1,256]{2,1,0:T(1,128)S(1)}, u32[]{:S(2)}, u32[]{:S(2)}) collective-permute-start(f32[4,1,256]{2,1,0:T(1,128)S(1)} %get-tuple-element.52.args_0_), channel_id=1, source_target_pairs={{0,4},{4,0},{8,12},{12,8},{1,5},{5,1},{9,13},{13,9},{2,6},{6,2},{1... | collective-permute-start | bytes 12296 | tf_op jit(solution)/shard_map/ppermute | solution.py:419
  31.4 2.1 %collective-permute-done.10.args_2_ = f32[4,1,256]{2,1,0:T(1,128)S(1)} collective-permute-done((f32[4,1,256]{2,1,0:T(1,128)S(1)}, f32[4,1,256]{2,1,0:T(1,128)S(1)}, u32[]{:S(2)}, u32[]{:S(2)}) %collective-permute-start.10) | collective-permute-done | bytes 4128 | tf_op jit(solution)/shard_map/ppermute | solution.py:419
  35.0 1.1 %collective-permute-start.12 = (f32[4,1,512]{2,1,0:T(1,128)S(1)}, f32[4,1,512]{2,1,0:T(1,128)S(1)}, u32[]{:S(2)}, u32[]{:S(2)}) collective-permute-start(f32[4,1,512]{2,1,0:T(1,128)S(1)} %get-tuple-element.53.args_0_), channel_id=1, source_target_pairs={{0,1},{1,0},{2,3},{3,2},{4,5},{5,4},{6,7},{7,6},{8,9},{9,8},{10,11... | collective-permute-start | bytes 24584 | tf_op jit(solution)/shard_map/ppermute | solution.py:419
  36.2 1.2 %collective-permute-done.14.args_3_ = f32[4,1,512]{2,1,0:T(1,128)S(1)} collective-permute-done((f32[4,1,512]{2,1,0:T(1,128)S(1)}, f32[4,1,512]{2,1,0:T(1,128)S(1)}, u32[]{:S(2)}, u32[]{:S(2)}) %collective-permute-start.14) | collective-permute-done | bytes 8224 | tf_op jit(solution)/shard_map/ppermute | solution.py:419
  38.7 1.1 %collective-permute-start.17 = (f32[4,1,256]{2,1,0:T(1,128)S(1)}, f32[4,1,256]{2,1,0:T(1,128)S(1)}, u32[]{:S(2)}, u32[]{:S(2)}) collective-permute-start(f32[4,1,256]{2,1,0:T(1,128)S(1)} %get-tuple-element.57.args_0_), channel_id=1, source_target_pairs={{0,8},{4,12},{8,0},{12,4},{1,9},{5,13},{9,1},{13,5},{2,10},{6,14},... | collective-permute-start | bytes 12296 | tf_op jit(solution)/shard_map/ppermute | solution.py:419
  39.8 1.8 %collective-permute-start.16 = (f32[4,1,256]{2,1,0:T(1,128)S(1)}, f32[4,1,256]{2,1,0:T(1,128)S(1)}, u32[]{:S(2)}, u32[]{:S(2)}) collective-permute-start(f32[4,1,256]{2,1,0:T(1,128)S(1)} %get-tuple-element.57.args_0_), channel_id=1, source_target_pairs={{0,12},{4,8},{8,4},{12,0},{1,13},{5,9},{9,5},{13,1},{2,14},{6,10},... | collective-permute-start | bytes 12296 | tf_op jit(solution)/shard_map/ppermute | solution.py:419
  43.3 1.9 %collective-permute-done.16.args_2_ = f32[4,1,256]{2,1,0:T(1,128)S(1)} collective-permute-done((f32[4,1,256]{2,1,0:T(1,128)S(1)}, f32[4,1,256]{2,1,0:T(1,128)S(1)}, u32[]{:S(2)}, u32[]{:S(2)}) %collective-permute-start.16) | collective-permute-done | bytes 4128 | tf_op jit(solution)/shard_map/ppermute | solution.py:419
  46.7 1.1 %collective-permute-start.18 = (f32[4,1,512]{2,1,0:T(1,128)S(1)}, f32[4,1,512]{2,1,0:T(1,128)S(1)}, u32[]{:S(2)}, u32[]{:S(2)}) collective-permute-start(f32[4,1,512]{2,1,0:T(1,128)S(1)} %get-tuple-element.60.args_0_), channel_id=1, source_target_pairs={{0,1},{1,0},{2,3},{3,2},{4,5},{5,4},{6,7},{7,6},{8,9},{9,8},{10,11... | collective-permute-start | bytes 24584 | tf_op jit(solution)/shard_map/ppermute | solution.py:419
  47.8 1.2 %collective-permute-done.20.args_3_ = f32[4,1,512]{2,1,0:T(1,128)S(1)} collective-permute-done((f32[4,1,512]{2,1,0:T(1,128)S(1)}, f32[4,1,512]{2,1,0:T(1,128)S(1)}, u32[]{:S(2)}, u32[]{:S(2)}) %collective-permute-start.20) | collective-permute-done | bytes 8224 | tf_op jit(solution)/shard_map/ppermute | solution.py:419
  49.7 1.1 %target_gradient_3.1 = (bf16[4,512,1024]{2,1,0:T(8,128)(2,1)S(1)}, f32[4,512,128]{2,1,0:T(8,128)S(1)}, bf16[256,256]{1,0:T(8,128)(2,1)S(1)}) custom-call(f32[4,1,512]{2,1,0:T(1,128)S(1)} %get-tuple-element.60.args_0_, f32[4,1,512]{2,1,0:T(1,128)S(1)} %collective-permute-done.18.args_1_, f32[4,1,512]{2,1,0:T(1,128)S(1)} %collective-permute-done.19.args_2_, ...), custom_call_target="tpu_custom_call" | custom-call | tf_op jit(solution)/shard_map/target_gradient_3/pallas_call | solution.py:391
  50.8 2.0 %collective-permute-start.21 = (bf16[256,256]{1,0:T(8,128)(2,1)S(1)}, bf16[256,256]{1,0:T(8,128)(2,1)S(1)}, u32[]{:S(2)}, u32[]{:S(2)}) collective-permute-start(bf16[256,256]{1,0:T(8,128)(2,1)S(1)} %get-tuple-element.65), channel_id=1, source_target_pairs={{0,12},{4,8},{8,4},{12,0},{1,13},{5,9},{9,5},{13,1},{2,14},{6,10},... | collective-permute-start | bytes 393224 | tf_op jit(solution)/shard_map/ppermute | solution.py:419
  53.9 1.0 %target_gradient_1.1 = (bf16[4,512,1024]{2,1,0:T(8,128)(2,1)S(1)}, bf16[256,256]{1,0:T(8,128)(2,1)S(1)}) custom-call(bf16[4,512,256]{2,1,0:T(8,128)(2,1)S(1)} %get-tuple-element.43.args_4_.args_0_, f32[4,512,1024]{2,1,0:T(8,128)S(1)} %get-tuple-element.46.args_5_.args_4_.args_1_, ...), custom_call_target="tpu_custom_call", output_to_operand_aliasing={{0}: (9, {})} | custom-call | tf_op jit(solution)/shard_map/target_gradient_1/pallas_call | solution.py:391
  55.0 2.4 %collective-permute-start.23 = (bf16[256,256]{1,0:T(8,128)(2,1)S(1)}, bf16[256,256]{1,0:T(8,128)(2,1)S(1)}, u32[]{:S(2)}, u32[]{:S(2)}) collective-permute-start(bf16[256,256]{1,0:T(8,128)(2,1)S(1)} %get-tuple-element.69), channel_id=1, source_target_pairs={{0,8},{4,12},{8,0},{12,4},{1,9},{5,13},{9,1},{13,5},{2,10},{6,14},... | collective-permute-start | bytes 393224 | tf_op jit(solution)/shard_map/ppermute | solution.py:419
  59.5 1.4 %source_gradient.1 = (f32[2,512,256]{2,1,0:T(8,128)S(1)}, bf16[2,512,256]{2,1,0:T(8,128)(2,1)S(1)}) custom-call(bf16[4,512,1024]{2,1,0:T(8,128)(2,1)S(1)} %get-tuple-element.71.bar_ref, bf16[4,256,256]{2,1,0:T(8,128)(2,1)S(1)} %get-tuple-element.72.y_ref), custom_call_target="tpu_custom_call" | custom-call | tf_op jit(solution)/shard_map/source_gradient/pallas_call | solution.py:391
  60.9 1.5 %collective-permute-done.22 = bf16[256,256]{1,0:T(8,128)(2,1)S(1)} collective-permute-done((bf16[256,256]{1,0:T(8,128)(2,1)S(1)}, bf16[256,256]{1,0:T(8,128)(2,1)S(1)}, u32[]{:S(2)}, u32[]{:S(2)}) %collective-permute-start.22) | collective-permute-done | bytes 131104 | tf_op jit(solution)/shard_map/ppermute | solution.py:419
  62.4 1.9 %collective-permute-done.23 = bf16[256,256]{1,0:T(8,128)(2,1)S(1)} collective-permute-done((bf16[256,256]{1,0:T(8,128)(2,1)S(1)}, bf16[256,256]{1,0:T(8,128)(2,1)S(1)}, u32[]{:S(2)}, u32[]{:S(2)}) %collective-permute-start.23) | collective-permute-done | bytes 131104 | tf_op jit(solution)/shard_map/ppermute | solution.py:419
  64.4 2.1 %collective-permute-start.26 = (bf16[256,256]{1,0:T(8,128)(2,1)S(1)}, bf16[256,256]{1,0:T(8,128)(2,1)S(1)}, u32[]{:S(2)}, u32[]{:S(2)}) collective-permute-start(bf16[256,256]{1,0:T(8,128)(2,1)S(1)} %add_convert_fusion.args_0_), channel_id=1, source_target_pairs={{0,12},{4,8},{8,4},{12,0},{1,13},{5,9},{9,5},{13,1},{2,14},{6,10},... | collective-permute-start | bytes 393224 | tf_op jit(solution)/shard_map/ppermute | solution.py:419
  66.6 1.4 %collective-permute-start.30 = (bf16[512,256]{1,0:T(8,128)(2,1)S(1)}, bf16[512,256]{1,0:T(8,128)(2,1)S(1)}, u32[]{:S(2)}, u32[]{:S(2)}) collective-permute-start(bf16[512,256]{1,0:T(8,128)(2,1)S(1)} %get-tuple-element.81), channel_id=1, source_target_pairs={{0,2},{2,0},{1,3},{3,1},{4,6},{6,4},{5,7},{7,5},{8,10},{10,8},{9,1... | collective-permute-start | bytes 786440 | tf_op jit(solution)/shard_map/ppermute | solution.py:419
  68.1 2.3 %collective-permute-start.24 = (bf16[256,256]{1,0:T(8,128)(2,1)S(1)}, bf16[256,256]{1,0:T(8,128)(2,1)S(1)}, u32[]{:S(2)}, u32[]{:S(2)}) collective-permute-start(bf16[256,256]{1,0:T(8,128)(2,1)S(1)} %add_convert_fusion.args_0_), channel_id=1, source_target_pairs={{0,4},{4,0},{8,12},{12,8},{1,5},{5,1},{9,13},{13,9},{2,6},{6,2},{1... | collective-permute-start | bytes 393224 | tf_op jit(solution)/shard_map/ppermute | solution.py:419
  70.4 2.3 %collective-permute-done.26.args_3_ = bf16[256,256]{1,0:T(8,128)(2,1)S(1)} collective-permute-done((bf16[256,256]{1,0:T(8,128)(2,1)S(1)}, bf16[256,256]{1,0:T(8,128)(2,1)S(1)}, u32[]{:S(2)}, u32[]{:S(2)}) %collective-permute-start.26) | collective-permute-done | bytes 131104 | tf_op jit(solution)/shard_map/ppermute | solution.py:419
  72.7 5.2 %collective-permute-done.25.args_2_ = bf16[256,256]{1,0:T(8,128)(2,1)S(1)} collective-permute-done((bf16[256,256]{1,0:T(8,128)(2,1)S(1)}, bf16[256,256]{1,0:T(8,128)(2,1)S(1)}, u32[]{:S(2)}, u32[]{:S(2)}) %collective-permute-start.25) | collective-permute-done | bytes 131104 | tf_op jit(solution)/shard_map/ppermute | solution.py:419
  78.4 1.0 %finish.1 = (bf16[512,256]{1,0:T(8,128)(2,1)}, bf16[2048,256]{1,0:T(8,128)(2,1)}) custom-call(bf16[256,256]{1,0:T(8,128)(2,1)S(1)} %add_convert_fusion.args_0_, bf16[256,256]{1,0:T(8,128)(2,1)S(1)} %collective-permute-done.24.args_1_, bf16[256,256]{1,0:T(8,128)(2,1)S(1)} %collective-permute-done.25.args_2_, ...), custom_call_target="tpu_custom_call" | custom-call | tf_op jit(solution)/shard_map/finish/pallas_call | solution.py:594
  (55 shorter events, 17.7 us)
Async XLA Ops:
  4.5 3.8 %collective-permute-start.2 = (f32[4,1,512]{2,1,0:T(1,128)S(1)}, f32[4,1,512]{2,1,0:T(1,128)S(1)}, u32[]{:S(2)}, u32[]{:S(2)}) collective-permute-start(f32[4,1,512]{2,1,0:T(1,128)S(1)} %get-tuple-element.44.own_ref.args_0_), channel_id=1, source_target_pairs={{0,3},{1,2},{2,1},{3,0},{4,7},{5,6},{6,5},{7,4},{8,11},{9,10},{10,... | collective-permute-start | bytes 24584 | tf_op jit(solution)/shard_map/ppermute | solution.py:419
  6.9 3.7 %collective-permute-start.1 = (f32[4,1,512]{2,1,0:T(1,128)S(1)}, f32[4,1,512]{2,1,0:T(1,128)S(1)}, u32[]{:S(2)}, u32[]{:S(2)}) collective-permute-start(f32[4,1,512]{2,1,0:T(1,128)S(1)} %get-tuple-element.44.own_ref.args_0_), channel_id=1, source_target_pairs={{0,2},{1,3},{2,0},{3,1},{4,6},{5,7},{6,4},{7,5},{8,10},{9,11},{10,... | collective-permute-start | bytes 24584 | tf_op jit(solution)/shard_map/ppermute | solution.py:419
  7.6 3.0 %collective-permute-start = (f32[4,1,512]{2,1,0:T(1,128)S(1)}, f32[4,1,512]{2,1,0:T(1,128)S(1)}, u32[]{:S(2)}, u32[]{:S(2)}) collective-permute-start(f32[4,1,512]{2,1,0:T(1,128)S(1)} %get-tuple-element.44.own_ref.args_0_), channel_id=1, source_target_pairs={{0,1},{1,0},{2,3},{3,2},{4,5},{5,4},{6,7},{7,6},{8,9},{9,8},{10,11... | collective-permute-start | bytes 24584 | tf_op jit(solution)/shard_map/ppermute | solution.py:419
  13.7 4.6 %collective-permute-start.5 = (f32[4,1,256]{2,1,0:T(1,128)S(1)}, f32[4,1,256]{2,1,0:T(1,128)S(1)}, u32[]{:S(2)}, u32[]{:S(2)}) collective-permute-start(f32[4,1,256]{2,1,0:T(1,128)S(1)} %get-tuple-element.47.args_0_), channel_id=1, source_target_pairs={{0,8},{4,12},{8,0},{12,4},{1,9},{5,13},{9,1},{13,5},{2,10},{6,14},... | collective-permute-start | bytes 12296 | tf_op jit(solution)/shard_map/ppermute | solution.py:419
  16.3 5.4 %collective-permute-start.4 = (f32[4,1,256]{2,1,0:T(1,128)S(1)}, f32[4,1,256]{2,1,0:T(1,128)S(1)}, u32[]{:S(2)}, u32[]{:S(2)}) collective-permute-start(f32[4,1,256]{2,1,0:T(1,128)S(1)} %get-tuple-element.47.args_0_), channel_id=1, source_target_pairs={{0,12},{4,8},{8,4},{12,0},{1,13},{5,9},{9,5},{13,1},{2,14},{6,10},... | collective-permute-start | bytes 12296 | tf_op jit(solution)/shard_map/ppermute | solution.py:419
  17.7 4.1 %collective-permute-start.3 = (f32[4,1,256]{2,1,0:T(1,128)S(1)}, f32[4,1,256]{2,1,0:T(1,128)S(1)}, u32[]{:S(2)}, u32[]{:S(2)}) collective-permute-start(f32[4,1,256]{2,1,0:T(1,128)S(1)} %get-tuple-element.47.args_0_), channel_id=1, source_target_pairs={{0,4},{4,0},{8,12},{12,8},{1,5},{5,1},{9,13},{13,9},{2,6},{6,2},{1... | collective-permute-start | bytes 12296 | tf_op jit(solution)/shard_map/ppermute | solution.py:419
  22.4 3.1 %collective-permute-start.8 = (f32[4,1,512]{2,1,0:T(1,128)S(1)}, f32[4,1,512]{2,1,0:T(1,128)S(1)}, u32[]{:S(2)}, u32[]{:S(2)}) collective-permute-start(f32[4,1,512]{2,1,0:T(1,128)S(1)} %get-tuple-element.49.args_0_), channel_id=1, source_target_pairs={{0,3},{1,2},{2,1},{3,0},{4,7},{5,6},{6,5},{7,4},{8,11},{9,10},{10,... | collective-permute-start | bytes 24584 | tf_op jit(solution)/shard_map/ppermute | solution.py:419
  22.5 3.7 %collective-permute-start.7 = (f32[4,1,512]{2,1,0:T(1,128)S(1)}, f32[4,1,512]{2,1,0:T(1,128)S(1)}, u32[]{:S(2)}, u32[]{:S(2)}) collective-permute-start(f32[4,1,512]{2,1,0:T(1,128)S(1)} %get-tuple-element.49.args_0_), channel_id=1, source_target_pairs={{0,2},{1,3},{2,0},{3,1},{4,6},{5,7},{6,4},{7,5},{8,10},{9,11},{10,... | collective-permute-start | bytes 24584 | tf_op jit(solution)/shard_map/ppermute | solution.py:419
  23.2 3.0 %collective-permute-start.6 = (f32[4,1,512]{2,1,0:T(1,128)S(1)}, f32[4,1,512]{2,1,0:T(1,128)S(1)}, u32[]{:S(2)}, u32[]{:S(2)}) collective-permute-start(f32[4,1,512]{2,1,0:T(1,128)S(1)} %get-tuple-element.49.args_0_), channel_id=1, source_target_pairs={{0,1},{1,0},{2,3},{3,2},{4,5},{5,4},{6,7},{7,6},{8,9},{9,8},{10,11... | collective-permute-start | bytes 24584 | tf_op jit(solution)/shard_map/ppermute | solution.py:419
  26.9 4.6 %collective-permute-start.11 = (f32[4,1,256]{2,1,0:T(1,128)S(1)}, f32[4,1,256]{2,1,0:T(1,128)S(1)}, u32[]{:S(2)}, u32[]{:S(2)}) collective-permute-start(f32[4,1,256]{2,1,0:T(1,128)S(1)} %get-tuple-element.52.args_0_), channel_id=1, source_target_pairs={{0,8},{4,12},{8,0},{12,4},{1,9},{5,13},{9,1},{13,5},{2,10},{6,14},... | collective-permute-start | bytes 12296 | tf_op jit(solution)/shard_map/ppermute | solution.py:419
  28.2 5.4 %collective-permute-start.10 = (f32[4,1,256]{2,1,0:T(1,128)S(1)}, f32[4,1,256]{2,1,0:T(1,128)S(1)}, u32[]{:S(2)}, u32[]{:S(2)}) collective-permute-start(f32[4,1,256]{2,1,0:T(1,128)S(1)} %get-tuple-element.52.args_0_), channel_id=1, source_target_pairs={{0,12},{4,8},{8,4},{12,0},{1,13},{5,9},{9,5},{13,1},{2,14},{6,10},... | collective-permute-start | bytes 12296 | tf_op jit(solution)/shard_map/ppermute | solution.py:419
  29.1 4.5 %collective-permute-start.9 = (f32[4,1,256]{2,1,0:T(1,128)S(1)}, f32[4,1,256]{2,1,0:T(1,128)S(1)}, u32[]{:S(2)}, u32[]{:S(2)}) collective-permute-start(f32[4,1,256]{2,1,0:T(1,128)S(1)} %get-tuple-element.52.args_0_), channel_id=1, source_target_pairs={{0,4},{4,0},{8,12},{12,8},{1,5},{5,1},{9,13},{13,9},{2,6},{6,2},{1... | collective-permute-start | bytes 12296 | tf_op jit(solution)/shard_map/ppermute | solution.py:419
  34.2 3.1 %collective-permute-start.14 = (f32[4,1,512]{2,1,0:T(1,128)S(1)}, f32[4,1,512]{2,1,0:T(1,128)S(1)}, u32[]{:S(2)}, u32[]{:S(2)}) collective-permute-start(f32[4,1,512]{2,1,0:T(1,128)S(1)} %get-tuple-element.53.args_0_), channel_id=1, source_target_pairs={{0,3},{1,2},{2,1},{3,0},{4,7},{5,6},{6,5},{7,4},{8,11},{9,10},{10,... | collective-permute-start | bytes 24584 | tf_op jit(solution)/shard_map/ppermute | solution.py:419
  34.3 3.7 %collective-permute-start.13 = (f32[4,1,512]{2,1,0:T(1,128)S(1)}, f32[4,1,512]{2,1,0:T(1,128)S(1)}, u32[]{:S(2)}, u32[]{:S(2)}) collective-permute-start(f32[4,1,512]{2,1,0:T(1,128)S(1)} %get-tuple-element.53.args_0_), channel_id=1, source_target_pairs={{0,2},{1,3},{2,0},{3,1},{4,6},{5,7},{6,4},{7,5},{8,10},{9,11},{10,... | collective-permute-start | bytes 24584 | tf_op jit(solution)/shard_map/ppermute | solution.py:419
  35.0 3.0 %collective-permute-start.12 = (f32[4,1,512]{2,1,0:T(1,128)S(1)}, f32[4,1,512]{2,1,0:T(1,128)S(1)}, u32[]{:S(2)}, u32[]{:S(2)}) collective-permute-start(f32[4,1,512]{2,1,0:T(1,128)S(1)} %get-tuple-element.53.args_0_), channel_id=1, source_target_pairs={{0,1},{1,0},{2,3},{3,2},{4,5},{5,4},{6,7},{7,6},{8,9},{9,8},{10,11... | collective-permute-start | bytes 24584 | tf_op jit(solution)/shard_map/ppermute | solution.py:419
  38.7 4.6 %collective-permute-start.17 = (f32[4,1,256]{2,1,0:T(1,128)S(1)}, f32[4,1,256]{2,1,0:T(1,128)S(1)}, u32[]{:S(2)}, u32[]{:S(2)}) collective-permute-start(f32[4,1,256]{2,1,0:T(1,128)S(1)} %get-tuple-element.57.args_0_), channel_id=1, source_target_pairs={{0,8},{4,12},{8,0},{12,4},{1,9},{5,13},{9,1},{13,5},{2,10},{6,14},... | collective-permute-start | bytes 12296 | tf_op jit(solution)/shard_map/ppermute | solution.py:419
  39.8 5.4 %collective-permute-start.16 = (f32[4,1,256]{2,1,0:T(1,128)S(1)}, f32[4,1,256]{2,1,0:T(1,128)S(1)}, u32[]{:S(2)}, u32[]{:S(2)}) collective-permute-start(f32[4,1,256]{2,1,0:T(1,128)S(1)} %get-tuple-element.57.args_0_), channel_id=1, source_target_pairs={{0,12},{4,8},{8,4},{12,0},{1,13},{5,9},{9,5},{13,1},{2,14},{6,10},... | collective-permute-start | bytes 12296 | tf_op jit(solution)/shard_map/ppermute | solution.py:419
  41.6 3.6 %collective-permute-start.15 = (f32[4,1,256]{2,1,0:T(1,128)S(1)}, f32[4,1,256]{2,1,0:T(1,128)S(1)}, u32[]{:S(2)}, u32[]{:S(2)}) collective-permute-start(f32[4,1,256]{2,1,0:T(1,128)S(1)} %get-tuple-element.57.args_0_), channel_id=1, source_target_pairs={{0,4},{4,0},{8,12},{12,8},{1,5},{5,1},{9,13},{13,9},{2,6},{6,2},{1... | collective-permute-start | bytes 12296 | tf_op jit(solution)/shard_map/ppermute | solution.py:419
  45.9 3.1 %collective-permute-start.20 = (f32[4,1,512]{2,1,0:T(1,128)S(1)}, f32[4,1,512]{2,1,0:T(1,128)S(1)}, u32[]{:S(2)}, u32[]{:S(2)}) collective-permute-start(f32[4,1,512]{2,1,0:T(1,128)S(1)} %get-tuple-element.60.args_0_), channel_id=1, source_target_pairs={{0,3},{1,2},{2,1},{3,0},{4,7},{5,6},{6,5},{7,4},{8,11},{9,10},{10,... | collective-permute-start | bytes 24584 | tf_op jit(solution)/shard_map/ppermute | solution.py:419
  46.0 3.7 %collective-permute-start.19 = (f32[4,1,512]{2,1,0:T(1,128)S(1)}, f32[4,1,512]{2,1,0:T(1,128)S(1)}, u32[]{:S(2)}, u32[]{:S(2)}) collective-permute-start(f32[4,1,512]{2,1,0:T(1,128)S(1)} %get-tuple-element.60.args_0_), channel_id=1, source_target_pairs={{0,2},{1,3},{2,0},{3,1},{4,6},{5,7},{6,4},{7,5},{8,10},{9,11},{10,... | collective-permute-start | bytes 24584 | tf_op jit(solution)/shard_map/ppermute | solution.py:419
  46.7 3.0 %collective-permute-start.18 = (f32[4,1,512]{2,1,0:T(1,128)S(1)}, f32[4,1,512]{2,1,0:T(1,128)S(1)}, u32[]{:S(2)}, u32[]{:S(2)}) collective-permute-start(f32[4,1,512]{2,1,0:T(1,128)S(1)} %get-tuple-element.60.args_0_), channel_id=1, source_target_pairs={{0,1},{1,0},{2,3},{3,2},{4,5},{5,4},{6,7},{7,6},{8,9},{9,8},{10,11... | collective-permute-start | bytes 24584 | tf_op jit(solution)/shard_map/ppermute | solution.py:419
  50.8 7.6 %collective-permute-start.21 = (bf16[256,256]{1,0:T(8,128)(2,1)S(1)}, bf16[256,256]{1,0:T(8,128)(2,1)S(1)}, u32[]{:S(2)}, u32[]{:S(2)}) collective-permute-start(bf16[256,256]{1,0:T(8,128)(2,1)S(1)} %get-tuple-element.65), channel_id=1, source_target_pairs={{0,12},{4,8},{8,4},{12,0},{1,13},{5,9},{9,5},{13,1},{2,14},{6,10},... | collective-permute-start | bytes 393224 | tf_op jit(solution)/shard_map/ppermute | solution.py:419
  54.9 7.5 %collective-permute-start.22 = (bf16[256,256]{1,0:T(8,128)(2,1)S(1)}, bf16[256,256]{1,0:T(8,128)(2,1)S(1)}, u32[]{:S(2)}, u32[]{:S(2)}) collective-permute-start(bf16[256,256]{1,0:T(8,128)(2,1)S(1)} %get-tuple-element.68), channel_id=1, source_target_pairs={{0,4},{4,0},{8,12},{12,8},{1,5},{5,1},{9,13},{13,9},{2,6},{6,2},{1... | collective-permute-start | bytes 393224 | tf_op jit(solution)/shard_map/ppermute | solution.py:419
  55.0 9.3 %collective-permute-start.23 = (bf16[256,256]{1,0:T(8,128)(2,1)S(1)}, bf16[256,256]{1,0:T(8,128)(2,1)S(1)}, u32[]{:S(2)}, u32[]{:S(2)}) collective-permute-start(bf16[256,256]{1,0:T(8,128)(2,1)S(1)} %get-tuple-element.69), channel_id=1, source_target_pairs={{0,8},{4,12},{8,0},{12,4},{1,9},{5,13},{9,1},{13,5},{2,10},{6,14},... | collective-permute-start | bytes 393224 | tf_op jit(solution)/shard_map/ppermute | solution.py:419
  64.3 2.2 %collective-permute-start.29 = (bf16[2,512,256]{2,1,0:T(8,128)(2,1)S(1)}, bf16[2,512,256]{2,1,0:T(8,128)(2,1)S(1)}, u32[]{:S(2)}, u32[]{:S(2)}) collective-permute-start(bf16[2,512,256]{2,1,0:T(8,128)(2,1)S(1)} %get-tuple-element.79), channel_id=1, source_target_pairs={{0,1},{1,0},{2,3},{3,2},{4,5},{5,4},{6,7},{7,6},{8,9},{9,8},{10,11... | collective-permute-start | bytes 1572872 | tf_op jit(solution)/shard_map/ppermute | solution.py:419
  64.4 8.3 %collective-permute-start.26 = (bf16[256,256]{1,0:T(8,128)(2,1)S(1)}, bf16[256,256]{1,0:T(8,128)(2,1)S(1)}, u32[]{:S(2)}, u32[]{:S(2)}) collective-permute-start(bf16[256,256]{1,0:T(8,128)(2,1)S(1)} %add_convert_fusion.args_0_), channel_id=1, source_target_pairs={{0,12},{4,8},{8,4},{12,0},{1,13},{5,9},{9,5},{13,1},{2,14},{6,10},... | collective-permute-start | bytes 393224 | tf_op jit(solution)/shard_map/ppermute | solution.py:419
  66.6 11.8 %collective-permute-start.30 = (bf16[512,256]{1,0:T(8,128)(2,1)S(1)}, bf16[512,256]{1,0:T(8,128)(2,1)S(1)}, u32[]{:S(2)}, u32[]{:S(2)}) collective-permute-start(bf16[512,256]{1,0:T(8,128)(2,1)S(1)} %get-tuple-element.81), channel_id=1, source_target_pairs={{0,2},{2,0},{1,3},{3,1},{4,6},{6,4},{5,7},{7,5},{8,10},{10,8},{9,1... | collective-permute-start | bytes 786440 | tf_op jit(solution)/shard_map/ppermute | solution.py:419
  68.1 9.8 %collective-permute-start.25 = (bf16[256,256]{1,0:T(8,128)(2,1)S(1)}, bf16[256,256]{1,0:T(8,128)(2,1)S(1)}, u32[]{:S(2)}, u32[]{:S(2)}) collective-permute-start(bf16[256,256]{1,0:T(8,128)(2,1)S(1)} %add_convert_fusion.args_0_), channel_id=1, source_target_pairs={{0,8},{4,12},{8,0},{12,4},{1,9},{5,13},{9,1},{13,5},{2,10},{6,14},... | collective-permute-start | bytes 393224 | tf_op jit(solution)/shard_map/ppermute | solution.py:419
  68.1 9.9 %collective-permute-start.24 = (bf16[256,256]{1,0:T(8,128)(2,1)S(1)}, bf16[256,256]{1,0:T(8,128)(2,1)S(1)}, u32[]{:S(2)}, u32[]{:S(2)}) collective-permute-start(bf16[256,256]{1,0:T(8,128)(2,1)S(1)} %add_convert_fusion.args_0_), channel_id=1, source_target_pairs={{0,4},{4,0},{8,12},{12,8},{1,5},{5,1},{9,13},{13,9},{2,6},{6,2},{1... | collective-permute-start | bytes 393224 | tf_op jit(solution)/shard_map/ppermute | solution.py:419
  70.4 8.0 %collective-permute-start.27 = (bf16[256,256]{1,0:T(8,128)(2,1)S(1)}, bf16[256,256]{1,0:T(8,128)(2,1)S(1)}, u32[]{:S(2)}, u32[]{:S(2)}) collective-permute-start(bf16[256,256]{1,0:T(8,128)(2,1)S(1)} %add_convert_fusion.args_0_), channel_id=1, source_target_pairs={{0,1},{1,0},{2,3},{3,2},{4,5},{5,4},{6,7},{7,6},{8,9},{9,8},{10,11... | collective-permute-start | bytes 393224 | tf_op jit(solution)/shard_map/ppermute | solution.py:419
  72.7 5.7 %collective-permute-start.28 = (bf16[256,256]{1,0:T(8,128)(2,1)S(1)}, bf16[256,256]{1,0:T(8,128)(2,1)S(1)}, u32[]{:S(2)}, u32[]{:S(2)}) collective-permute-start(bf16[256,256]{1,0:T(8,128)(2,1)S(1)} %collective-permute-done.26.args_3_), channel_id=1, source_target_pairs={{0,1},{1,0},{2,3},{3,2},{4,5},{5,4},{6,7},{7,6},{8,9},{9,8},{10,11... | collective-permute-start | bytes 393224 | tf_op jit(solution)/shard_map/ppermute | solution.py:419
  77.9 1.6 %collective-permute-start.32 = (bf16[256,256]{1,0:T(8,128)(2,1)S(1)}, bf16[256,256]{1,0:T(8,128)(2,1)S(1)}, u32[]{:S(2)}, u32[]{:S(2)}) collective-permute-start(bf16[256,256]{1,0:T(8,128)(2,1)S(1)} %collective-permute-done.25.args_2_), channel_id=1, source_target_pairs={{0,1},{1,0},{2,3},{3,2},{4,5},{5,4},{6,7},{7,6},{8,9},{9,8},{10,11... | collective-permute-start | bytes 393224 | tf_op jit(solution)/shard_map/ppermute | solution.py:419
  (3 other events, 13.3 us)
